TPU v7x, 32 devices: a whole 2x2x4 slice. The times are simulated.
32 devices in a mesh: rows: 8 (over y, x, core), cols: 4 (over z).
Axes of the slice: x: 2, y: 2, z: 4, core: 2. Of those that a mesh axis runs over, the one named last changes fastest.
Arguments:
- features: bfloat16 [64, 256, 256], P('rows', 'cols'), may hold values from -6 to 6
- crop_ids: int32 [64, 256], P(None, 'cols'), may hold values from 0 to 1023, as said below
- conditioning: bfloat16 [2, 768], replicated, may hold values from -6 to 6
- qkv_weight: bfloat16 [256, 768], P(('rows', 'cols')), may hold values from -0.375 to 0.375
- out_weight: bfloat16 [256, 256], P(('rows', 'cols')), may hold values from -1.5 to 1.5
- up_weight: bfloat16 [256, 1536], P(('rows', 'cols')), may hold values from -0.375 to 0.375
- down_weight: bfloat16 [768, 256], P(('rows', 'cols')), may hold values from -0.21875 to 0.21875
- attn_cond_weight: bfloat16 [768, 256], P(('rows', 'cols')), may hold values from -0.109375 to 0.109375
- feed_cond_weight: bfloat16 [768, 256], P(('rows', 'cols')), may hold values from -0.109375 to 0.109375
- attention_scale: float32 [4], replicated, may hold values from 6 to 20
- cotangent: bfloat16 [64, 256, 256], P('rows', 'cols'), may hold values from -6 to 6
Outputs:
- output: bfloat16 [64, 256, 256], P('rows', 'cols')
- grad_features: float32 [64, 256, 256], P('rows', 'cols')
- grad_qkv: float32 [256, 768], P(('rows', 'cols'))
- grad_out: float32 [256, 256], P(('rows', 'cols'))
- grad_up: float32 [256, 1536], P(('rows', 'cols'))
- grad_down: float32 [768, 256], P(('rows', 'cols'))
- grad_attn_cond: float32 [768, 256], P(('rows', 'cols'))
- grad_feed_cond: float32 [768, 256], P(('rows', 'cols'))
- grad_scale: float32 [4], replicated
Inputs may be any that keep to these rules, and one draw needn't show every extreme that they name: `crop_ids`: every crop is a run of whole rows inside one band of 16 columns (columns 16 * b to 16 * b + 15 of the array); different crops have different ids, ids of band b lie in b * 64 to b * 64 + 63 and its last crop has b * 64 + 63, and within a band the ids do not fall from row to row.
All inputs are finite; a program needn't handle non-finite values.
Results may differ from a plain program's by a relative error of at most 0.02.
Values may be sent and summed in bfloat16 or wider, within the bound.
No kernel may reach another device: no remote copies, remote signals or barrier semaphores. Data moves between devices by JAX's collectives and lax.ppermute only.
A program may use at most 256 MiB of HBM per device.

v0:
```python
import math

import jax
import jax.numpy as jnp
from jax import lax
from jax.sharding import PartitionSpec as P

W = 128


HIGH = lax.Precision.HIGHEST


def extended_2(shard, sides, width):
    for axis, dim in sides:
        size, length = (lax.axis_size(axis), shard.shape[dim])
        up = [(i, (i + 1) % size) for i in range(size - 1)]
        down = [(j, i) for i, j in up]
        last = lax.slice_in_dim(shard, length - width, length, axis=dim)
        initial = lax.slice_in_dim(shard, 0, width, axis=dim)
        before = lax.ppermute(last, axis, up)
        after = lax.ppermute(initial, axis, down)
        shard = jnp.concatenate([before, shard, after], axis=dim)
    return shard


def passed_along(shard, axis, by):
    size = lax.axis_size(axis)
    pairs = [(i, i + by) for i in range(size) if 0 <= i + by < size]
    return lax.ppermute(shard, axis, pairs)


def ada_norm(values, gain):
    return values * lax.rsqrt(jnp.mean(values * values, axis=-1, keepdims=True) + 1e-06) * gain


def cosine_prep(vectors, scale):
    return (
        vectors
        * jnp.sqrt(scale)[:, None]
        * lax.rsqrt(jnp.sum(vectors * vectors, axis=-1, keepdims=True) + 1e-06)
    )


def rotate(vectors, row_place, col_place):
    quarter = vectors.shape[-1] // 8
    indices = jnp.arange(quarter).astype(jnp.float32)
    frequency = math.pi / 8.0 * jnp.exp(indices * (-math.log(10.0) / quarter))
    row_angle = row_place.astype(jnp.float32)[:, None] * frequency
    col_angle = col_place.astype(jnp.float32)[:, None] * frequency
    row_cos = jnp.cos(row_angle)[:, None, None, :]
    row_sin = jnp.sin(row_angle)[:, None, None, :]
    col_cos = jnp.cos(col_angle)[None, :, None, :]
    col_sin = jnp.sin(col_angle)[None, :, None, :]
    part_a = vectors[..., :quarter]
    part_b = vectors[..., quarter : 2 * quarter]
    part_c = vectors[..., 2 * quarter : 3 * quarter]
    part_d = vectors[..., 3 * quarter : 4 * quarter]
    remainder = vectors[..., 4 * quarter :]
    return jnp.concatenate(
        [
            part_a * row_cos - part_b * row_sin,
            part_a * row_sin + part_b * row_cos,
            part_c * col_cos - part_d * col_sin,
            part_c * col_sin + part_d * col_cos,
            remainder,
        ],
        axis=-1,
    )


def windows(extended, offset, row_count, col_count):
    stripe = extended[offset : offset + row_count]
    return jnp.stack([stripe[:, column : column + col_count] for column in range(7)], axis=2)


def score_table(queries_low, extended, row_count, col_count):
    parts = [
        jnp.einsum(
            "rchd,rcxhd->rchx",
            queries_low,
            windows(extended, offset, row_count, col_count),
            preferred_element_type=jnp.float32,
        )
        for offset in range(7)
    ]
    return jnp.concatenate(parts, axis=-1)


def mix_table(weights_low, extended, row_count, col_count):
    mixed = None
    for offset in range(7):
        term = jnp.einsum(
            "rchx,rcxhd->rchd",
            weights_low[..., 7 * offset : 7 * offset + 7],
            windows(extended, offset, row_count, col_count),
            preferred_element_type=jnp.float32,
        )
        mixed = term if mixed is None else mixed + term
    return mixed


def allowed_table(id_ext, own_ids, row_count, col_count):
    parts = [
        windows(id_ext, offset, row_count, col_count) == own_ids[:, :, None] for offset in range(7)
    ]
    return jnp.concatenate(parts, axis=-1)[:, :, None, :]


def spread_back(d_scores_low, probs_low, queries_low, d_attended_low, row_count, col_count):
    shape = (row_count + 6, col_count + 6) + queries_low.shape[2:]
    key_total = jnp.zeros(shape, jnp.float32)
    value_total = jnp.zeros(shape, jnp.float32)
    for offset in range(7):
        for column in range(7):
            index = 7 * offset + column
            key_total = key_total.at[offset : offset + row_count, column : column + col_count].add(
                jnp.einsum(
                    "rch,rchd->rchd",
                    d_scores_low[..., index],
                    queries_low,
                    preferred_element_type=jnp.float32,
                )
            )
            value_total = value_total.at[
                offset : offset + row_count, column : column + col_count
            ].add(
                jnp.einsum(
                    "rch,rchd->rchd",
                    probs_low[..., index],
                    d_attended_low,
                    preferred_element_type=jnp.float32,
                )
            )
    return jnp.stack([key_total, value_total], axis=2)


def geglu(expanded):
    hidden = expanded.shape[1] // 2
    return expanded[:, :hidden] * jax.nn.gelu(expanded[:, hidden:], approximate=False)


def inner_rows(left, right):
    return lax.dot_general(
        left, right, (((0,), (0,)), ((), ())), preferred_element_type=jnp.float32
    )


def outer_cols(left, right):
    return lax.dot_general(
        left, right, (((1,), (1,)), ((), ())), preferred_element_type=jnp.float32
    )


def on_device(
    features,
    crop_ids,
    conditioning,
    qkv_weight,
    out_weight,
    up_weight,
    down_weight,
    attn_cond_weight,
    feed_cond_weight,
    attention_scale,
    cotangent,
):
    row_count, col_count, model_width = features.shape
    head_count = attention_scale.shape[0]
    head_size = model_width // head_count
    token_count = row_count * col_count
    full_qkv, full_out, full_up, full_down, full_attn_cond, full_feed_cond = (
        lax.all_gather(qkv_weight, ("rows", "cols"), axis=0, tiled=True),
        lax.all_gather(out_weight, ("rows", "cols"), axis=0, tiled=True),
        lax.all_gather(up_weight, ("rows", "cols"), axis=0, tiled=True),
        lax.all_gather(down_weight, ("rows", "cols"), axis=0, tiled=True),
        lax.all_gather(attn_cond_weight, ("rows", "cols"), axis=0, tiled=True),
        lax.all_gather(feed_cond_weight, ("rows", "cols"), axis=0, tiled=True),
    )
    row_start = lax.axis_index("rows") * row_count
    col_start = lax.axis_index("cols") * col_count
    cond_row = lax.dynamic_slice_in_dim(conditioning, col_start // W, 1, 0)
    cond_float = cond_row.astype(jnp.float32)
    inputs = features.astype(jnp.float32).reshape(token_count, model_width)
    gain_attn = 1.0 + jnp.dot(cond_row, full_attn_cond, preferred_element_type=jnp.float32)
    normed_attn, attn_norm_pull = jax.vjp(ada_norm, inputs, gain_attn)
    normed_attn_low = normed_attn.astype(jnp.bfloat16)
    projected = jnp.dot(normed_attn_low, full_qkv, preferred_element_type=jnp.float32)
    projected = projected.reshape(row_count, col_count, 3, head_count, head_size)
    row_place = row_start + jnp.arange(row_count, dtype=jnp.int32)
    col_place = (col_start + jnp.arange(col_count, dtype=jnp.int32)) % W

    def prepare(query_raw, key_raw, scale):
        return (
            rotate(cosine_prep(query_raw, scale), row_place, col_place),
            rotate(cosine_prep(key_raw, scale), row_place, col_place),
        )

    (query_rot, key_rot), prepare_pull = jax.vjp(
        prepare, projected[:, :, 0], projected[:, :, 1], attention_scale
    )
    queries_low = query_rot.astype(jnp.bfloat16)
    key_value = jnp.stack([key_rot, projected[:, :, 2]], axis=2).astype(jnp.bfloat16)
    key_value = key_value.reshape(row_count, col_count, 2 * model_width)
    padded = jnp.pad(extended_2(key_value, (("rows", 0),), 3), ((0, 0), (3, 3), (0, 0)))
    extended = padded.reshape(row_count + 6, col_count + 6, 2, head_count, head_size)
    id_pad = jnp.pad(crop_ids, 3, constant_values=-1)
    id_ext = lax.dynamic_slice_in_dim(id_pad, row_start, row_count + 6, 0)
    allowed = allowed_table(
        id_ext, id_ext[3 : 3 + row_count, 3 : 3 + col_count], row_count, col_count
    )
    masked = jnp.where(
        allowed, score_table(queries_low, extended[:, :, 0], row_count, col_count), -1000000000.0
    )
    top_score = jnp.max(masked, axis=-1, keepdims=True)
    raised = jnp.exp(masked - top_score)
    total = jnp.sum(raised, axis=-1, keepdims=True)
    log_total = top_score + jnp.log(total)
    probs_low = (raised / total).astype(jnp.bfloat16)
    attended_low = mix_table(probs_low, extended[:, :, 1], row_count, col_count).astype(
        jnp.bfloat16
    )
    attended_low = attended_low.reshape(token_count, model_width)
    middle = inputs + jnp.dot(attended_low, full_out, preferred_element_type=jnp.float32)
    gain_feed = 1.0 + jnp.dot(cond_row, full_feed_cond, preferred_element_type=jnp.float32)
    normed_feed, feed_norm_pull = jax.vjp(ada_norm, middle, gain_feed)
    normed_feed_low = normed_feed.astype(jnp.bfloat16)
    expanded = jnp.dot(normed_feed_low, full_up, preferred_element_type=jnp.float32)
    gated, geglu_pull = jax.vjp(geglu, expanded)
    gated_low = gated.astype(jnp.bfloat16)
    result = middle + jnp.dot(gated_low, full_down, preferred_element_type=jnp.float32)
    output = result.astype(jnp.bfloat16).reshape(row_count, col_count, model_width)
    upstream = cotangent.reshape(token_count, model_width)
    grad_down = inner_rows(gated_low, upstream)
    (d_expanded,) = geglu_pull(outer_cols(upstream, full_down))
    d_expanded_low = d_expanded.astype(jnp.bfloat16)
    grad_up = inner_rows(normed_feed_low, d_expanded_low)
    d_middle_norm, d_gain_feed = feed_norm_pull(outer_cols(d_expanded_low, full_up))
    grad_feed_cond = lax.dot_general(
        cond_float, d_gain_feed, (((0,), (0,)), ((), ())), precision=HIGH
    )
    d_middle = upstream.astype(jnp.float32) + d_middle_norm
    d_branch_low = d_middle.astype(jnp.bfloat16)
    grad_out = inner_rows(attended_low, d_branch_low)
    d_attended_low = outer_cols(d_branch_low, full_out).astype(jnp.bfloat16)
    d_attended_low = d_attended_low.reshape(row_count, col_count, head_count, head_size)
    masked = jnp.where(
        allowed, score_table(queries_low, extended[:, :, 0], row_count, col_count), -1000000000.0
    )
    probs = jnp.exp(masked - log_total)
    probs_low = probs.astype(jnp.bfloat16)
    d_probs = score_table(d_attended_low, extended[:, :, 1], row_count, col_count)
    d_scores_low = (probs * (d_probs - jnp.sum(probs * d_probs, axis=-1, keepdims=True))).astype(
        jnp.bfloat16
    )
    d_query = mix_table(d_scores_low, extended[:, :, 0], row_count, col_count)
    spread = spread_back(d_scores_low, probs_low, queries_low, d_attended_low, row_count, col_count)
    top_rim = spread[0:3, 3 : 3 + col_count].reshape(3, col_count, 2 * model_width)
    bottom_rim = spread[row_count + 3 : row_count + 6, 3 : 3 + col_count].reshape(
        3, col_count, 2 * model_width
    )
    from_below = passed_along(top_rim.astype(jnp.bfloat16), "rows", -1).astype(top_rim.dtype)
    from_above = passed_along(bottom_rim.astype(jnp.bfloat16), "rows", 1).astype(bottom_rim.dtype)
    own_grads = spread[3 : 3 + row_count, 3 : 3 + col_count].reshape(
        row_count, col_count, 2 * model_width
    )
    own_grads = own_grads.at[:3].add(from_above).at[row_count - 3 :].add(from_below)
    own_grads = own_grads.reshape(row_count, col_count, 2, head_count, head_size)
    d_query_raw, d_key_raw, d_scale = prepare_pull((d_query, own_grads[:, :, 0]))
    d_projected_low = jnp.stack([d_query_raw, d_key_raw, own_grads[:, :, 1]], axis=2).astype(
        jnp.bfloat16
    )
    d_projected_low = d_projected_low.reshape(token_count, 3 * model_width)
    grad_qkv = inner_rows(normed_attn_low, d_projected_low)
    d_input_norm, d_gain_attn = attn_norm_pull(outer_cols(d_projected_low, full_qkv))
    grad_features = (d_middle + d_input_norm).reshape(row_count, col_count, model_width)
    grad_attn_cond = lax.dot_general(
        cond_float, d_gain_attn, (((0,), (0,)), ((), ())), precision=HIGH
    )
    grad_scale = lax.psum(d_scale, ("rows", "cols"))
    weight_sums = (
        lax.psum_scatter(grad_qkv, ("rows", "cols"), scatter_dimension=0, tiled=True),
        lax.psum_scatter(grad_out, ("rows", "cols"), scatter_dimension=0, tiled=True),
        lax.psum_scatter(grad_up, ("rows", "cols"), scatter_dimension=0, tiled=True),
        lax.psum_scatter(grad_down, ("rows", "cols"), scatter_dimension=0, tiled=True),
        lax.psum_scatter(grad_attn_cond, ("rows", "cols"), scatter_dimension=0, tiled=True),
        lax.psum_scatter(grad_feed_cond, ("rows", "cols"), scatter_dimension=0, tiled=True),
    )
    return (
        output,
        grad_features,
        weight_sums[0],
        weight_sums[1],
        weight_sums[2],
        weight_sums[3],
        weight_sums[4],
        weight_sums[5],
        grad_scale,
    )


def solution(mesh):
    return jax.shard_map(
        on_device,
        mesh=mesh,
        in_specs=(
            P("rows", "cols", None),
            P(None, "cols"),
            P(),
            P(("rows", "cols"), None),
            P(("rows", "cols"), None),
            P(("rows", "cols"), None),
            P(("rows", "cols"), None),
            P(("rows", "cols"), None),
            P(("rows", "cols"), None),
            P(),
            P("rows", "cols", None),
        ),
        out_specs=(
            P("rows", "cols", None),
            P("rows", "cols", None),
            P(("rows", "cols"), None),
            P(("rows", "cols"), None),
            P(("rows", "cols"), None),
            P(("rows", "cols"), None),
            P(("rows", "cols"), None),
            P(("rows", "cols"), None),
            P(),
        ),
        check_vma=False,
    )
```

profile of v0, /device:TPU:0, one launch (start us, length us, event | category | flops | bytes accessed | tf_op | source)
XLA Modules:
  0.0 2154.0 jit_solution(1288261716238663722)
XLA Ops:
  9.0 73.0 %all_gather.19 = bf16[256,768]{1,0:T(8,128)(2,1)S(1)} all-gather(bf16[8,768]{1,0:T(8,128)(2,1)} %param.214), channel_id=1, replica_groups=mesh['rows'=8,'cols'=4] {'rows','cols'}, dimensions={0}, use_global_device_ids=true | all-gather | bytes 405504 | tf_op jit(solution)/shard_map/all_gather | solution.py:173
  83.0 66.8 %all_gather.18 = bf16[768,256]{1,0:T(8,128)(2,1)S(1)} all-gather(bf16[24,256]{1,0:T(8,128)(2,1)} %param.218), channel_id=1, replica_groups=mesh['rows'=8,'cols'=4] {'rows','cols'}, dimensions={0}, use_global_device_ids=true | all-gather | bytes 405504 | tf_op jit(solution)/shard_map/all_gather | solution.py:177
  171.1 68.7 %all_gather.21 = bf16[768,256]{1,0:T(8,128)(2,1)S(1)} all-gather(bf16[24,256]{1,0:T(8,128)(2,1)S(1)} %copy-done.70), channel_id=1, replica_groups=mesh['rows'=8,'cols'=4] {'rows','cols'}, dimensions={0}, use_global_device_ids=true | all-gather | bytes 405504 | tf_op jit(solution)/shard_map/all_gather | solution.py:178
  240.0 74.5 %all_gather.22 = bf16[256,1536]{1,0:T(8,128)(2,1)} all-gather(bf16[8,1536]{1,0:T(8,128)(2,1)S(1)} %copy-done.66), channel_id=1, replica_groups=mesh['rows'=8,'cols'=4] {'rows','cols'}, dimensions={0}, use_global_device_ids=true | all-gather | bytes 811008 | tf_op jit(solution)/shard_map/all_gather | solution.py:175
  315.1 66.5 %all_gather.20 = bf16[256,256]{1,0:T(8,128)(2,1)S(1)} all-gather(bf16[8,256]{1,0:T(8,128)(2,1)S(1)} %copy-done.76), channel_id=1, replica_groups=mesh['rows'=8,'cols'=4] {'rows','cols'}, dimensions={0}, use_global_device_ids=true | all-gather | bytes 135168 | tf_op jit(solution)/shard_map/all_gather | solution.py:174
  381.7 71.7 %all_gather.23 = bf16[768,256]{1,0:T(8,128)(2,1)} all-gather(bf16[24,256]{1,0:T(8,128)(2,1)S(1)} %copy-done.71), channel_id=1, replica_groups=mesh['rows'=8,'cols'=4] {'rows','cols'}, dimensions={0}, use_global_device_ids=true | all-gather | bytes 405504 | tf_op jit(solution)/shard_map/all_gather | solution.py:176
  555.2 15.1 multiply_reduce_fusion.21
  633.5 17.9 multiply_reduce_fusion.7
  670.9 9.6 scatter-add.335
  684.5 9.5 scatter-add.336
  697.8 9.4 scatter-add.339
  711.3 9.5 scatter-add.340
  724.8 9.4 scatter-add.341
  738.1 9.5 scatter-add.344
  756.5 8.2 scatter-add.346
  766.7 8.2 scatter-add.349
  777.0 8.2 scatter-add.350
  787.2 8.2 scatter-add.351
  797.5 8.2 scatter-add.354
  825.0 8.2 scatter-add.359
  835.3 8.2 scatter-add.360
  845.5 8.2 scatter-add.361
  855.8 8.2 scatter-add.364
  876.3 8.2 scatter-add.366
  893.3 8.2 scatter-add.370
  913.9 8.2 scatter-add.374
  924.1 8.2 scatter-add.375
  944.6 8.2 scatter-add.379
  962.1 8.2 scatter-add.381
  982.6 8.2 scatter-add.385
  992.9 8.2 scatter-add.386
  1153.0 9.4 scatter-add.416
  1166.4 9.5 scatter-add.419
  1179.8 9.4 scatter-add.420
  1193.2 9.5 scatter-add.421
  1206.7 9.4 scatter-add.424
  1220.1 9.5 scatter-add.425
  1248.6 8.4 scatter-add.430
  1375.2 8.6 scatter-add.454
  1501.9 8.4 scatter-add.476
  1604.6 8.2 scatter-add.414
  1614.2 8.4 scatter-add.495
  1688.4 41.0 %psum.7 = f32[4]{0:T(128)} all-reduce(f32[4]{0:T(128)S(1)} %divide_multiply_fusion), channel_id=1, replica_groups=mesh['rows'=8,'cols'=4] {'rows','cols'}, use_global_device_ids=true, to_apply=%region_26.27 | all-reduce | flops 4 | bytes 32 | tf_op jit(solution)/shard_map/psum | solution.py:280
  1730.4 10.9 reduce-scatter.13.cloned.1.call-done
  1741.3 101.1 %reduce-scatter.7.cloned.1.call-done = f32[8,768]{1,0:T(8,128)} async-done(((f32[256,768]{1,0:T(8,128)}), f32[8,768]{1,0:T(8,128)}) %reduce-scatter.7.cloned.1.call-update) | async-done | bytes 24592 | tf_op jit(solution)/shard_map/reduce_scatter | solution.py:282
  1842.4 101.0 %reduce-scatter.17.cloned.1.call-done = f32[24,256]{1,0:T(8,128)} async-done(((f32[768,256]{1,0:T(8,128)}), f32[24,256]{1,0:T(8,128)}) %reduce-scatter.17.cloned.1.call-update) | async-done | bytes 24592 | tf_op jit(solution)/shard_map/reduce_scatter | solution.py:287
  1943.4 100.9 %reduce-scatter.15.cloned.1.call-done = f32[24,256]{1,0:T(8,128)} async-done(((f32[768,256]{1,0:T(8,128)}), f32[24,256]{1,0:T(8,128)}) %reduce-scatter.15.cloned.1.call-update) | async-done | bytes 24592 | tf_op jit(solution)/shard_map/reduce_scatter | solution.py:286
  2044.3 102.6 %reduce-scatter.11.cloned.1.call-done = f32[8,1536]{1,0:T(8,128)} async-done(((f32[256,1536]{1,0:T(8,128)}), f32[8,1536]{1,0:T(8,128)}) %reduce-scatter.11.cloned.1.call-update) | async-done | bytes 49168 | tf_op jit(solution)/shard_map/reduce_scatter | solution.py:284
  (633 shorter events, 930.7 us)
Async XLA Ops:
  7.2 142.5 %copy-start = (bf16[2,768]{1,0:T(2,128)(2,1)S(1)}, bf16[2,768]{1,0:T(2,128)(2,1)}, u32[]{:S(2)}) copy-start(bf16[2,768]{1,0:T(2,128)(2,1)} %param.213) | copy-start | bytes 9220
  7.2 1723.2 %reduce-scatter.9.cloned.1.call-start = ((), (), s32[]{:S(2)}) async-start(), calls=%async_computation.7 | async-start | bytes 270336 | tf_op jit(solution)/shard_map/reduce_scatter | solution.py:283
  82.0 69.0 %copy-start.37 = (bf16[256,768]{1,0:T(8,128)(2,1)}, bf16[256,768]{1,0:T(8,128)(2,1)S(1)}, u32[]{:S(2)}) copy-start(bf16[256,768]{1,0:T(8,128)(2,1)S(1)} %all_gather.19) | copy-start | bytes 1179652
  155.1 159.7 %copy-start.53 = (f32[64,8]{0,1:T(8,128)}, f32[64,8]{0,1:T(8,128)S(1)}, u32[]{:S(2)}) copy-start(f32[64,8]{0,1:T(8,128)S(1)} %get-tuple-element.1428) | copy-start | bytes 6148
  155.1 159.7 %copy-start.55 = (f32[64,8]{0,1:T(8,128)}, f32[64,8]{0,1:T(8,128)S(1)}, u32[]{:S(2)}) copy-start(f32[64,8]{0,1:T(8,128)S(1)} %get-tuple-element.1429) | copy-start | bytes 6148
  155.3 159.4 %copy-start.57 = (f32[8,8]{1,0:T(8,128)}, f32[8,8]{1,0:T(8,128)S(1)}, u32[]{:S(2)}) copy-start(f32[8,8]{1,0:T(8,128)S(1)} %get-tuple-element.1430) | copy-start | bytes 772
  155.3 159.4 %copy-start.59 = (f32[8,8]{1,0:T(8,128)}, f32[8,8]{1,0:T(8,128)S(1)}, u32[]{:S(2)}) copy-start(f32[8,8]{1,0:T(8,128)S(1)} %get-tuple-element.1431) | copy-start | bytes 772
  156.7 9.3 copy-start.77
  156.7 12.0 copy-start.5
  156.7 14.4 copy-start.70
  156.8 83.1 %copy-start.66 = (bf16[8,1536]{1,0:T(8,128)(2,1)S(1)}, bf16[8,1536]{1,0:T(8,128)(2,1)}, u32[]{:S(2)}) copy-start(bf16[8,1536]{1,0:T(8,128)(2,1)} %param.216) | copy-start | bytes 73732
  157.0 157.5 %copy-start.26 = (f32[8,64,4,64]{1,3,2,0:T(8,128)S(1)}, f32[8,64,4,64]{1,3,2,0:T(8,128)}, u32[]{:S(2)}) copy-start(f32[8,64,4,64]{1,3,2,0:T(8,128)} %get-tuple-element.1248) | copy-start | bytes 1572868
  157.4 157.7 %copy-start.76 = (bf16[8,256]{1,0:T(8,128)(2,1)S(1)}, bf16[8,256]{1,0:T(8,128)(2,1)}, u32[]{:S(2)}) copy-start(bf16[8,256]{1,0:T(8,128)(2,1)} %param.215) | copy-start | bytes 12292
  158.3 223.3 %copy-start.71 = (bf16[24,256]{1,0:T(8,128)(2,1)S(1)}, bf16[24,256]{1,0:T(8,128)(2,1)}, u32[]{:S(2)}) copy-start(bf16[24,256]{1,0:T(8,128)(2,1)} %param.217) | copy-start | bytes 36868
  158.3 295.1 %collective-permute-start.1 = (bf16[3,64,512]{1,2,0:T(8,128)(2,1)}, bf16[3,64,512]{1,2,0:T(8,128)(2,1)S(1)}, u32[]{:S(2)}, u32[]{:S(2)}) collective-permute-start(bf16[3,64,512]{1,2,0:T(8,128)(2,1)} %bitcast.89), channel_id=1, source_target_pairs={{4,0},{8,4},{12,8},{16,12},{20,16},{24,20},{28,24},{5,1},{9,5},{13... | collective-permute-start | bytes 589832 | tf_op jit(solution)/shard_map/ppermute | solution.py:22
  159.8 293.7 %collective-permute-start = (bf16[3,64,512]{1,2,0:T(8,128)(2,1)}, bf16[3,64,512]{1,2,0:T(8,128)(2,1)}, u32[]{:S(2)}, u32[]{:S(2)}) collective-permute-start(bf16[3,64,512]{1,2,0:T(8,128)(2,1)} %bitcast.87), channel_id=1, source_target_pairs={{0,4},{4,8},{8,12},{12,16},{16,20},{20,24},{24,28},{1,5},{5,9},{9,... | collective-permute-start | bytes 589832 | tf_op jit(solution)/shard_map/ppermute | solution.py:21
  239.9 391.5 %copy-start.68 = (f32[256]{0:T(256)}, f32[256]{0:T(256)S(1)}, u32[]{:S(2)}) copy-start(f32[256]{0:T(256)S(1)} %broadcast_add_fusion) | copy-start | bytes 3076
  541.2 14.0 copy-start.13
  544.1 11.1 copy-start.11
  548.2 7.0 copy-start.7
  622.2 9.2 copy-start.17
  622.2 9.2 copy-start.64
  631.7 19.7 copy-start.19
  655.8 1085.4 %reduce-scatter.13.cloned.1.call-start = ((), (), s32[]{:S(2)}) async-start(), calls=%async_computation.9 | async-start | bytes 811008 | tf_op jit(solution)/shard_map/reduce_scatter | solution.py:285
  1633.9 12.1 copy-start.21
  1633.9 12.1 copy-start.47
  1636.1 11.3 copy-start.54
  1636.1 11.3 copy-start.56
  1636.1 11.3 copy-start.58
  1638.5 8.9 copy-start.32
  1638.5 10.4 copy-start.25
  1638.5 11.4 collective-permute-start.3
  1642.2 6.7 collective-permute-start.2
  1647.4 195.0 %reduce-scatter.7.cloned.1.call-start = ((), (), s32[]{:S(2)}) async-start(), calls=%async_computation.6 | async-start | bytes 811008 | tf_op jit(solution)/shard_map/reduce_scatter | solution.py:282
  1653.4 8.3 copy-start.4
  1653.4 8.3 copy-start.41
  1659.7 9.9 copy-start.75
  1673.4 7.3 copy-start.78
  1675.4 7.4 copy-start.18
  1675.4 7.4 copy-start.24
  1675.4 7.4 copy-start.65
  1675.4 7.4 copy-start.69
  1678.1 265.2 %reduce-scatter.17.cloned.1.call-start = ((), (), s32[]{:S(2)}) async-start(), calls=%async_computation.11 | async-start | bytes 811008 | tf_op jit(solution)/shard_map/reduce_scatter | solution.py:287
  1682.1 362.1 %reduce-scatter.15.cloned.1.call-start = ((), (), s32[]{:S(2)}) async-start(), calls=%async_computation.10 | async-start | bytes 811008 | tf_op jit(solution)/shard_map/reduce_scatter | solution.py:286
  1682.7 46.7 %copy-start.20 = (f32[512,256]{1,0:T(8,128)S(1)}, f32[512,256]{1,0:T(8,128)}, u32[]{:S(2)}) copy-start(f32[512,256]{1,0:T(8,128)} %copy-done.19) | copy-start | bytes 1572868
  1682.7 464.2 %reduce-scatter.11.cloned.1.call-start = ((), (), s32[]{:S(2)}) async-start(), calls=%async_computation.8 | async-start | bytes 1622016 | tf_op jit(solution)/shard_map/reduce_scatter | solution.py:284
  1686.2 43.2 %copy-start.30 = (bf16[8,64,256]{2,1,0:T(8,128)(2,1)S(1)}, bf16[8,64,256]{2,1,0:T(8,128)(2,1)}, u32[]{:S(2)}) copy-start(bf16[8,64,256]{2,1,0:T(8,128)(2,1)} %param.211) | copy-start | bytes 786436
  1686.2 43.2 %copy-start.48 = (f32[512,256]{1,0:T(8,128)S(1)}, f32[512,256]{1,0:T(8,128)}, u32[]{:S(2)}) copy-start(f32[512,256]{1,0:T(8,128)} %get-tuple-element.1450) | copy-start | bytes 1572868
  (43 other events, 138.8 us)
Sparse Core Ops, SparseCore 0:
  655.9 132.3 reduce-scatter.8
  1647.5 93.7 reduce-scatter.12
  1747.8 94.5 reduce-scatter.6
  1848.7 94.5 reduce-scatter.16
  1949.7 94.5 reduce-scatter.14
  2050.8 96.0 reduce-scatter.10
where the time goes:
time: 2170 us; the launch traced here: 2150 us
  local copies, waits for them, and re-layouts  924 us (43%)
  blocking collectives  462 us (21%)
  waiting for transfers between devices  417 us (19%)
  other arithmetic  301 us (14%)
  matrix products  22.8 us (1%)
    scatter-add x49, local copies, waits for them, and re-layouts, spread_back(): key_total.at[offset:offset + row_count, column:column + col_count]  382 us
    scatter-add x49, local copies, waits for them, and re-layouts, spread_back(): value_total = value_total.at[offset:offset + row_count, column:column + c...  382 us
    reduce_scatter x1, waiting for transfers between devices, on_device(): lax.psum_scatter(grad_up, ('rows', 'cols'), scatter_dimension=0, tiled=True)  103 us
    reduce_scatter x1, waiting for transfers between devices, on_device(): lax.psum_scatter(grad_qkv, ('rows', 'cols'), scatter_dimension=0, tiled=T...  101 us
    reduce_scatter x1, waiting for transfers between devices, on_device(): lax.psum_scatter(grad_feed_cond, ('rows', 'cols'), scatter_dimension=0, t...  101 us
    reduce_scatter x1, waiting for transfers between devices, on_device(): lax.psum_scatter(grad_attn_cond, ('rows', 'cols'), scatter_dimension=0, t...  101 us
    unnamed x281, local copies, waits for them, and re-layouts  93.5 us
    add x42, other arithmetic, spread_back(): key_total.at[offset:offset + row_count, column:column + col_count]  86.3 us
  transfers between devices with their start and end apart: 10, of which 5 were waited for; matrix products, arithmetic and copies ran while one was open for 48% of the time, Pallas kernels for 0%

commit v1 on v0

v1 whole, which is shorter than its diff:
```python
import functools
import math

import jax
import jax.numpy as jnp
from jax import lax
from jax.experimental import pallas as pl
from jax.experimental.pallas import tpu as pltpu
from jax.sharding import PartitionSpec as P

CANVAS = 128
BAND = 16
REACH = 3
AXES = ("rows", "cols")
F32 = jnp.float32
BF16 = jnp.bfloat16
EPS = 1e-06
VMEM_LIMIT = 32 * 1024 * 1024


class Place:
    def __init__(self, direct, cols, n_cols):
        self.direct, self.cols, self.n_cols = direct, cols, n_cols

    def __getitem__(self, item):
        row, col = lax.axis_index("rows"), lax.axis_index("cols")
        if item == 0:
            return col * self.cols // CANVAS
        if item == 4:
            return row * self.n_cols + col
        if item == 5:
            return lax.rem(row, 2)
        if not self.direct:
            return (0, 0, 0, 0, 0, 0, 1)[item]
        return (None, row // 2, lax.rem(row, 2), col, None, None, 2 - lax.rem(row, 2))[item]


def mm(left, right):
    return lax.dot_general(left, right, (((1,), (0,)), ((), ())), preferred_element_type=F32)


def mm_rt(left, right):
    return lax.dot_general(left, right, (((1,), (1,)), ((), ())), preferred_element_type=F32)


def mm_lt(left, right):
    return lax.dot_general(left, right, (((0,), (0,)), ((), ())), preferred_element_type=F32)


def same_head(width, size):
    first = lax.broadcasted_iota(jnp.int32, (width, width), 0) // size
    second = lax.broadcasted_iota(jnp.int32, (width, width), 1) // size
    return jnp.where(first == second, 1.0, 0.0).astype(BF16)


def stack_heads(values, heads):
    lane = head_of(values.shape, heads)
    return jnp.concatenate(
        [jnp.where(lane == h, values, 0.0).astype(BF16) for h in range(heads)], axis=0
    )


def fold_heads(values, heads):
    count = values.shape[0] // heads
    lane = head_of((count, values.shape[1]), heads)
    total = values[:count]
    for h in range(1, heads):
        total = jnp.where(lane == h, values[h * count : (h + 1) * count], total)
    return total


def turned_order(width, heads):
    size = width // heads
    part = size // 8
    row = lax.broadcasted_iota(jnp.int32, (width, width), 0)
    col = lax.broadcasted_iota(jnp.int32, (width, width), 1)
    half, lane = col // (width // 2), col % (width // 2)
    head, j = lane // (size // 2), lane % (size // 2)
    rotated = j // part * 2 * part + j % part + half * part
    kept = 4 * part + j - 2 * part + half * 2 * part
    return jnp.where(row == head * size + jnp.where(j < 2 * part, rotated, kept), 1.0, 0.0).astype(BF16)


def halves(values):
    half = values.shape[1] // 2
    return values[:, :half], values[:, half:]


def head_of(shape, heads):
    half = shape[1] // 2
    return lax.broadcasted_iota(jnp.int32, shape, 1) % half // (half // heads)


def own_rows(values, count):
    edge = REACH * BAND
    return jnp.concatenate(
        [values[start + edge : start + edge + count] for start in range(0, values.shape[0], 2 * count)], axis=0
    )


def bands_of(ref, bands):
    parts = [
        ref[:, band * BAND : (band + 1) * BAND, :].astype(F32).reshape(-1, ref.shape[-1])
        for band in range(bands)
    ]
    return jnp.concatenate(parts, axis=0)


def pair_lanes(values, heads, pair):
    size = values.shape[1] // heads
    part = values[:, 128 * pair : 128 * pair + 128]
    lane = lax.broadcasted_iota(jnp.int32, part.shape, 1)
    return jnp.concatenate(
        [jnp.where(lane < size, part, 0.0), jnp.where(lane < size, 0.0, part)], axis=0
    ).astype(BF16)


def merge_pair(values, size):
    count = values.shape[0] // 2
    lane = lax.broadcasted_iota(jnp.int32, (count, 128), 1)
    return jnp.where(lane < size, values[:count], values[count:])


def close(shape, query_row, key_row):
    token = lax.broadcasted_iota(jnp.int32, shape, 0)
    place = lax.broadcasted_iota(jnp.int32, shape, 1)
    return (jnp.abs(token // BAND + query_row - place // BAND - key_row) <= REACH) & (
        jnp.abs(token % BAND - place % BAND) <= REACH
    )


def norm_scale(values):
    return lax.rsqrt(jnp.mean(values * values, axis=-1, keepdims=True) + EPS)


def place_parts(place, part_refs, wide_ref, last):
    lanes = wide_ref.shape[-1]
    for index, part in enumerate(part_refs):
        chip = place[1] ^ (index % 4)
        core = place[2] ^ (index // 4)
        group = part.shape[0]
        start = part.shape[-1] - lanes if last else 0
        for col in range(group):
            wide_ref[(chip * 2 + core) * group + col] = part[col, :, start : start + lanes].astype(F32)


def columns(wide_ref, start, width):
    chunks = wide_ref.shape[0]
    return wide_ref[:, :, start : start + width].reshape(chunks * 8, width).astype(BF16)


def split_parts(place, wide_ref, mine_ref, other_ref):
    group = mine_ref.shape[1]
    for chip in range(mine_ref.shape[0]):
        for col in range(group):
            mine_ref[chip, col] = wide_ref[(chip * 2 + place[2]) * group + col].astype(BF16)
            other_ref[chip, col] = wide_ref[(chip * 2 + 1 - place[2]) * group + col].astype(BF16)


def pack_kernel(
    per_canvas, place, cond_ref, qkv_ref, up_ref, out_ref, down_ref, attn_ref, feed_ref,
    near_ref, far_ref, cond_own_ref,
):
    own = attn_ref.shape[0]
    canvases, total = cond_ref.shape
    width = out_ref.shape[1]
    row = lax.broadcasted_iota(jnp.int32, (own, total), 0) + place[4] * own
    pick = jnp.where(row == lax.broadcasted_iota(jnp.int32, (own, total), 1), 1.0, 0.0).astype(BF16)
    cond = mm_rt(pick, cond_ref[...])
    cond_own_ref[...] = cond
    tails = []
    for canvas in range(canvases):
        lines = []
        for weight_ref in (attn_ref, feed_ref):
            line = jnp.sum(
                cond[:, canvas : canvas + 1] * weight_ref[...].astype(F32), axis=0, keepdims=True
            )
            high = line.astype(BF16).astype(F32)
            for part in (high, line - high):
                lines += [part[:, :128], part[:, 128:]]
        tails.append(jnp.concatenate(lines, axis=0))
    down = down_ref[...].astype(F32)
    parts = [up_ref[...], out_ref[...]] + [down[8 * i : 8 * i + 8].astype(BF16) for i in range(down.shape[0] // 8)]
    qkv = qkv_ref.shape[1]
    mine = place[0] == 0
    for ref, tail in (
        (near_ref, jnp.where(mine, tails[0], tails[1])),
        (far_ref, jnp.where(mine, tails[1], tails[0])),
    ):
        ref[:, :qkv] = qkv_ref[...]
        ref[:, qkv : qkv + 128] = tail.astype(BF16)
        at = qkv + 128
        for part in parts:
            ref[:, at : at + part.shape[1]] = part
            at += part.shape[1]


def line_kernel(place, p0, p1, p2, p3, line_ref):
    for index, part in enumerate((p0, p1, p2, p3)):
        line_ref[place[3] ^ index] = part[...]


def core_sum_kernel(place, mine_ref, got_ref, *refs):
    lanes = mine_ref.shape[-1]
    for index, out_ref in enumerate(refs[-4:]):
        chip = place[1] ^ (0, place[6], place[6] ^ 3, 3)[index]
        start = 0 if len(refs) == 4 else out_ref.shape[-1] - lanes
        out_ref[:, :, start : start + lanes] = (
            mine_ref[chip].astype(F32) + got_ref[chip].astype(F32)
        ).astype(BF16)


def pair_sum_kernel(one_ref, two_ref, out_ref):
    out_ref[...] = (one_ref[...].astype(F32) + two_ref[...].astype(F32)).astype(BF16)


def chip_sum_kernel(place, p0, p1, p2, o0, o1, o2, o3, keep_ref):
    keep_ref[...] = p0[...].astype(F32) + p1[...].astype(F32) + p2[...].astype(F32)
    for index, out_ref in enumerate((o0, o1, o2, o3)):
        out_ref[...] = keep_ref[place[3] ^ index].astype(out_ref.dtype)


def last_kernel(
    per_canvas, size, place, cond_ref, own_ref, one_ref, two_ref, three_ref,
    qkv_ref, out_ref, up_ref, down_ref, attn_ref, feed_ref, scale_ref,
):
    parts = [own_ref[...]] + [ref[...].astype(F32) for ref in (one_ref, two_ref, three_ref)]
    total = parts[0] + parts[1] + parts[2] + parts[3]
    width = out_ref.shape[1]
    at = up_ref.shape[1]
    up_ref[...] = total[:, :at]
    out_ref[...] = total[:, at : at + width]
    for i in range(down_ref.shape[0] // 8):
        at += width
        down_ref[8 * i : 8 * i + 8, :] = total[:, at : at + width]
    at += width
    qkv_ref[...] = total[:, at : at + qkv_ref.shape[1]]
    at += qkv_ref.shape[1]
    cond = cond_ref[...]
    attn, feed = 0.0, 0.0
    for canvas in range(cond.shape[1]):
        tail = jnp.zeros((8, 128), F32)
        for index, part in enumerate(parts):
            same = (place[3] ^ index) // per_canvas == canvas
            tail = tail + jnp.where(same, part[:, at:], 0.0)
        weight = cond[:, canvas : canvas + 1]
        attn = attn + weight * jnp.concatenate([tail[0:1], tail[1:2]], axis=1)
        feed = feed + weight * jnp.concatenate([tail[2:3], tail[3:4]], axis=1)
    attn_ref[...] = attn
    feed_ref[...] = feed
    tail = total[:, at:]
    scale = tail[4:5] + tail[5:6]
    for h in range(scale_ref.shape[0]):
        scale_ref[h] = scale[0, h * size]


def ready_kernel(
    heads, place, scale_ref, feat_ref, cot_ref, swap_ref, beside_ref, row_ref, col_ref, id_query_ref, id_key_ref,
    unit_ref, unit_turned_ref, own_turned_ref, cos_ref, sine_ref, mask_ref, inputs_ref, cot_out_ref, root_ref,
):
    rows, cols, width = feat_ref.shape
    count = rows * BAND
    bands = cols // BAND
    odd = place[5] == 1
    near = close((count, 2 * count), REACH, 0)
    lane = lax.broadcasted_iota(jnp.int32, (1, width // 2), 1) // (width // 2 // heads)
    root = jnp.zeros((1, width // 2), F32)
    for h in range(heads):
        root = jnp.where(lane == h, scale_ref[h], root)
    root_ref[...] = jnp.sqrt(root)
    inputs_ref[...] = bands_of(feat_ref, bands)
    cot_out_ref[...] = bands_of(cot_ref, bands).astype(BF16)
    for band in range(bands):
        part = slice(band * BAND, (band + 1) * BAND)
        swapped = swap_ref[:, part, :].astype(F32)
        beside = beside_ref[:, part, :].astype(F32)
        full = jnp.concatenate(
            [
                jnp.where(odd, swapped, beside),
                feat_ref[:, part, :].astype(F32),
                jnp.where(odd, beside, swapped),
                jnp.zeros((2, BAND, width), F32),
            ],
            axis=0,
        ).reshape(2 * count, width)
        span = slice(2 * band * count, 2 * (band + 1) * count)
        unit = full * norm_scale(full)
        unit_ref[span] = unit
        turned = jnp.transpose(unit).astype(BF16)
        unit_turned_ref[:, span] = turned
        own = slice(REACH * BAND, REACH * BAND + count)
        own_turned_ref[:, band * count : (band + 1) * count] = jnp.transpose(unit[own]).astype(BF16)
        for i, ref in enumerate((cos_ref, sine_ref)):
            ref[span] = (row_ref[i][:, None, :] + col_ref[i, part, :][None]).reshape(2 * count, width // 2)
        alike = id_query_ref[REACH * BAND : REACH * BAND + count, band : band + 1] == id_key_ref[
            band : band + 1, :
        ]
        mask_ref[band] = jnp.where(near & alike, 1.0, 0.0).astype(BF16)


def attend_kernel(
    heads, place, root_ref, unit_ref, cos_ref, sine_ref, mask_ref, p0, p1, p2, p3, p4, p5, p6, p7,
    query_ref, key_ref, value_ref, raised_ref, mixed_ref, inverse_ref, along_q_ref, length_q_ref, along_k_ref, length_k_ref,
    gain_ref, gain_col_ref, w_ref,
    wide_ref,
):
    bands, count = mask_ref.shape[:2]
    width = unit_ref.shape[1]
    size = width // heads
    edge = REACH * BAND
    place_parts(place, (p0, p1, p2, p3, p4, p5, p6, p7), wide_ref, False)
    weight = columns(wide_ref, 0, 3 * width)
    order = turned_order(width, heads)
    turned = mm(
        jnp.concatenate([weight[:, :width], weight[:, width : 2 * width]], axis=0), order
    ).astype(BF16)
    w_ref[:, :width], w_ref[:, width : 2 * width] = turned[:width], turned[width:]
    w_ref[:, 2 * width :] = weight[:, 2 * width :]
    sums = jnp.sum(wide_ref[:, :, 3 * width :], axis=0)
    pairs = [sums[i : i + 2] + sums[i + 2 : i + 4] for i in (0, 4)]
    picked = 1.0 + jnp.concatenate(
        [jnp.concatenate([pair[0:1], pair[1:2]], axis=1) for pair in pairs], axis=0
    )
    gain_ref[...] = picked
    gain_col_ref[...] = jnp.transpose(jnp.broadcast_to(picked[0:1], (128, width)))
    root = root_ref[...]
    unit = unit_ref[...]
    normed = (unit * picked[0:1]).astype(BF16)
    value_ref[...] = mm(normed, weight[:, 2 * width :]).astype(BF16)
    ones_head = same_head(width // 2, size // 2)
    cos, sine = cos_ref[...], sine_ref[...]
    for i, ref in enumerate((query_ref, key_ref)):
        first, second = halves(mm(normed, turned[i * width : (i + 1) * width]))
        short = lax.rsqrt(mm((first * first + second * second).astype(BF16), ones_head) + EPS)
        length = short * root
        ref[...] = jnp.concatenate(
            [(first * cos - second * sine) * length, (second * cos + first * sine) * length], axis=1
        ).astype(BF16)
        along = jnp.concatenate([first * short, second * short], axis=1)
        if i == 0:
            along_q_ref[...], length_q_ref[...] = own_rows(along, count), own_rows(length, count)
        else:
            along_k_ref[...], length_k_ref[...] = along, length
    ones_half = jnp.ones((2 * count, 128), BF16)
    for band in range(bands):
        start = 2 * band * count
        query = query_ref[start + edge : start + edge + count, :].astype(F32)
        scores = mm_rt(stack_heads(query, heads), key_ref[start : start + 2 * count, :])
        raised = jnp.exp(scores).astype(BF16) * jnp.concatenate([mask_ref[band]] * heads, axis=0)
        raised_ref[band] = raised
        value = value_ref[start : start + 2 * count, :]
        span = slice(band * count, (band + 1) * count)
        for pair in range(heads // 2):
            lanes = slice(128 * pair, 128 * pair + 128)
            both = mm(
                raised[2 * pair * count : 2 * (pair + 1) * count],
                jnp.concatenate([value[:, lanes], ones_half], axis=1),
            )
            inverse = 1.0 / merge_pair(both[:, 128:], size)
            mixed_ref[span, lanes] = merge_pair(both[:, :128], size) * inverse
            inverse_ref[span, lanes] = inverse


def feed_kernel(
    heads, place, inputs_ref, cot_ref, p0, p1, p2, p3, p4, p5, p6, p7, gain_ref, mixed_ref, inverse_ref,
    middle_ref, middle_grad_ref, shrunk_ref, gain_grad_ref,
    w_down_ref, mixed_low_ref, normed_ref, gated_ref, d_exp_ref, branch_ref,
    wide_ref,
):
    width = inputs_ref.shape[1]
    chunks = wide_ref.shape[0]
    hidden = w_down_ref.shape[0]
    own_down = hidden // chunks
    ups = 2 * hidden
    place_parts(place, (p0, p1, p2, p3, p4, p5, p6, p7), wide_ref, True)
    w_up = columns(wide_ref, 0, ups)
    w_out = columns(wide_ref, ups, width)
    w_down = (
        jnp.concatenate(
            [
                wide_ref[:, :, ups + width * (i + 1) : ups + width * (i + 2)]
                for i in range(own_down // 8)
            ],
            axis=1,
        )
        .reshape(hidden, width)
        .astype(BF16)
    )
    w_down_ref[...] = w_down
    gain_feed = gain_ref[1:2]
    mixed = mixed_ref[...]
    mixed_low = mixed.astype(BF16)
    mixed_low_ref[...] = mixed_low
    middle = inputs_ref[...] + mm(mixed_low, w_out)
    middle_ref[...] = middle
    scale = norm_scale(middle)
    unit = middle * scale
    normed = (unit * gain_feed).astype(BF16)
    normed_ref[...] = normed
    cot = cot_ref[...].astype(F32)
    half = math.sqrt(0.5)
    density = 1.0 / math.sqrt(2.0 * math.pi)
    pulled = None
    for start in range(0, hidden, width):
        here = slice(start, start + width)
        there = slice(hidden + start, hidden + start + width)
        left = mm(normed, w_up[:, here])
        gate = mm(normed, w_up[:, there])
        d_gated = mm_rt(cot_ref[...], w_down[here])
        phi = 0.5 + 0.5 * lax.erf(gate * half)
        shaped = gate * phi
        gated_ref[:, here] = (left * shaped).astype(BF16)
        slope = phi + gate * (jnp.exp(gate * gate * -0.5) * density)
        d_left = (d_gated * shaped).astype(BF16)
        d_gate = (d_gated * left * slope).astype(BF16)
        d_exp_ref[:, here] = d_left
        d_exp_ref[:, there] = d_gate
        part = mm_rt(d_left, w_up[:, here]) + mm_rt(d_gate, w_up[:, there])
        pulled = part if pulled is None else pulled + part
    gain_grad_ref[...] = jnp.sum(pulled * unit, axis=0, keepdims=True)
    inner = pulled * gain_feed
    d_middle = cot + scale * (inner - unit * jnp.mean(unit * inner, axis=-1, keepdims=True))
    middle_grad_ref[...] = d_middle
    branch = d_middle.astype(BF16)
    branch_ref[...] = branch
    shrunk_ref[...] = (mm_rt(branch, w_out) * inverse_ref[...]).astype(BF16)


def weights_kernel(
    place, cot_ref, mixed_low_ref, normed_ref, gated_ref, d_exp_ref, branch_ref, mine_ref, other_ref, wide_ref
):
    width = cot_ref.shape[1]
    chunks = wide_ref.shape[0]
    ups = d_exp_ref.shape[1]
    own_down = gated_ref.shape[1] // chunks
    wide_ref[:, :, :ups] = mm_lt(normed_ref[...], d_exp_ref[...]).reshape(chunks, 8, ups)
    wide_ref[:, :, ups : ups + width] = mm_lt(mixed_low_ref[...], branch_ref[...]).reshape(
        chunks, 8, width
    )
    grad = mm_lt(gated_ref[...], cot_ref[...]).reshape(chunks, own_down, width)
    for i in range(own_down // 8):
        start = ups + width * (i + 1)
        wide_ref[:, :, start : start + width] = grad[:, 8 * i : 8 * i + 8]
    split_parts(place, wide_ref, mine_ref, other_ref)


def output_kernel(middle_ref, gated_ref, w_down_ref, out_ref):
    rows, cols, width = out_ref.shape
    total = (middle_ref[...] + mm(gated_ref[...], w_down_ref[...])).astype(BF16)
    count = rows * BAND
    for band in range(cols // BAND):
        out_ref[:, band * BAND : (band + 1) * BAND, :] = total[band * count : (band + 1) * count].reshape(
            rows, BAND, width
        )


def back_kernel(
    heads, shrunk_ref, mixed_ref, raised_ref, query_ref, key_ref, value_ref, dq_ref, dk_ref, dv_ref
):
    bands, _, keys = raised_ref.shape
    count = keys // 2
    edge = REACH * BAND
    ones_half = jnp.ones((keys, 128), BF16)
    for band in range(bands):
        span = slice(band * count, (band + 1) * count)
        start = band * keys
        whole = slice(start, start + keys)
        shrunk = shrunk_ref[span].astype(F32)
        level_rows = -(shrunk * mixed_ref[span])
        value = value_ref[whole, :]
        raised = raised_ref[band]
        parts, stacks = [], []
        for pair in range(heads // 2):
            lanes = slice(128 * pair, 128 * pair + 128)
            stacks.append(pair_lanes(shrunk, heads, pair))
            parts.append(
                mm_rt(
                    jnp.concatenate([stacks[-1], pair_lanes(level_rows, heads, pair)], axis=1),
                    jnp.concatenate([value[:, lanes], ones_half], axis=1),
                )
            )
        d_scores = (raised.astype(F32) * jnp.concatenate(parts, axis=0)).astype(BF16)
        dq_ref[span] = fold_heads(mm(d_scores, key_ref[whole, :]), heads)
        query = query_ref[start + edge : start + edge + count, :].astype(F32)
        dk_ref[whole, :] = mm_lt(d_scores, stack_heads(query, heads))
        for pair in range(heads // 2):
            lanes = slice(128 * pair, 128 * pair + 128)
            dv_ref[whole, lanes] = mm_lt(raised[2 * pair * count : 2 * (pair + 1) * count], stacks[pair])


def pull_head(grad, along, length, cos, sine, heads):
    first, second = halves(grad)
    along_first, along_second = halves(along)
    first, second = first * cos + second * sine, second * cos - first * sine
    ones_head = same_head(first.shape[1], first.shape[1] // heads)
    part = mm((along_first * first + along_second * second).astype(BF16), ones_head)
    grad = jnp.concatenate(
        [length * (first - along_first * part), length * (second - along_second * part)], axis=1
    )
    return grad.astype(BF16), jnp.sum(part, axis=0, keepdims=True)


def lane_sums(product):
    total = product[:, :128]
    for start in range(128, product.shape[1], 128):
        total = total + product[:, start : start + 128]
    return jnp.sum(jnp.transpose(total), axis=0, keepdims=True)


def project_kernel(
    heads, rows, place, root_ref, cos_ref, sine_ref, w_ref, gain_col_ref, unit_turned_ref, own_turned_ref,
    along_q_ref, length_q_ref, along_k_ref, length_k_ref, dq_ref, dk_ref, dv_ref, gain_grad_ref,
    d_query_ref, d_rest_ref, mine_ref, other_ref, wide_ref,
):
    tokens, width = dq_ref.shape
    chunks = wide_ref.shape[0]
    cos, sine = cos_ref[...], sine_ref[...]
    count = rows * BAND
    d_key, along_k = pull_head(dk_ref[...], along_k_ref[...], length_k_ref[...], cos, sine, heads)
    d_value = dv_ref[...].astype(BF16)
    d_query, along_q = pull_head(
        dq_ref[...], along_q_ref[...], length_q_ref[...], own_rows(cos, count), own_rows(sine, count), heads
    )
    d_query_ref[...] = d_query
    d_rest = jnp.concatenate([d_key, d_value], axis=1)
    d_rest_ref[...] = d_rest
    plain = jnp.concatenate(
        [
            mm(own_turned_ref[...], d_query),
            mm(unit_turned_ref[...], d_rest),
        ],
        axis=1,
    )
    scaled = plain * jnp.concatenate([gain_col_ref[...]] * (3 * width // 128), axis=1)
    turned = jnp.concatenate([scaled[:, :width], scaled[:, width : 2 * width]], axis=0).astype(BF16)
    plain_order = mm_rt(turned, turned_order(width, heads))
    wide_ref[:, :, :width] = plain_order[:width].reshape(chunks, 8, width)
    wide_ref[:, :, width : 2 * width] = plain_order[width:].reshape(chunks, 8, width)
    wide_ref[:, :, 2 * width : 3 * width] = scaled[:, 2 * width :].reshape(chunks, 8, width)
    gain_total = lane_sums(plain * w_ref[...].astype(F32))
    lines = []
    for total in (gain_total, gain_grad_ref[...]):
        lines += [total[:, :128], total[:, 128:]]
    total = (along_q + along_k) * 0.5 / root_ref[...]
    high = total.astype(BF16).astype(F32)
    lines += [high, total - high, jnp.zeros((2, 128), F32)]
    wide_ref[:, :, 3 * width :] = jnp.broadcast_to(
        jnp.concatenate(lines, axis=0)[None], (chunks, 8, 128)
    )
    split_parts(place, wide_ref, mine_ref, other_ref)


def normed_back_kernel(
    rows, place, w_ref, d_query_ref, d_rest_ref, own_ref, rim_swap_ref, rim_beside_ref
):
    width = own_ref.shape[1]
    count, edge = rows * BAND, REACH * BAND
    odd = place[5] == 1
    whole = mm_rt(d_rest_ref[...], w_ref[:, width:])
    own_ref[...] = mm_rt(d_query_ref[...], w_ref[:, :width]) + own_rows(whole, count)
    for band in range(whole.shape[0] // (2 * count)):
        start = 2 * band * count
        upper, lower = whole[start : start + edge], whole[start + edge + count : start + 2 * edge + count]
        here = slice(band * edge, (band + 1) * edge)
        rim_swap_ref[here] = jnp.where(odd, upper, lower).astype(BF16)
        rim_beside_ref[here] = jnp.where(odd, lower, upper).astype(BF16)


def features_kernel(place, inputs_ref, gain_ref, own_ref, rim_swap_ref, rim_beside_ref, middle_grad_ref, grad_ref):
    rows, cols, width = grad_ref.shape
    bands = cols // BAND
    count, edge = rows * BAND, REACH * BAND
    odd = place[5] == 1
    zeros = jnp.zeros((count - 2 * edge, width), F32)
    rims = []
    for band in range(bands):
        here = slice(band * edge, (band + 1) * edge)
        swapped, beside = rim_swap_ref[here].astype(F32), rim_beside_ref[here].astype(F32)
        rims += [jnp.where(odd, swapped, beside), zeros, jnp.where(odd, beside, swapped)]
    inner = (own_ref[...] + jnp.concatenate(rims, axis=0)) * gain_ref[0:1]
    inputs = inputs_ref[...]
    scale = norm_scale(inputs)
    unit = inputs * scale
    grad = middle_grad_ref[...] + scale * (inner - unit * jnp.mean(unit * inner, axis=-1, keepdims=True))
    for band in range(bands):
        grad_ref[:, band * BAND : (band + 1) * BAND, :] = grad[band * count : (band + 1) * count].reshape(
            rows, BAND, width
        )


def forward_kernel(
    heads, place, root_ref, unit_ref, cos_ref, sine_ref, mask_ref, inputs_ref, cot_ref,
    p0, p1, p2, p3, p4, p5, p6, p7,
    query_ref, key_ref, value_ref, raised_ref, mixed_ref, along_q_ref, length_q_ref, along_k_ref, length_k_ref,
    gain_ref, gain_col_ref, w_ref, middle_ref, middle_grad_ref, shrunk_ref, gain_grad_ref,
    w_down_ref, gated_ref, mine_ref, other_ref,
    inverse_ref, first_wide_ref, second_wide_ref, mixed_low_ref, normed_ref, d_exp_ref, branch_ref,
):
    parts = (p0, p1, p2, p3, p4, p5, p6, p7)
    attend_kernel(
        heads, place, root_ref, unit_ref, cos_ref, sine_ref, mask_ref, *parts,
        query_ref, key_ref, value_ref, raised_ref, mixed_ref, inverse_ref,
        along_q_ref, length_q_ref, along_k_ref, length_k_ref, gain_ref, gain_col_ref, w_ref, first_wide_ref,
    )
    feed_kernel(
        heads, place, inputs_ref, cot_ref, *parts, gain_ref, mixed_ref, inverse_ref,
        middle_ref, middle_grad_ref, shrunk_ref, gain_grad_ref,
        w_down_ref, mixed_low_ref, normed_ref, gated_ref, d_exp_ref, branch_ref, second_wide_ref,
    )
    weights_kernel(
        place, cot_ref, mixed_low_ref, normed_ref, gated_ref, d_exp_ref, branch_ref, mine_ref, other_ref,
        second_wide_ref,
    )


def backward_kernel(
    heads, rows, place, root_ref, shrunk_ref, mixed_ref, raised_ref, query_ref, key_ref, value_ref,
    cos_ref, sine_ref, w_ref, gain_col_ref, unit_turned_ref, own_turned_ref, along_q_ref, length_q_ref, along_k_ref, length_k_ref,
    gain_grad_ref,
    d_query_ref, d_rest_ref, mine_ref, other_ref, dq_ref, dk_ref, dv_ref, wide_ref,
):
    back_kernel(
        heads, shrunk_ref, mixed_ref, raised_ref, query_ref, key_ref, value_ref, dq_ref, dk_ref, dv_ref
    )
    project_kernel(
        heads, rows, place, root_ref, cos_ref, sine_ref, w_ref, gain_col_ref, unit_turned_ref, own_turned_ref,
        along_q_ref, length_q_ref, along_k_ref, length_k_ref, dq_ref, dk_ref, dv_ref, gain_grad_ref,
        d_query_ref, d_rest_ref, mine_ref, other_ref, wide_ref,
    )


def call(kernel, outs, scratch=(), place=None, smem=0, smem_out=0, flops=10**9, pin=True, aliases=None):
    if place is not None:
        kernel = functools.partial(kernel, place)

    def run(*args):
        args = [
            arg if i < smem else pltpu.with_memory_space_constraint(arg, pltpu.VMEM if pin else pltpu.HBM)
            for i, arg in enumerate(args)
        ]
        return pl.pallas_call(
            kernel,
            out_shape=outs,
            in_specs=[
                pl.BlockSpec(memory_space=pltpu.SMEM if i < smem else pltpu.VMEM)
                for i in range(len(args))
            ],
            out_specs=[
                pl.BlockSpec(memory_space=pltpu.SMEM if i >= len(outs) - smem_out else pltpu.VMEM)
                for i in range(len(outs))
            ],
            scratch_shapes=list(scratch),
            input_output_aliases=aliases or {},
            compiler_params=pltpu.CompilerParams(vmem_limit_bytes=VMEM_LIMIT),
            cost_estimate=pl.CostEstimate(flops=flops, bytes_accessed=4 * 10**6 if flops > 1 else 1, transcendentals=0),
        )(*args)

    return run


def rotation_tables(row_place, col_place, heads, size):
    part = size // 8
    lane = jnp.arange(heads * size // 2) % (size // 2)
    index = (lane % part).astype(F32)
    frequency = math.pi / 8.0 * jnp.exp(index * (-math.log(10.0) / part))
    group = lane // part

    def table(place, kind):
        angle = place.astype(F32)[:, None] * frequency
        cos = jnp.where(group == kind, jnp.cos(angle), 0.0)
        if kind:
            cos = jnp.where(group >= 2, 1.0, cos)
        return jnp.stack([cos, jnp.where(group == kind, jnp.sin(angle), 0.0)])

    return table(row_place, 0), table(col_place, 1)


def window_ids(crop_ids, row_start, rows):
    ids = jnp.pad(crop_ids[:, ::BAND], ((REACH, 2 * rows), (0, 0)), constant_values=-1)
    ids = lax.dynamic_slice_in_dim(ids, row_start, 2 * rows, 0)
    return jnp.repeat(ids, BAND, axis=0), jnp.repeat(ids.T, BAND, axis=1)


def on_device(
    features, crop_ids, conditioning, qkv_weight, out_weight, up_weight, down_weight,
    attn_cond_weight, feed_cond_weight, attention_scale, cotangent,
):
    rows, cols, width = features.shape
    heads = attention_scale.shape[0]
    size = width // heads
    bands = cols // BAND
    count = rows * BAND
    tokens = rows * cols
    edge = REACH * BAND
    n_rows, n_cols = lax.axis_size("rows"), lax.axis_size("cols")
    devices = n_rows * n_cols
    hidden = down_weight.shape[0] * devices
    own_cond = attn_cond_weight.shape[0]
    canvases = conditioning.shape[0]
    row, col = lax.axis_index("rows"), lax.axis_index("cols")
    row_start, col_start = row * rows, col * cols
    canvas = col_start // CANVAS
    group, chips = 4, 4
    chunks = 2 * chips * group
    direct = (n_rows, n_cols) == (2 * chips, group) and chunks * 8 == width
    first_lanes = 3 * width + 128
    second_lanes = 2 * hidden + width + hidden * width // (8 * chunks)
    per_canvas = max(n_cols // canvases, 1)
    place = Place(direct, cols, n_cols)

    def result(*dims, dtype=F32):
        return jax.ShapeDtypeStruct(dims, dtype)

    def shape(*dims, dtype=F32):
        return pltpu.VMEM(dims, dtype)

    def low(*dims):
        return shape(*dims, dtype=BF16)

    def over(axis, by):
        size_of = lax.axis_size(axis)
        return lambda value: lax.ppermute(value, axis, [(i, i ^ by) for i in range(size_of)])

    z_moves = [over("cols", k) for k in range(1, group)]
    xy_moves = [over("rows", 2 * m) for m in range(1, chips)]

    def chip_pairs(step):
        return [(i, i ^ (4 if i % 2 == step else 2)) for i in range(n_rows)]

    def first_chip(value):
        return lax.ppermute(value, "rows", chip_pairs(0))

    def second_chip(value):
        return lax.ppermute(value, "rows", chip_pairs(1))

    core_move = over("rows", 1)

    if direct:
        near, far, cond_own = call(
            functools.partial(pack_kernel, per_canvas),
            [
                low(8, first_lanes + second_lanes),
                low(8, first_lanes + second_lanes),
                shape(own_cond, canvases),
            ],
            place=place,
            pin=False,
        )(conditioning, qkv_weight, up_weight, out_weight, down_weight, attn_cond_weight, feed_cond_weight)
        line = call(line_kernel, [low(group, 8, first_lanes + second_lanes)], place=place)(
            near,
            *[move(near if k // per_canvas == 0 else far) for k, move in enumerate(z_moves, 1)],
        )[0]
        mine = [line] + [move(line) for move in xy_moves]
    else:
        def parts_of(full):
            full = full.reshape(chips, 2, group, 8, full.shape[-1])
            return [full[m, core] for core in range(2) for m in range(chips)]

        def whole(weight):
            return lax.all_gather(weight, AXES, axis=0, tiled=True)

        cond = lax.dynamic_slice_in_dim(conditioning, place[4] * own_cond, own_cond, 1)
        cond_own = cond.T.astype(F32)
        sums = [
            lax.psum(jnp.dot(cond, weight, preferred_element_type=F32), AXES)
            for weight in (attn_cond_weight, feed_cond_weight)
        ]
        lines = []
        for part in sums:
            part = lax.dynamic_slice_in_dim(part, canvas, 1, 0).reshape(-1, 128)
            high = lax.reduce_precision(part, 8, 7)
            lines += [high, part - high]
        lines = jnp.pad(jnp.concatenate(lines).astype(BF16), ((0, width - 8), (0, 0)))
        down = whole(down_weight).reshape(chunks, -1, 8, width).transpose(0, 2, 1, 3).reshape(width, -1)
        parts = parts_of(
            jnp.concatenate([whole(qkv_weight), lines, whole(up_weight), whole(out_weight), down], axis=1)
        )

    odd = row % 2 == 1
    beside_pairs = [(i, (i + 1 if i % 2 else i - 1) % n_rows) for i in range(n_rows)]

    def beside_move(value):
        return lax.ppermute(value, "rows", beside_pairs)

    first_rows, last_rows = features[:REACH], features[rows - REACH :]
    halo_swap = core_move(jnp.where(odd, first_rows, last_rows))
    halo_beside = beside_move(jnp.where(odd, last_rows, first_rows))

    row_place = row_start - REACH + jnp.arange(2 * rows, dtype=jnp.int32)
    col_place = (col_start + jnp.arange(cols, dtype=jnp.int32)) % CANVAS
    row_table, col_table = rotation_tables(row_place, col_place, heads, size)
    id_query, id_key = window_ids(crop_ids, row_start, rows)

    unit, unit_turned, own_turned, cos, sine, mask, inputs, cot, root = call(
        functools.partial(ready_kernel, heads),
        [
            shape(2 * tokens, width),
            low(width, 2 * tokens),
            low(width, tokens),
            shape(2 * tokens, width // 2),
            shape(2 * tokens, width // 2),
            low(bands, count, 2 * count),
            shape(tokens, width),
            low(tokens, width),
            shape(1, width // 2),
        ],
        place=place,
        smem=1,
    )(attention_scale, features, cotangent, halo_swap, halo_beside, row_table, col_table, id_query, id_key)
    if direct:
        mine = mine[:1] + [lax.optimization_barrier((part, unit))[0] for part in mine[1:]]
        far = core_move(mine[3])
        for i in (1, 2):
            mine[i], far = lax.optimization_barrier((mine[i], far))
        parts = mine + [core_move(part) for part in mine[:3]] + [far]

    (
        query, key, value, raised, mixed, along_q, length_q, along_k, length_k, gain, gain_col, w_qkv,
        middle, middle_grad, shrunk, gain_grad, w_down, gated, mine_second, other_second,
    ) = call(
        functools.partial(forward_kernel, heads),
        [
            low(2 * tokens, width),
            low(2 * tokens, width),
            low(2 * tokens, width),
            low(bands, heads * count, 2 * count),
            shape(tokens, width),
            shape(tokens, width),
            shape(tokens, width // 2),
            shape(2 * tokens, width),
            shape(2 * tokens, width // 2),
            shape(2, width),
            shape(width, 128),
            low(width, 3 * width),
            shape(tokens, width),
            shape(tokens, width),
            low(tokens, width),
            shape(1, width),
            low(hidden, width),
            low(tokens, hidden),
            low(chips, group, 8, second_lanes),
            low(chips, group, 8, second_lanes),
        ],
        scratch=[
            pltpu.VMEM((tokens, width), F32),
            pltpu.VMEM((chunks, 8, first_lanes), F32),
            pltpu.VMEM((chunks, 8, second_lanes), F32),
            pltpu.VMEM((tokens, width), BF16),
            pltpu.VMEM((tokens, width), BF16),
            pltpu.VMEM((tokens, 2 * hidden), BF16),
            pltpu.VMEM((tokens, width), BF16),
        ],
        place=place,
    )(root, unit, cos, sine, mask, inputs, cot, *parts)

    d_query, d_rest, mine_first, other_first = call(
        functools.partial(backward_kernel, heads, rows),
        [
            low(tokens, width),
            low(2 * tokens, 2 * width),
            low(chips, group, 8, first_lanes),
            low(chips, group, 8, first_lanes),
        ],
        scratch=[
            pltpu.VMEM((tokens, width), F32),
            pltpu.VMEM((2 * tokens, width), F32),
            pltpu.VMEM((2 * tokens, width), F32),
            pltpu.VMEM((chunks, 8, first_lanes), F32),
        ],
        place=place,
        flops=1,
    )(
        root, shrunk, mixed, raised, query, key, value, cos, sine, w_qkv, gain_col, unit_turned, own_turned,
        along_q, length_q, along_k, length_k, gain_grad,
    )

    def last_output(gated):
        return call(output_kernel, [result(rows, cols, width, dtype=BF16)])(middle, gated, w_down)[0]

    def normed_back(d_query, d_rest):
        return call(
            functools.partial(normed_back_kernel, rows),
            [shape(tokens, width), low(bands * edge, width), low(bands * edge, width)],
            place=place,
        )(w_qkv, d_query, d_rest)

    def last_features(own, rim_swap, rim_beside):
        return call(features_kernel, [result(rows, cols, width)], place=place)(
            inputs, gain, own, rim_swap, rim_beside, middle_grad
        )[0]

    if direct:
        all_lanes = second_lanes + first_lanes
        lines = [low(group, 8, all_lanes) for _ in range(chips)]
        second_got = core_move(other_second)
        sums = call(core_sum_kernel, lines, place=place)(mine_second, second_got)
        sums = call(core_sum_kernel, lines, place=place, aliases={2 + i: i for i in range(chips)})(
            mine_first, core_move(other_first), *sums
        )
        sums, d_rest = lax.optimization_barrier((sums, d_rest))
        own, first_part, second_part, far_part = sums
        far_got, second_got = second_chip(far_part), second_chip(second_part)
        first_part = call(pair_sum_kernel, [low(group, 8, all_lanes)], flops=1)(first_part, far_got)[0]
        sums = [own, first_chip(first_part), second_got]
        own_grad, rim_swap, rim_beside = normed_back(d_query, d_rest)
        rim_swap, rim_beside = core_move(rim_swap), beside_move(rim_beside)
        blocks = call(
            chip_sum_kernel,
            [shape(8, all_lanes)] + [low(8, all_lanes) for _ in z_moves],
            scratch=[pltpu.VMEM((group, 8, all_lanes), F32)],
            place=place,
        )(*sums)
        blocks, gated, own_grad = lax.optimization_barrier((blocks, gated, own_grad))
        output = last_output(gated)
        grad_features = last_features(own_grad, rim_swap, rim_beside)
        grad_qkv, grad_out, grad_up, grad_down, grad_attn_cond, grad_feed_cond, grad_scale = call(
            functools.partial(last_kernel, per_canvas, size // 2),
            [
                result(8, 3 * width),
                result(8, width),
                result(8, 2 * hidden),
                result(hidden // chunks, width),
                result(own_cond, width),
                result(own_cond, width),
                result(heads),
            ],
            place=place,
            smem_out=1,
        )(cond_own, blocks[0], *[move(block) for move, block in zip(z_moves, blocks[1:])])
    else:
        own_grad, rim_swap, rim_beside = normed_back(d_query, d_rest)
        grad_features = last_features(own_grad, core_move(rim_swap), beside_move(rim_beside))
        output = last_output(gated)

        def joined(mine, other):
            return jnp.stack([mine, other], axis=1).astype(F32).reshape(chunks, 8, mine.shape[-1])

        def scattered(grad):
            return lax.psum_scatter(grad.reshape(-1, grad.shape[-1]), AXES, scatter_dimension=0, tiled=True)

        last = joined(mine_first, other_first)
        second = joined(mine_second, other_second)
        ups = 2 * hidden
        grad_qkv = scattered(last[:, :, : 3 * width])
        grad_up = scattered(second[:, :, :ups])
        grad_out = scattered(second[:, :, ups : ups + width])
        grad_down = scattered(
            second[:, :, ups + width :].reshape(chunks, 8, -1, width).transpose(0, 2, 1, 3)
        )
        spot = (jnp.arange(canvases) == canvas).astype(F32)[:, None, None]
        tail = lax.psum(spot * last[0, :, 3 * width :][None], AXES)

        def cond_grad(sums):
            return jnp.sum(cond_own[:, :, None] * sums.reshape(canvases, width)[None], axis=1)

        grad_attn_cond = cond_grad(tail[:, 0:2])
        grad_feed_cond = cond_grad(tail[:, 2:4])
        grad_scale = jnp.sum(tail[:, 4] + tail[:, 5], axis=0)[:: size // 2]
    return (
        output, grad_features, grad_qkv, grad_out, grad_up, grad_down, grad_attn_cond, grad_feed_cond, grad_scale,
    )


def solution(mesh):
    tile, whole, split = P("rows", "cols", None), P(), P(AXES, None)
    return jax.shard_map(
        on_device,
        mesh=mesh,
        in_specs=(tile, P(None, "cols"), whole, split, split, split, split, split, split, whole, tile),
        out_specs=(tile, tile, split, split, split, split, split, split, whole),
        check_vma=False,
    )
```

time: 2170 us -> 59.3 us (0.03)
  local copies, waits for them, and re-layouts: 924 us -> 1.76 us
  blocking collectives: 462 us -> 0 us
  waiting for transfers between devices: 417 us -> 18.9 us
  other arithmetic: 301 us -> 0.39 us
  matrix products: 22.8 us -> 0 us
    scatter-add x98 -> x0, local copies, waits for them, and re-layouts: 764 us -> none  [the longest x49 382 us: spread_back(): key_total.at[offset:offset + row_count, column:column + col_count]]
    all_gather x6 -> x0, blocking collectives: 421 us -> none  [the longest x1 74.5 us: on_device(): lax.all_gather(up_weight, ('rows', 'cols'), axis=0, tiled=True)]
    reduce_scatter x6 -> x0, waiting for transfers between devices: 416 us -> none  [the longest x1 103 us: on_device(): lax.psum_scatter(grad_up, ('rows', 'cols'), scatter_dimension=0, tiled=True)]
    add x91 -> x0, other arithmetic: 147 us -> none  [the longest x42 86.3 us: spread_back(): key_total.at[offset:offset + row_count, column:column + col_count]]
    unnamed x281 -> x8, local copies, waits for them, and re-layouts: 93.5 us -> 1.39 us
    another operation x30 -> x2, other arithmetic: 56.2 us -> 0.01 us  [table(): return jnp.stack([cos, jnp.where(group == kind, jnp.sin(angle), 0.0)])]
    dot_general x12 -> x0, other arithmetic: 45.2 us -> none  [the longest x2 32.9 us: score_table(): jnp.einsum('rchd,rcxhd->rchx', queries_low, windows(extended, offset, row...]
    psum x1 -> x0, blocking collectives: 41 us -> none  [on_device(): grad_scale = lax.psum(d_scale, ('rows', 'cols'))]
  transfers between devices with their start and end apart: 10 -> 22, of which waited for: 5 -> 12; matrix products, arithmetic and copies ran while one was open for 48% -> 1% of each run, Pallas kernels for 0% -> 13%
where the time goes in v1:
time: 59.3 us; the launch traced here: 59.1 us
  starting transfers between devices  22.6 us (38%)
  waiting for transfers between devices  18.9 us (32%)
  Pallas kernels  14.6 us (25%)
  local copies, waits for them, and re-layouts  1.76 us (3%)
  between operations  0.86 us (1%)
    ppermute x17, starting transfers between devices, over(): lax.ppermute(value, axis, [(i, i ^ by) for i in range(size_of)])  16 us
    pallas_call x13, Pallas kernels, run(): pl.pallas_call(kernel, out_shape=outs, in_specs=[pl.BlockSpec(memory_spac...  14.6 us
    ppermute x17, waiting for transfers between devices, over(): lax.ppermute(value, axis, [(i, i ^ by) for i in range(size_of)])  12.7 us
    ppermute x2, waiting for transfers between devices, second_chip(): return lax.ppermute(value, 'rows', chip_pairs(1))  3.91 us
    ppermute x2, starting transfers between devices, beside_move(): return lax.ppermute(value, 'rows', beside_pairs)  3.02 us
    ppermute x1, waiting for transfers between devices, first_chip(): return lax.ppermute(value, 'rows', chip_pairs(0))  2.29 us
    ppermute x2, starting transfers between devices, second_chip(): return lax.ppermute(value, 'rows', chip_pairs(1))  2.09 us
    ppermute x1, starting transfers between devices, first_chip(): return lax.ppermute(value, 'rows', chip_pairs(0))  1.48 us
  transfers between devices with their start and end apart: 22, of which 12 were waited for; matrix products, arithmetic and copies ran while one was open for 1% of the time, Pallas kernels for 13%

profile of v1, /device:TPU:0, one launch (start us, length us, event | category | flops | bytes accessed | tf_op | source)
XLA Modules:
  0.0 59.1 jit_solution(9914159123932355606)
XLA Ops:
  0.7 1.1 %shard_map.179 = (bf16[8,3456]{1,0:T(8,128)(2,1)S(1)}, bf16[8,3456]{1,0:T(8,128)(2,1)S(1)}, f32[24,2]{1,0:T(8,128)S(1)}) custom-call(bf16[2,768]{1,0:T(2,128)(2,1)} %cond_ref.1, bf16[8,768]{1,0:T(8,128)(2,1)} %qkv_ref.1, bf16[8,1536]{1,0:T(8,128)(2,1)} %up_ref.1, bf16[8,256]{1,0:T(8,128)(2,1)} %out_ref.1, bf16[24,256]{1,0:T(8,128)(2,1)} %down_ref.1, ...), custom_call_target="tpu_custom_call" | custom-call | flops 1000000000 | bytes 4000000 | tf_op jit(solution)/shard_map/pallas_call | solution.py:641
  1.7 5.1 %collective-permute-start.4 = (bf16[8,3456]{1,0:T(8,128)(2,1)S(1)}, bf16[8,3456]{1,0:T(8,128)(2,1)S(1)}, u32[]{:S(2)}, u32[]{:S(2)}) collective-permute-start(bf16[8,3456]{1,0:T(8,128)(2,1)S(1)} %get-tuple-element.93), channel_id=1, source_target_pairs={{0,3},{1,2},{2,1},{3,0},{4,7},{5,6},{6,5},{7,4},{8,11},{9,10},{10,... | collective-permute-start | bytes 165896 | tf_op jit(solution)/shard_map/ppermute | solution.py:722
  6.8 0.6 %collective-permute-start.2 = (bf16[8,3456]{1,0:T(8,128)(2,1)S(1)}, bf16[8,3456]{1,0:T(8,128)(2,1)S(1)}, u32[]{:S(2)}, u32[]{:S(2)}) collective-permute-start(bf16[8,3456]{1,0:T(8,128)(2,1)S(1)} %get-tuple-element.92.p0), channel_id=1, source_target_pairs={{0,1},{1,0},{2,3},{3,2},{4,5},{5,4},{6,7},{7,6},{8,9},{9,8},{10,11... | collective-permute-start | bytes 165896 | tf_op jit(solution)/shard_map/ppermute | solution.py:722
  7.5 1.4 %collective-permute-start.1 = (bf16[3,64,256]{2,1,0:T(8,128)(2,1)S(1)}, bf16[3,64,256]{2,1,0:T(8,128)(2,1)S(1)}, u32[]{:S(2)}, u32[]{:S(2)}) collective-permute-start(bf16[3,64,256]{2,1,0:T(8,128)(2,1)S(1)} %get-tuple-element.161), channel_id=1, source_target_pairs={{0,28},{4,8},{8,4},{12,16},{16,12},{20,24},{24,20},{28,0},{1,29},{... | collective-permute-start | bytes 294920 | tf_op jit(solution)/shard_map/ppermute | solution.py:783
  8.9 0.4 collective-permute-start
  9.4 0.1 fusion.3
  9.5 0.2 fusion.1
  9.8 0.7 %copy-done.3 = s32[64,64]{1,0:T(8,128)S(1)} copy-done((s32[64,64]{1,0:T(8,128)S(1)}, s32[64,64]{1,0:T(8,128)}, u32[]{:S(2)}) %copy-start.3) | copy-done | bytes 16408
  10.5 0.1 slice.11
  10.6 0.4 collective-permute-done.2.p1
  11.0 0.9 %collective-permute-done.3.p2 = bf16[8,3456]{1,0:T(8,128)(2,1)S(1)} collective-permute-done((bf16[8,3456]{1,0:T(8,128)(2,1)S(1)}, bf16[8,3456]{1,0:T(8,128)(2,1)S(1)}, u32[]{:S(2)}, u32[]{:S(2)}) %collective-permute-start.3) | collective-permute-done | bytes 55328 | tf_op jit(solution)/shard_map/ppermute | solution.py:722
  11.9 2.5 %collective-permute-start.6 = (bf16[4,8,3456]{2,1,0:T(8,128)(2,1)S(1)}, bf16[4,8,3456]{2,1,0:T(8,128)(2,1)S(1)}, u32[]{:S(2)}, u32[]{:S(2)}) collective-permute-start(bf16[4,8,3456]{2,1,0:T(8,128)(2,1)S(1)} %shard_map.180.p0), channel_id=1, source_target_pairs={{0,24},{4,28},{8,16},{12,20},{16,8},{20,12},{24,0},{28,4},{1,25},{... | collective-permute-start | bytes 663560 | tf_op jit(solution)/shard_map/ppermute | solution.py:722
  14.5 0.1 copy.24
  14.6 0.1 broadcast_in_dim.49
  14.6 0.1 reshape.363.id_key_ref
  14.7 0.6 collective-permute-start.8
  15.3 0.5 collective-permute-start.5
  15.9 0.6 %copy-done.2 = f32[4]{0:T(128)S(1)} copy-done((f32[4]{0:T(128)S(1)}, f32[4]{0:T(128)}, u32[]{:S(2)}) %copy-start.2) | copy-done | bytes 40
  16.5 1.3 %shard_map.178 = (f32[1024,256]{1,0:T(8,128)S(1)}, bf16[256,1024]{1,0:T(8,128)(2,1)S(1)}, bf16[256,512]{1,0:T(8,128)(2,1)S(1)}, f32[1024,128]{1,0:T(8,128)S(1)},...) custom-call(f32[4]{0:T(128)S(1)} %copy-done.2, ...), custom_call_target="tpu_custom_call" | custom-call | flops 1000000000 | bytes 4000000 | tf_op jit(solution)/shard_map/pallas_call | solution.py:641
  17.8 3.3 %collective-permute-done.6.p3 = bf16[4,8,3456]{2,1,0:T(8,128)(2,1)S(1)} collective-permute-done((bf16[4,8,3456]{2,1,0:T(8,128)(2,1)S(1)}, bf16[4,8,3456]{2,1,0:T(8,128)(2,1)S(1)}, u32[]{:S(2)}, u32[]{:S(2)}) %collective-permute-start.6) | collective-permute-done | bytes 221216 | tf_op jit(solution)/shard_map/ppermute | solution.py:722
  21.1 0.5 collective-permute-start.9
  21.6 2.4 %collective-permute-done.8.p2 = bf16[4,8,3456]{2,1,0:T(8,128)(2,1)S(1)} collective-permute-done((bf16[4,8,3456]{2,1,0:T(8,128)(2,1)S(1)}, bf16[4,8,3456]{2,1,0:T(8,128)(2,1)S(1)}, u32[]{:S(2)}, u32[]{:S(2)}) %collective-permute-start.8) | collective-permute-done | bytes 221216 | tf_op jit(solution)/shard_map/ppermute | solution.py:722
  24.0 0.2 collective-permute-done.5.p1
  24.2 0.5 collective-permute-start.10
  24.7 1.0 %collective-permute-done.11.p6 = bf16[4,8,3456]{2,1,0:T(8,128)(2,1)S(1)} collective-permute-done((bf16[4,8,3456]{2,1,0:T(8,128)(2,1)S(1)}, bf16[4,8,3456]{2,1,0:T(8,128)(2,1)S(1)}, u32[]{:S(2)}, u32[]{:S(2)}) %collective-permute-start.11) | collective-permute-done | bytes 221216 | tf_op jit(solution)/shard_map/ppermute | solution.py:722
  25.7 0.3 collective-permute-done.10.p5
  26.0 5.4 %shard_map.181 = (bf16[1024,256]{1,0:T(8,128)(2,1)S(1)}, bf16[1024,256]{1,0:T(8,128)(2,1)S(1)}, bf16[1024,256]{1,0:T(8,128)(2,1)S(1)}, bf16[4,512,256]{2,1,0:T(8...) custom-call(f32[1,128]{1,0:T(1,128)S(1)} %get-tuple-element.85.root_, ...), custom_call_target="tpu_custom_call" | custom-call | flops 1000000000 | bytes 4000000 | tf_op jit(solution)/shard_map/pallas_call | solution.py:641
  31.4 0.3 collective-permute-start.13
  31.7 3.0 %shard_map.182 = (bf16[512,256]{1,0:T(8,128)(2,1)S(1)}, bf16[1024,512]{1,0:T(8,128)(2,1)S(1)}, bf16[4,4,8,896]{3,2,1,0:T(8,128)(2,1)S(1)}, bf16[4,4,8,896]{3,2,1,0:T(8,128)(2,1)S(1)}) custom-call(f32[1,128]{1,0:T(1,128)S(1)} %get-tuple-element.85.root_ref, bf16[512,256]{1,0:T(8,128)(2,1)S(1)} %get-tuple-element.102.shrunk_ref, ...), custom_call_target="tpu_custom_call" | custom-call | flops 1 | bytes 1 | tf_op jit(solution)/shard_map/pallas_call | solution.py:641
  34.7 0.3 collective-permute-start.12
  35.0 0.2 shard_map.183
  35.2 1.1 %collective-permute-done.12.got_ref = bf16[4,4,8,896]{3,2,1,0:T(8,128)(2,1)S(1)} collective-permute-done((bf16[4,4,8,896]{3,2,1,0:T(8,128)(2,1)S(1)}, bf16[4,4,8,896]{3,2,1,0:T(8,128)(2,1)S(1)}, u32[]{:S(2)}, u32[]{:S(2)}) %collective-permute-start.12) | collective-permute-done | bytes 229408 | tf_op jit(solution)/shard_map/ppermute | solution.py:722
  36.3 1.5 %collective-permute-start.14 = (bf16[4,8,3456]{2,1,0:T(8,128)(2,1)S(1)}, bf16[4,8,3456]{2,1,0:T(8,128)(2,1)S(1)}, u32[]{:S(2)}, u32[]{:S(2)}) collective-permute-start(bf16[4,8,3456]{2,1,0:T(8,128)(2,1)S(1)} %get-tuple-element.132), channel_id=1, source_target_pairs={{0,8},{4,20},{8,0},{12,28},{16,24},{20,4},{24,16},{28,12},{1,9},{5... | collective-permute-start | bytes 663560 | tf_op jit(solution)/shard_map/ppermute | solution.py:734
  37.9 0.5 collective-permute-start.16
  38.4 3.9 %collective-permute-done.14.two_ref = bf16[4,8,3456]{2,1,0:T(8,128)(2,1)S(1)} collective-permute-done((bf16[4,8,3456]{2,1,0:T(8,128)(2,1)S(1)}, bf16[4,8,3456]{2,1,0:T(8,128)(2,1)S(1)}, u32[]{:S(2)}, u32[]{:S(2)}) %collective-permute-start.14) | collective-permute-done | bytes 221216 | tf_op jit(solution)/shard_map/ppermute | solution.py:734
  42.4 1.5 %collective-permute-start.15 = (bf16[4,8,3456]{2,1,0:T(8,128)(2,1)S(1)}, bf16[4,8,3456]{2,1,0:T(8,128)(2,1)S(1)}, u32[]{:S(2)}, u32[]{:S(2)}) collective-permute-start(bf16[4,8,3456]{2,1,0:T(8,128)(2,1)S(1)} %shard_map.185), channel_id=1, source_target_pairs={{0,16},{4,12},{8,24},{12,4},{16,0},{20,28},{24,8},{28,20},{1,17},{... | collective-permute-start | bytes 663560 | tf_op jit(solution)/shard_map/ppermute | solution.py:731
  43.9 0.5 shard_map.187
  44.5 1.6 %collective-permute-start.18 = (bf16[192,256]{1,0:T(8,128)(2,1)S(1)}, bf16[192,256]{1,0:T(8,128)(2,1)S(1)}, u32[]{:S(2)}, u32[]{:S(2)}) collective-permute-start(bf16[192,256]{1,0:T(8,128)(2,1)S(1)} %get-tuple-element.147), channel_id=1, source_target_pairs={{0,28},{4,8},{8,4},{12,16},{16,12},{20,24},{24,20},{28,0},{1,29},{... | collective-permute-start | bytes 294920 | tf_op jit(solution)/shard_map/ppermute | solution.py:783
  46.1 2.3 %collective-permute-done.15.p1 = bf16[4,8,3456]{2,1,0:T(8,128)(2,1)S(1)} collective-permute-done((bf16[4,8,3456]{2,1,0:T(8,128)(2,1)S(1)}, bf16[4,8,3456]{2,1,0:T(8,128)(2,1)S(1)}, u32[]{:S(2)}, u32[]{:S(2)}) %collective-permute-start.15) | collective-permute-done | bytes 221216 | tf_op jit(solution)/shard_map/ppermute | solution.py:731
  48.4 0.1 shard_map.186
  48.6 1.1 %collective-permute-start.19 = (bf16[8,3456]{1,0:T(8,128)(2,1)S(1)}, bf16[8,3456]{1,0:T(8,128)(2,1)S(1)}, u32[]{:S(2)}, u32[]{:S(2)}) collective-permute-start(bf16[8,3456]{1,0:T(8,128)(2,1)S(1)} %get-tuple-element.151), channel_id=1, source_target_pairs={{0,1},{1,0},{2,3},{3,2},{4,5},{5,4},{6,7},{7,6},{8,9},{9,8},{10,11... | collective-permute-start | bytes 165896 | tf_op jit(solution)/shard_map/ppermute | solution.py:722
  49.6 2.8 %collective-permute-start.20 = (bf16[8,3456]{1,0:T(8,128)(2,1)S(1)}, bf16[8,3456]{1,0:T(8,128)(2,1)S(1)}, u32[]{:S(2)}, u32[]{:S(2)}) collective-permute-start(bf16[8,3456]{1,0:T(8,128)(2,1)S(1)} %get-tuple-element.152), channel_id=1, source_target_pairs={{0,2},{1,3},{2,0},{3,1},{4,6},{5,7},{6,4},{7,5},{8,10},{9,11},{10,... | collective-permute-start | bytes 165896 | tf_op jit(solution)/shard_map/ppermute | solution.py:722
  52.4 0.6 collective-permute-start.21
  53.0 1.1 %shard_map.188 = bf16[8,64,256]{2,1,0:T(8,128)(2,1)} custom-call(f32[512,256]{1,0:T(8,128)S(1)} %get-tuple-element.101.middle_ref, bf16[512,768]{1,0:T(8,128)(2,1)S(1)} %get-tuple-element.142.gated_ref, bf16[768,256]{1,0:T(8,128)(2,1)S(1)} %get-tuple-element.143.w_down_ref), custom_call_target="tpu_custom_call" | custom-call | flops 1000000000 | bytes 4000000 | tf_op jit(solution)/shard_map/pallas_call | solution.py:641
  54.1 1.1 %shard_map.189 = f32[8,64,256]{2,1,0:T(8,128)} custom-call(f32[512,256]{1,0:T(8,128)S(1)} %get-tuple-element.90.inputs_ref, f32[2,256]{1,0:T(2,128)S(1)} %get-tuple-element.144.gain_ref, f32[512,256]{1,0:T(8,128)S(1)} %get-tuple-element.145.own_ref, bf16[192,256]{1,0:T(8,128)(2,1)S(1)} %collective-permute-done.17.rim_swap_ref, ...), custom_call_target="tpu_custom_call" | custom-call | flops 1000000000 | bytes 4000000 | tf_op jit(solution)/shard_map/pallas_call | solution.py:641
  55.2 0.7 %collective-permute-done.20.two_ref = bf16[8,3456]{1,0:T(8,128)(2,1)S(1)} collective-permute-done((bf16[8,3456]{1,0:T(8,128)(2,1)S(1)}, bf16[8,3456]{1,0:T(8,128)(2,1)S(1)}, u32[]{:S(2)}, u32[]{:S(2)}) %collective-permute-start.20) | collective-permute-done | bytes 55328 | tf_op jit(solution)/shard_map/ppermute | solution.py:722
  55.9 2.5 %collective-permute-done.21.three_ref = bf16[8,3456]{1,0:T(8,128)(2,1)S(1)} collective-permute-done((bf16[8,3456]{1,0:T(8,128)(2,1)S(1)}, bf16[8,3456]{1,0:T(8,128)(2,1)S(1)}, u32[]{:S(2)}, u32[]{:S(2)}) %collective-permute-start.21) | collective-permute-done | bytes 55328 | tf_op jit(solution)/shard_map/ppermute | solution.py:722
  58.4 0.7 %shard_map.190 = (f32[8,768]{1,0:T(8,128)}, f32[8,256]{1,0:T(8,128)}, f32[8,1536]{1,0:T(8,128)}, f32[24,256]{1,0:T(8,128)}, f32[24,256]{1,0:T(8,128)}, /*index=5*/f32[24,256]{1,0:T(8,128)}, f32[4]{0:T(128)}) custom-call(f32[24,2]{1,0:T(8,128)S(1)} %get-tuple-element.149.cond_ref, f32[8,3456]{1,0:T(8,128)S(1)} %get-tuple-element.150.own_ref, ...), custom_call_target="tpu_custom_call" | custom-call | flops 1000000000 | bytes 4000000 | tf_op jit(solution)/shard_map/pallas_call | solution.py:641
  (34 shorter events, 0.4 us)
Async XLA Ops:
  0.6 6.8 %copy-start = (bf16[8,64,256]{2,1,0:T(8,128)(2,1)S(1)}, bf16[8,64,256]{2,1,0:T(8,128)(2,1)}, u32[]{:S(2)}) copy-start(bf16[8,64,256]{2,1,0:T(8,128)(2,1)} %feat_ref.1) | copy-start | bytes 786436
  1.7 9.3 %collective-permute-start.4 = (bf16[8,3456]{1,0:T(8,128)(2,1)S(1)}, bf16[8,3456]{1,0:T(8,128)(2,1)S(1)}, u32[]{:S(2)}, u32[]{:S(2)}) collective-permute-start(bf16[8,3456]{1,0:T(8,128)(2,1)S(1)} %get-tuple-element.93), channel_id=1, source_target_pairs={{0,3},{1,2},{2,1},{3,0},{4,7},{5,6},{6,5},{7,4},{8,11},{9,10},{10,... | collective-permute-start | bytes 165896 | tf_op jit(solution)/shard_map/ppermute | solution.py:722
  6.8 5.1 %collective-permute-start.3 = (bf16[8,3456]{1,0:T(8,128)(2,1)S(1)}, bf16[8,3456]{1,0:T(8,128)(2,1)S(1)}, u32[]{:S(2)}, u32[]{:S(2)}) collective-permute-start(bf16[8,3456]{1,0:T(8,128)(2,1)S(1)} %get-tuple-element.93), channel_id=1, source_target_pairs={{0,2},{1,3},{2,0},{3,1},{4,6},{5,7},{6,4},{7,5},{8,10},{9,11},{10,... | collective-permute-start | bytes 165896 | tf_op jit(solution)/shard_map/ppermute | solution.py:722
  6.8 4.2 %collective-permute-start.2 = (bf16[8,3456]{1,0:T(8,128)(2,1)S(1)}, bf16[8,3456]{1,0:T(8,128)(2,1)S(1)}, u32[]{:S(2)}, u32[]{:S(2)}) collective-permute-start(bf16[8,3456]{1,0:T(8,128)(2,1)S(1)} %get-tuple-element.92.p0), channel_id=1, source_target_pairs={{0,1},{1,0},{2,3},{3,2},{4,5},{5,4},{6,7},{7,6},{8,9},{9,8},{10,11... | collective-permute-start | bytes 165896 | tf_op jit(solution)/shard_map/ppermute | solution.py:722
  7.5 8.3 %collective-permute-start.1 = (bf16[3,64,256]{2,1,0:T(8,128)(2,1)S(1)}, bf16[3,64,256]{2,1,0:T(8,128)(2,1)S(1)}, u32[]{:S(2)}, u32[]{:S(2)}) collective-permute-start(bf16[3,64,256]{2,1,0:T(8,128)(2,1)S(1)} %get-tuple-element.161), channel_id=1, source_target_pairs={{0,28},{4,8},{8,4},{12,16},{16,12},{20,24},{24,20},{28,0},{1,29},{... | collective-permute-start | bytes 294920 | tf_op jit(solution)/shard_map/ppermute | solution.py:783
  8.9 6.9 %collective-permute-start = (bf16[3,64,256]{2,1,0:T(8,128)(2,1)S(1)}, bf16[3,64,256]{2,1,0:T(8,128)(2,1)S(1)}, u32[]{:S(2)}, u32[]{:S(2)}) collective-permute-start(bf16[3,64,256]{2,1,0:T(8,128)(2,1)S(1)} %get-tuple-element.162), channel_id=1, source_target_pairs={{0,4},{4,0},{8,12},{12,8},{16,20},{20,16},{24,28},{28,24},{1,5},{5... | collective-permute-start | bytes 294920 | tf_op jit(solution)/shard_map/ppermute | solution.py:722
  9.8 0.8 %copy-start.3 = (s32[64,64]{1,0:T(8,128)S(1)}, s32[64,64]{1,0:T(8,128)}, u32[]{:S(2)}) copy-start(s32[64,64]{1,0:T(8,128)} %param.12) | copy-start | bytes 49156
  11.9 3.9 %copy-start.1 = (bf16[8,64,256]{2,1,0:T(8,128)(2,1)S(1)}, bf16[8,64,256]{2,1,0:T(8,128)(2,1)}, u32[]{:S(2)}) copy-start(bf16[8,64,256]{2,1,0:T(8,128)(2,1)} %cot_ref.1) | copy-start | bytes 786436
  11.9 9.2 %collective-permute-start.6 = (bf16[4,8,3456]{2,1,0:T(8,128)(2,1)S(1)}, bf16[4,8,3456]{2,1,0:T(8,128)(2,1)S(1)}, u32[]{:S(2)}, u32[]{:S(2)}) collective-permute-start(bf16[4,8,3456]{2,1,0:T(8,128)(2,1)S(1)} %shard_map.180.p0), channel_id=1, source_target_pairs={{0,24},{4,28},{8,16},{12,20},{16,8},{20,12},{24,0},{28,4},{1,25},{... | collective-permute-start | bytes 663560 | tf_op jit(solution)/shard_map/ppermute | solution.py:722
  14.7 9.3 %collective-permute-start.8 = (bf16[4,8,3456]{2,1,0:T(8,128)(2,1)S(1)}, bf16[4,8,3456]{2,1,0:T(8,128)(2,1)S(1)}, u32[]{:S(2)}, u32[]{:S(2)}) collective-permute-start(bf16[4,8,3456]{2,1,0:T(8,128)(2,1)S(1)} %shard_map.180.p0), channel_id=1, source_target_pairs={{0,16},{4,20},{8,24},{12,28},{16,0},{20,4},{24,8},{28,12},{1,17},{... | collective-permute-start | bytes 663560 | tf_op jit(solution)/shard_map/ppermute | solution.py:722
  15.3 8.9 %collective-permute-start.5 = (bf16[4,8,3456]{2,1,0:T(8,128)(2,1)S(1)}, bf16[4,8,3456]{2,1,0:T(8,128)(2,1)S(1)}, u32[]{:S(2)}, u32[]{:S(2)}) collective-permute-start(bf16[4,8,3456]{2,1,0:T(8,128)(2,1)S(1)} %shard_map.180.p0), channel_id=1, source_target_pairs={{0,8},{4,12},{8,0},{12,4},{16,24},{20,28},{24,16},{28,20},{1,9},{5... | collective-permute-start | bytes 663560 | tf_op jit(solution)/shard_map/ppermute | solution.py:722
  15.9 0.7 %copy-start.2 = (f32[4]{0:T(128)S(1)}, f32[4]{0:T(128)}, u32[]{:S(2)}) copy-start(f32[4]{0:T(128)} %scale_ref.1) | copy-start | bytes 52
  21.1 3.1 %collective-permute-start.7 = (bf16[4,8,3456]{2,1,0:T(8,128)(2,1)S(1)}, bf16[4,8,3456]{2,1,0:T(8,128)(2,1)S(1)}, u32[]{:S(2)}, u32[]{:S(2)}) collective-permute-start(bf16[4,8,3456]{2,1,0:T(8,128)(2,1)S(1)} %collective-permute-done.6.p3), channel_id=1, source_target_pairs={{0,4},{4,0},{8,12},{12,8},{16,20},{20,16},{24,28},{28,24},{1,5},{5... | collective-permute-start | bytes 663560 | tf_op jit(solution)/shard_map/ppermute | solution.py:722
  21.1 3.6 %collective-permute-start.9 = (bf16[4,8,3456]{2,1,0:T(8,128)(2,1)S(1)}, bf16[4,8,3456]{2,1,0:T(8,128)(2,1)S(1)}, u32[]{:S(2)}, u32[]{:S(2)}) collective-permute-start(bf16[4,8,3456]{2,1,0:T(8,128)(2,1)S(1)} %shard_map.180.p0), channel_id=1, source_target_pairs={{0,4},{4,0},{8,12},{12,8},{16,20},{20,16},{24,28},{28,24},{1,5},{5... | collective-permute-start | bytes 663560 | tf_op jit(solution)/shard_map/ppermute | solution.py:722
  24.2 1.5 %collective-permute-start.11 = (bf16[4,8,3456]{2,1,0:T(8,128)(2,1)S(1)}, bf16[4,8,3456]{2,1,0:T(8,128)(2,1)S(1)}, u32[]{:S(2)}, u32[]{:S(2)}) collective-permute-start(bf16[4,8,3456]{2,1,0:T(8,128)(2,1)S(1)} %collective-permute-done.8.p2), channel_id=1, source_target_pairs={{0,4},{4,0},{8,12},{12,8},{16,20},{20,16},{24,28},{28,24},{1,5},{5... | collective-permute-start | bytes 663560 | tf_op jit(solution)/shard_map/ppermute | solution.py:722
  24.2 1.8 %collective-permute-start.10 = (bf16[4,8,3456]{2,1,0:T(8,128)(2,1)S(1)}, bf16[4,8,3456]{2,1,0:T(8,128)(2,1)S(1)}, u32[]{:S(2)}, u32[]{:S(2)}) collective-permute-start(bf16[4,8,3456]{2,1,0:T(8,128)(2,1)S(1)} %collective-permute-done.5.p1), channel_id=1, source_target_pairs={{0,4},{4,0},{8,12},{12,8},{16,20},{20,16},{24,28},{28,24},{1,5},{5... | collective-permute-start | bytes 663560 | tf_op jit(solution)/shard_map/ppermute | solution.py:722
  31.4 3.7 %collective-permute-start.13 = (bf16[4,4,8,2560]{3,2,1,0:T(8,128)(2,1)S(1)}, bf16[4,4,8,2560]{3,2,1,0:T(8,128)(2,1)S(1)}, u32[]{:S(2)}, u32[]{:S(2)}) collective-permute-start(bf16[4,4,8,2560]{3,2,1,0:T(8,128)(2,1)S(1)} %get-tuple-element.120), channel_id=1, source_target_pairs={{0,4},{4,0},{8,12},{12,8},{16,20},{20,16},{24,28},{28,24},{1,5},{5... | collective-permute-start | bytes 1966088 | tf_op jit(solution)/shard_map/ppermute | solution.py:722
  34.7 1.6 %collective-permute-start.12 = (bf16[4,4,8,896]{3,2,1,0:T(8,128)(2,1)S(1)}, bf16[4,4,8,896]{3,2,1,0:T(8,128)(2,1)S(1)}, u32[]{:S(2)}, u32[]{:S(2)}) collective-permute-start(bf16[4,4,8,896]{3,2,1,0:T(8,128)(2,1)S(1)} %get-tuple-element.118), channel_id=1, source_target_pairs={{0,4},{4,0},{8,12},{12,8},{16,20},{20,16},{24,28},{28,24},{1,5},{5... | collective-permute-start | bytes 688136 | tf_op jit(solution)/shard_map/ppermute | solution.py:722
  36.3 6.0 %collective-permute-start.14 = (bf16[4,8,3456]{2,1,0:T(8,128)(2,1)S(1)}, bf16[4,8,3456]{2,1,0:T(8,128)(2,1)S(1)}, u32[]{:S(2)}, u32[]{:S(2)}) collective-permute-start(bf16[4,8,3456]{2,1,0:T(8,128)(2,1)S(1)} %get-tuple-element.132), channel_id=1, source_target_pairs={{0,8},{4,20},{8,0},{12,28},{16,24},{20,4},{24,16},{28,12},{1,9},{5... | collective-permute-start | bytes 663560 | tf_op jit(solution)/shard_map/ppermute | solution.py:734
  37.9 8.2 %collective-permute-start.16 = (bf16[4,8,3456]{2,1,0:T(8,128)(2,1)S(1)}, bf16[4,8,3456]{2,1,0:T(8,128)(2,1)S(1)}, u32[]{:S(2)}, u32[]{:S(2)}) collective-permute-start(bf16[4,8,3456]{2,1,0:T(8,128)(2,1)S(1)} %get-tuple-element.133), channel_id=1, source_target_pairs={{0,8},{4,20},{8,0},{12,28},{16,24},{20,4},{24,16},{28,12},{1,9},{5... | collective-permute-start | bytes 663560 | tf_op jit(solution)/shard_map/ppermute | solution.py:734
  42.4 6.0 %collective-permute-start.15 = (bf16[4,8,3456]{2,1,0:T(8,128)(2,1)S(1)}, bf16[4,8,3456]{2,1,0:T(8,128)(2,1)S(1)}, u32[]{:S(2)}, u32[]{:S(2)}) collective-permute-start(bf16[4,8,3456]{2,1,0:T(8,128)(2,1)S(1)} %shard_map.185), channel_id=1, source_target_pairs={{0,16},{4,12},{8,24},{12,4},{16,0},{20,28},{24,8},{28,20},{1,17},{... | collective-permute-start | bytes 663560 | tf_op jit(solution)/shard_map/ppermute | solution.py:731
  44.4 9.7 %collective-permute-start.17 = (bf16[192,256]{1,0:T(8,128)(2,1)S(1)}, bf16[192,256]{1,0:T(8,128)(2,1)S(1)}, u32[]{:S(2)}, u32[]{:S(2)}) collective-permute-start(bf16[192,256]{1,0:T(8,128)(2,1)S(1)} %get-tuple-element.146), channel_id=1, source_target_pairs={{0,4},{4,0},{8,12},{12,8},{16,20},{20,16},{24,28},{28,24},{1,5},{5... | collective-permute-start | bytes 294920 | tf_op jit(solution)/shard_map/ppermute | solution.py:722
  44.5 9.6 %collective-permute-start.18 = (bf16[192,256]{1,0:T(8,128)(2,1)S(1)}, bf16[192,256]{1,0:T(8,128)(2,1)S(1)}, u32[]{:S(2)}, u32[]{:S(2)}) collective-permute-start(bf16[192,256]{1,0:T(8,128)(2,1)S(1)} %get-tuple-element.147), channel_id=1, source_target_pairs={{0,28},{4,8},{8,4},{12,16},{16,12},{20,24},{24,20},{28,0},{1,29},{... | collective-permute-start | bytes 294920 | tf_op jit(solution)/shard_map/ppermute | solution.py:783
  48.6 6.6 %collective-permute-start.19 = (bf16[8,3456]{1,0:T(8,128)(2,1)S(1)}, bf16[8,3456]{1,0:T(8,128)(2,1)S(1)}, u32[]{:S(2)}, u32[]{:S(2)}) collective-permute-start(bf16[8,3456]{1,0:T(8,128)(2,1)S(1)} %get-tuple-element.151), channel_id=1, source_target_pairs={{0,1},{1,0},{2,3},{3,2},{4,5},{5,4},{6,7},{7,6},{8,9},{9,8},{10,11... | collective-permute-start | bytes 165896 | tf_op jit(solution)/shard_map/ppermute | solution.py:722
  49.6 6.2 %collective-permute-start.20 = (bf16[8,3456]{1,0:T(8,128)(2,1)S(1)}, bf16[8,3456]{1,0:T(8,128)(2,1)S(1)}, u32[]{:S(2)}, u32[]{:S(2)}) collective-permute-start(bf16[8,3456]{1,0:T(8,128)(2,1)S(1)} %get-tuple-element.152), channel_id=1, source_target_pairs={{0,2},{1,3},{2,0},{3,1},{4,6},{5,7},{6,4},{7,5},{8,10},{9,11},{10,... | collective-permute-start | bytes 165896 | tf_op jit(solution)/shard_map/ppermute | solution.py:722
  52.4 6.0 %collective-permute-start.21 = (bf16[8,3456]{1,0:T(8,128)(2,1)S(1)}, bf16[8,3456]{1,0:T(8,128)(2,1)S(1)}, u32[]{:S(2)}, u32[]{:S(2)}) collective-permute-start(bf16[8,3456]{1,0:T(8,128)(2,1)S(1)} %get-tuple-element.153), channel_id=1, source_target_pairs={{0,3},{1,2},{2,1},{3,0},{4,7},{5,6},{6,5},{7,4},{8,11},{9,10},{10,... | collective-permute-start | bytes 165896 | tf_op jit(solution)/shard_map/ppermute | solution.py:722

commit v2 on v1

--- a/solution.py
+++ b/solution.py
@@ -133,28 +133,32 @@
     return lax.rsqrt(jnp.mean(values * values, axis=-1, keepdims=True) + EPS)
 
 
-def place_parts(place, part_refs, wide_ref, last):
-    lanes = wide_ref.shape[-1]
+def place_parts(place, part_refs):
     for index, part in enumerate(part_refs):
         chip = place[1] ^ (index % 4)
         core = place[2] ^ (index // 4)
         group = part.shape[0]
-        start = part.shape[-1] - lanes if last else 0
-        for col in range(group):
-            wide_ref[(chip * 2 + core) * group + col] = part[col, :, start : start + lanes].astype(F32)
-
-
-def columns(wide_ref, start, width):
-    chunks = wide_ref.shape[0]
-    return wide_ref[:, :, start : start + width].reshape(chunks * 8, width).astype(BF16)
-
-
-def split_parts(place, wide_ref, mine_ref, other_ref):
-    group = mine_ref.shape[1]
-    for chip in range(mine_ref.shape[0]):
-        for col in range(group):
-            mine_ref[chip, col] = wide_ref[(chip * 2 + place[2]) * group + col].astype(BF16)
-            other_ref[chip, col] = wide_ref[(chip * 2 + 1 - place[2]) * group + col].astype(BF16)
+        yield (chip * 2 + core) * group, part[...].astype(F32)
+
+
+def store_rows(ref, start, rows):
+    group, count, lanes = rows.shape
+    ref[pl.ds(pl.multiple_of(start * count, group * count), group * count), :] = rows.reshape(
+        group * count, lanes
+    ).astype(ref.dtype)
+
+
+def split_parts(place, values, mine_ref, other_ref, start):
+    chips, group = mine_ref.shape[:2]
+    count = values.shape[0] // (2 * chips)
+    first = place[2] == 0
+    for chip in range(chips):
+        zero, one = [values[(2 * chip + core) * count : (2 * chip + core + 1) * count] for core in range(2)]
+        for ref, part in ((mine_ref, jnp.where(first, zero, one)), (other_ref, jnp.where(first, one, zero))):
+            part = part.reshape(group, count // group, values.shape[1])
+            for i in range(count // group // 8):
+                at = start + i * values.shape[1]
+                ref[chip, :, :, at : at + values.shape[1]] = part[:, 8 * i : 8 * i + 8].astype(BF16)
 
 
 def pack_kernel(
@@ -195,33 +199,37 @@
             at += part.shape[1]
 
 
-def line_kernel(place, p0, p1, p2, p3, line_ref):
-    for index, part in enumerate((p0, p1, p2, p3)):
+def line_kernel(order, place, p0, p1, p2, p3, line_ref):
+    for index, part in zip((0,) + order, (p0, p1, p2, p3)):
         line_ref[place[3] ^ index] = part[...]
 
 
-def core_sum_kernel(place, mine_ref, got_ref, *refs):
-    lanes = mine_ref.shape[-1]
-    for index, out_ref in enumerate(refs[-4:]):
+def core_sum_kernel(place, mine_ref, got_ref, *outs):
+    for index, out_ref in enumerate(outs):
         chip = place[1] ^ (0, place[6], place[6] ^ 3, 3)[index]
-        start = 0 if len(refs) == 4 else out_ref.shape[-1] - lanes
-        out_ref[:, :, start : start + lanes] = (
-            mine_ref[chip].astype(F32) + got_ref[chip].astype(F32)
-        ).astype(BF16)
+        out_ref[...] = (mine_ref[chip].astype(F32) + got_ref[chip].astype(F32)).astype(BF16)
+
+
+def join_kernel(one_ref, two_ref, out_ref):
+    split = one_ref.shape[-1]
+    out_ref[:, :, :split] = one_ref[...]
+    out_ref[:, :, split:] = two_ref[...]
 
 
 def pair_sum_kernel(one_ref, two_ref, out_ref):
     out_ref[...] = (one_ref[...].astype(F32) + two_ref[...].astype(F32)).astype(BF16)
 
 
-def chip_sum_kernel(place, p0, p1, p2, o0, o1, o2, o3, keep_ref):
-    keep_ref[...] = p0[...].astype(F32) + p1[...].astype(F32) + p2[...].astype(F32)
+def chip_sum_kernel(place, p0, p1, q0, q1, both, o0, o1, o2, o3, keep_ref):
+    split = p0.shape[-1]
+    keep_ref[:, :, :split] = p0[...].astype(F32) + p1[...].astype(F32) + both[:, :, :split].astype(F32)
+    keep_ref[:, :, split:] = q0[...].astype(F32) + q1[...].astype(F32) + both[:, :, split:].astype(F32)
     for index, out_ref in enumerate((o0, o1, o2, o3)):
         out_ref[...] = keep_ref[place[3] ^ index].astype(out_ref.dtype)
 
 
 def last_kernel(
-    per_canvas, size, place, cond_ref, own_ref, one_ref, two_ref, three_ref,
+    per_canvas, size, place, cond_ref, own_ref, three_ref, two_ref, one_ref,
     qkv_ref, out_ref, up_ref, down_ref, attn_ref, feed_ref, scale_ref,
 ):
     parts = [own_ref[...]] + [ref[...].astype(F32) for ref in (one_ref, two_ref, three_ref)]
@@ -299,24 +307,21 @@
 
 
 def attend_kernel(
-    heads, place, root_ref, unit_ref, cos_ref, sine_ref, mask_ref, p0, p1, p2, p3, p4, p5, p6, p7,
+    heads, root_ref, unit_ref, cos_ref, sine_ref, mask_ref, sums, raw_ref,
     query_ref, key_ref, value_ref, raised_ref, mixed_ref, inverse_ref, along_q_ref, length_q_ref, along_k_ref, length_k_ref,
     gain_ref, gain_col_ref, w_ref,
-    wide_ref,
 ):
     bands, count = mask_ref.shape[:2]
     width = unit_ref.shape[1]
     size = width // heads
     edge = REACH * BAND
-    place_parts(place, (p0, p1, p2, p3, p4, p5, p6, p7), wide_ref, False)
-    weight = columns(wide_ref, 0, 3 * width)
+    weight = raw_ref[...]
     order = turned_order(width, heads)
     turned = mm(
         jnp.concatenate([weight[:, :width], weight[:, width : 2 * width]], axis=0), order
     ).astype(BF16)
     w_ref[:, :width], w_ref[:, width : 2 * width] = turned[:width], turned[width:]
     w_ref[:, 2 * width :] = weight[:, 2 * width :]
-    sums = jnp.sum(wide_ref[:, :, 3 * width :], axis=0)
     pairs = [sums[i : i + 2] + sums[i + 2 : i + 4] for i in (0, 4)]
     picked = 1.0 + jnp.concatenate(
         [jnp.concatenate([pair[0:1], pair[1:2]], axis=1) for pair in pairs], axis=0
@@ -362,31 +367,13 @@
 
 
 def feed_kernel(
-    heads, place, inputs_ref, cot_ref, p0, p1, p2, p3, p4, p5, p6, p7, gain_ref, mixed_ref, inverse_ref,
+    heads, inputs_ref, cot_ref, w_up_ref, w_out_ref, gain_ref, mixed_ref, inverse_ref,
     middle_ref, middle_grad_ref, shrunk_ref, gain_grad_ref,
     w_down_ref, mixed_low_ref, normed_ref, gated_ref, d_exp_ref, branch_ref,
-    wide_ref,
 ):
     width = inputs_ref.shape[1]
-    chunks = wide_ref.shape[0]
     hidden = w_down_ref.shape[0]
-    own_down = hidden // chunks
-    ups = 2 * hidden
-    place_parts(place, (p0, p1, p2, p3, p4, p5, p6, p7), wide_ref, True)
-    w_up = columns(wide_ref, 0, ups)
-    w_out = columns(wide_ref, ups, width)
-    w_down = (
-        jnp.concatenate(
-            [
-                wide_ref[:, :, ups + width * (i + 1) : ups + width * (i + 2)]
-                for i in range(own_down // 8)
-            ],
-            axis=1,
-        )
-        .reshape(hidden, width)
-        .astype(BF16)
-    )
-    w_down_ref[...] = w_down
+    w_up, w_out, w_down = w_up_ref[...], w_out_ref[...], w_down_ref[...]
     gain_feed = gain_ref[1:2]
     mixed = mixed_ref[...]
     mixed_low = mixed.astype(BF16)
@@ -426,22 +413,11 @@
     shrunk_ref[...] = (mm_rt(branch, w_out) * inverse_ref[...]).astype(BF16)
 
 
-def weights_kernel(
-    place, cot_ref, mixed_low_ref, normed_ref, gated_ref, d_exp_ref, branch_ref, mine_ref, other_ref, wide_ref
-):
-    width = cot_ref.shape[1]
-    chunks = wide_ref.shape[0]
-    ups = d_exp_ref.shape[1]
-    own_down = gated_ref.shape[1] // chunks
-    wide_ref[:, :, :ups] = mm_lt(normed_ref[...], d_exp_ref[...]).reshape(chunks, 8, ups)
-    wide_ref[:, :, ups : ups + width] = mm_lt(mixed_low_ref[...], branch_ref[...]).reshape(
-        chunks, 8, width
-    )
-    grad = mm_lt(gated_ref[...], cot_ref[...]).reshape(chunks, own_down, width)
-    for i in range(own_down // 8):
-        start = ups + width * (i + 1)
-        wide_ref[:, :, start : start + width] = grad[:, 8 * i : 8 * i + 8]
-    split_parts(place, wide_ref, mine_ref, other_ref)
+def weights_kernel(place, cot_ref, mixed_low_ref, normed_ref, gated_ref, d_exp_ref, branch_ref, mine_ref, other_ref):
+    width, ups = cot_ref.shape[1], d_exp_ref.shape[1]
+    split_parts(place, mm_lt(normed_ref[...], d_exp_ref[...]), mine_ref, other_ref, 0)
+    split_parts(place, mm_lt(mixed_low_ref[...], branch_ref[...]), mine_ref, other_ref, ups)
+    split_parts(place, mm_lt(gated_ref[...], cot_ref[...]), mine_ref, other_ref, ups + width)
 
 
 def output_kernel(middle_ref, gated_ref, w_down_ref, out_ref):
@@ -454,40 +430,6 @@
         )
 
 
-def back_kernel(
-    heads, shrunk_ref, mixed_ref, raised_ref, query_ref, key_ref, value_ref, dq_ref, dk_ref, dv_ref
-):
-    bands, _, keys = raised_ref.shape
-    count = keys // 2
-    edge = REACH * BAND
-    ones_half = jnp.ones((keys, 128), BF16)
-    for band in range(bands):
-        span = slice(band * count, (band + 1) * count)
-        start = band * keys
-        whole = slice(start, start + keys)
-        shrunk = shrunk_ref[span].astype(F32)
-        level_rows = -(shrunk * mixed_ref[span])
-        value = value_ref[whole, :]
-        raised = raised_ref[band]
-        parts, stacks = [], []
-        for pair in range(heads // 2):
-            lanes = slice(128 * pair, 128 * pair + 128)
-            stacks.append(pair_lanes(shrunk, heads, pair))
-            parts.append(
-                mm_rt(
-                    jnp.concatenate([stacks[-1], pair_lanes(level_rows, heads, pair)], axis=1),
-                    jnp.concatenate([value[:, lanes], ones_half], axis=1),
-                )
-            )
-        d_scores = (raised.astype(F32) * jnp.concatenate(parts, axis=0)).astype(BF16)
-        dq_ref[span] = fold_heads(mm(d_scores, key_ref[whole, :]), heads)
-        query = query_ref[start + edge : start + edge + count, :].astype(F32)
-        dk_ref[whole, :] = mm_lt(d_scores, stack_heads(query, heads))
-        for pair in range(heads // 2):
-            lanes = slice(128 * pair, 128 * pair + 128)
-            dv_ref[whole, lanes] = mm_lt(raised[2 * pair * count : 2 * (pair + 1) * count], stacks[pair])
-
-
 def pull_head(grad, along, length, cos, sine, heads):
     first, second = halves(grad)
     along_first, along_second = halves(along)
@@ -505,49 +447,6 @@
     for start in range(128, product.shape[1], 128):
         total = total + product[:, start : start + 128]
     return jnp.sum(jnp.transpose(total), axis=0, keepdims=True)
-
-
-def project_kernel(
-    heads, rows, place, root_ref, cos_ref, sine_ref, w_ref, gain_col_ref, unit_turned_ref, own_turned_ref,
-    along_q_ref, length_q_ref, along_k_ref, length_k_ref, dq_ref, dk_ref, dv_ref, gain_grad_ref,
-    d_query_ref, d_rest_ref, mine_ref, other_ref, wide_ref,
-):
-    tokens, width = dq_ref.shape
-    chunks = wide_ref.shape[0]
-    cos, sine = cos_ref[...], sine_ref[...]
-    count = rows * BAND
-    d_key, along_k = pull_head(dk_ref[...], along_k_ref[...], length_k_ref[...], cos, sine, heads)
-    d_value = dv_ref[...].astype(BF16)
-    d_query, along_q = pull_head(
-        dq_ref[...], along_q_ref[...], length_q_ref[...], own_rows(cos, count), own_rows(sine, count), heads
-    )
-    d_query_ref[...] = d_query
-    d_rest = jnp.concatenate([d_key, d_value], axis=1)
-    d_rest_ref[...] = d_rest
-    plain = jnp.concatenate(
-        [
-            mm(own_turned_ref[...], d_query),
-            mm(unit_turned_ref[...], d_rest),
-        ],
-        axis=1,
-    )
-    scaled = plain * jnp.concatenate([gain_col_ref[...]] * (3 * width // 128), axis=1)
-    turned = jnp.concatenate([scaled[:, :width], scaled[:, width : 2 * width]], axis=0).astype(BF16)
-    plain_order = mm_rt(turned, turned_order(width, heads))
-    wide_ref[:, :, :width] = plain_order[:width].reshape(chunks, 8, width)
-    wide_ref[:, :, width : 2 * width] = plain_order[width:].reshape(chunks, 8, width)
-    wide_ref[:, :, 2 * width : 3 * width] = scaled[:, 2 * width :].reshape(chunks, 8, width)
-    gain_total = lane_sums(plain * w_ref[...].astype(F32))
-    lines = []
-    for total in (gain_total, gain_grad_ref[...]):
-        lines += [total[:, :128], total[:, 128:]]
-    total = (along_q + along_k) * 0.5 / root_ref[...]
-    high = total.astype(BF16).astype(F32)
-    lines += [high, total - high, jnp.zeros((2, 128), F32)]
-    wide_ref[:, :, 3 * width :] = jnp.broadcast_to(
-        jnp.concatenate(lines, axis=0)[None], (chunks, 8, 128)
-    )
-    split_parts(place, wide_ref, mine_ref, other_ref)
 
 
 def normed_back_kernel(
@@ -594,39 +493,96 @@
     query_ref, key_ref, value_ref, raised_ref, mixed_ref, along_q_ref, length_q_ref, along_k_ref, length_k_ref,
     gain_ref, gain_col_ref, w_ref, middle_ref, middle_grad_ref, shrunk_ref, gain_grad_ref,
     w_down_ref, gated_ref, mine_ref, other_ref,
-    inverse_ref, first_wide_ref, second_wide_ref, mixed_low_ref, normed_ref, d_exp_ref, branch_ref,
+    inverse_ref, raw_ref, w_up_ref, w_out_ref, mixed_low_ref, normed_ref, d_exp_ref, branch_ref,
 ):
-    parts = (p0, p1, p2, p3, p4, p5, p6, p7)
+    width = inputs_ref.shape[1]
+    first, ups = 3 * width + 128, w_up_ref.shape[1]
+    sums = jnp.zeros((8, 128), F32)
+    for start, rows in place_parts(place, (p0, p1, p2, p3, p4, p5, p6, p7)):
+        store_rows(raw_ref, start, rows[:, :, : 3 * width])
+        sums = sums + jnp.sum(rows[:, :, 3 * width : first], axis=0)
+        store_rows(w_up_ref, start, rows[:, :, first : first + ups])
+        store_rows(w_out_ref, start, rows[:, :, first + ups : first + ups + width])
+        down = [rows[:, :, at : at + width] for at in range(first + ups + width, rows.shape[2], width)]
+        store_rows(w_down_ref, start, jnp.concatenate(down, axis=1))
     attend_kernel(
-        heads, place, root_ref, unit_ref, cos_ref, sine_ref, mask_ref, *parts,
+        heads, root_ref, unit_ref, cos_ref, sine_ref, mask_ref, sums, raw_ref,
         query_ref, key_ref, value_ref, raised_ref, mixed_ref, inverse_ref,
-        along_q_ref, length_q_ref, along_k_ref, length_k_ref, gain_ref, gain_col_ref, w_ref, first_wide_ref,
+        along_q_ref, length_q_ref, along_k_ref, length_k_ref, gain_ref, gain_col_ref, w_ref,
     )
     feed_kernel(
-        heads, place, inputs_ref, cot_ref, *parts, gain_ref, mixed_ref, inverse_ref,
+        heads, inputs_ref, cot_ref, w_up_ref, w_out_ref, gain_ref, mixed_ref, inverse_ref,
         middle_ref, middle_grad_ref, shrunk_ref, gain_grad_ref,
-        w_down_ref, mixed_low_ref, normed_ref, gated_ref, d_exp_ref, branch_ref, second_wide_ref,
+        w_down_ref, mixed_low_ref, normed_ref, gated_ref, d_exp_ref, branch_ref,
     )
     weights_kernel(
-        place, cot_ref, mixed_low_ref, normed_ref, gated_ref, d_exp_ref, branch_ref, mine_ref, other_ref,
-        second_wide_ref,
+        place, cot_ref, mixed_low_ref, normed_ref, gated_ref, d_exp_ref, branch_ref, mine_ref, other_ref
     )
 
 
 def backward_kernel(
     heads, rows, place, root_ref, shrunk_ref, mixed_ref, raised_ref, query_ref, key_ref, value_ref,
-    cos_ref, sine_ref, w_ref, gain_col_ref, unit_turned_ref, own_turned_ref, along_q_ref, length_q_ref, along_k_ref, length_k_ref,
-    gain_grad_ref,
-    d_query_ref, d_rest_ref, mine_ref, other_ref, dq_ref, dk_ref, dv_ref, wide_ref,
+    cos_ref, sine_ref, w_ref, gain_col_ref, unit_turned_ref, own_turned_ref, along_q_ref, length_q_ref,
+    along_k_ref, length_k_ref, gain_grad_ref,
+    d_query_ref, d_rest_ref, mine_ref, other_ref,
 ):
-    back_kernel(
-        heads, shrunk_ref, mixed_ref, raised_ref, query_ref, key_ref, value_ref, dq_ref, dk_ref, dv_ref
-    )
-    project_kernel(
-        heads, rows, place, root_ref, cos_ref, sine_ref, w_ref, gain_col_ref, unit_turned_ref, own_turned_ref,
-        along_q_ref, length_q_ref, along_k_ref, length_k_ref, dq_ref, dk_ref, dv_ref, gain_grad_ref,
-        d_query_ref, d_rest_ref, mine_ref, other_ref, wide_ref,
-    )
+    bands, _, keys = raised_ref.shape
+    count, edge = keys // 2, REACH * BAND
+    width = shrunk_ref.shape[1]
+    ones_half = jnp.ones((keys, 128), BF16)
+    along_total = jnp.zeros((1, width // 2), F32)
+    for band in range(bands):
+        span = slice(band * count, (band + 1) * count)
+        start = band * keys
+        whole = slice(start, start + keys)
+        own = slice(start + edge, start + edge + count)
+        shrunk = shrunk_ref[span].astype(F32)
+        level_rows = -(shrunk * mixed_ref[span])
+        value = value_ref[whole, :]
+        raised = raised_ref[band]
+        parts, stacks = [], []
+        for pair in range(heads // 2):
+            lanes = slice(128 * pair, 128 * pair + 128)
+            stacks.append(pair_lanes(shrunk, heads, pair))
+            parts.append(
+                mm_rt(
+                    jnp.concatenate([stacks[-1], pair_lanes(level_rows, heads, pair)], axis=1),
+                    jnp.concatenate([value[:, lanes], ones_half], axis=1),
+                )
+            )
+        d_scores = (raised.astype(F32) * jnp.concatenate(parts, axis=0)).astype(BF16)
+        query = query_ref[own, :].astype(F32)
+        d_key = mm_lt(d_scores, stack_heads(query, heads))
+        d_query = fold_heads(mm(d_scores, key_ref[whole, :]), heads)
+        for pair in range(heads // 2):
+            lanes = slice(width + 128 * pair, width + 128 * pair + 128)
+            d_value = mm_lt(raised[2 * pair * count : 2 * (pair + 1) * count], stacks[pair])
+            d_rest_ref[whole, lanes] = d_value.astype(BF16)
+        d_rest_ref[whole, :width], along_k = pull_head(
+            d_key, along_k_ref[whole, :], length_k_ref[whole, :], cos_ref[whole, :], sine_ref[whole, :], heads
+        )
+        d_query_ref[span, :], along_q = pull_head(
+            d_query, along_q_ref[span, :], length_q_ref[span, :], cos_ref[own, :], sine_ref[own, :], heads
+        )
+        along_total = along_total + along_k + along_q
+    plain = jnp.concatenate(
+        [mm(own_turned_ref[...], d_query_ref[...]), mm(unit_turned_ref[...], d_rest_ref[...])], axis=1
+    )
+    scaled = plain * jnp.concatenate([gain_col_ref[...]] * (3 * width // 128), axis=1)
+    turned = jnp.concatenate([scaled[:, :width], scaled[:, width : 2 * width]], axis=0).astype(BF16)
+    plain_order = mm_rt(turned, turned_order(width, heads))
+    split_parts(place, plain_order[:width], mine_ref, other_ref, 0)
+    split_parts(place, plain_order[width:], mine_ref, other_ref, width)
+    split_parts(place, scaled[:, 2 * width :], mine_ref, other_ref, 2 * width)
+    lines = []
+    for total in (lane_sums(plain * w_ref[...].astype(F32)), gain_grad_ref[...]):
+        lines += [total[:, :128], total[:, 128:]]
+    total = along_total * 0.5 / root_ref[...]
+    high = total.astype(BF16).astype(F32)
+    lines += [high, total - high, jnp.zeros((2, 128), F32)]
+    tail = jnp.concatenate(lines, axis=0).astype(BF16)
+    for ref in (mine_ref, other_ref):
+        ref[:, :, :, 3 * width :] = jnp.broadcast_to(tail[None, None], ref.shape[:2] + tail.shape)
 
 
 def call(kernel, outs, scratch=(), place=None, smem=0, smem_out=0, flops=10**9, pin=True, aliases=None):
@@ -746,9 +702,10 @@
             place=place,
             pin=False,
         )(conditioning, qkv_weight, up_weight, out_weight, down_weight, attn_cond_weight, feed_cond_weight)
-        line = call(line_kernel, [low(group, 8, first_lanes + second_lanes)], place=place)(
+        z_order = (3, 1, 2)
+        line = call(functools.partial(line_kernel, z_order), [low(group, 8, first_lanes + second_lanes)], place=place)(
             near,
-            *[move(near if k // per_canvas == 0 else far) for k, move in enumerate(z_moves, 1)],
+            *[z_moves[k - 1](near if k // per_canvas == 0 else far) for k in z_order],
         )[0]
         mine = [line] + [move(line) for move in xy_moves]
     else:
@@ -843,8 +800,9 @@
         ],
         scratch=[
             pltpu.VMEM((tokens, width), F32),
-            pltpu.VMEM((chunks, 8, first_lanes), F32),
-            pltpu.VMEM((chunks, 8, second_lanes), F32),
+            pltpu.VMEM((width, 3 * width), BF16),
+            pltpu.VMEM((width, 2 * hidden), BF16),
+            pltpu.VMEM((width, width), BF16),
             pltpu.VMEM((tokens, width), BF16),
             pltpu.VMEM((tokens, width), BF16),
             pltpu.VMEM((tokens, 2 * hidden), BF16),
@@ -861,12 +819,6 @@
             low(chips, group, 8, first_lanes),
             low(chips, group, 8, first_lanes),
         ],
-        scratch=[
-            pltpu.VMEM((tokens, width), F32),
-            pltpu.VMEM((2 * tokens, width), F32),
-            pltpu.VMEM((2 * tokens, width), F32),
-            pltpu.VMEM((chunks, 8, first_lanes), F32),
-        ],
         place=place,
         flops=1,
     )(
@@ -891,17 +843,27 @@
 
     if direct:
         all_lanes = second_lanes + first_lanes
-        lines = [low(group, 8, all_lanes) for _ in range(chips)]
-        second_got = core_move(other_second)
-        sums = call(core_sum_kernel, lines, place=place)(mine_second, second_got)
-        sums = call(core_sum_kernel, lines, place=place, aliases={2 + i: i for i in range(chips)})(
-            mine_first, core_move(other_first), *sums
-        )
-        sums, d_rest = lax.optimization_barrier((sums, d_rest))
-        own, first_part, second_part, far_part = sums
-        far_got, second_got = second_chip(far_part), second_chip(second_part)
-        first_part = call(pair_sum_kernel, [low(group, 8, all_lanes)], flops=1)(first_part, far_got)[0]
-        sums = [own, first_chip(first_part), second_got]
+        def core_sum(mine, got):
+            return call(core_sum_kernel, [low(group, 8, mine.shape[-1]) for _ in range(chips)], place=place)(mine, got)
+
+        def pair_sum(one, two):
+            return call(pair_sum_kernel, [low(*one.shape)], flops=1)(one, two)[0]
+
+        first_got = core_move(other_first)
+        second_own, second_near, second_beside, second_far = core_sum(mine_second, core_move(other_second))
+        second_far = second_chip(second_far)
+        first_own, first_near, first_beside, first_far = core_sum(mine_first, first_got)
+        first_far = second_chip(first_far)
+        second_far, first_far = lax.optimization_barrier((second_far, first_far))
+        first_own, d_rest = lax.optimization_barrier((first_own, d_rest))
+        beside = second_chip(call(join_kernel, [low(group, 8, all_lanes)], flops=1)(second_beside, first_beside)[0])
+        sums = [
+            second_own,
+            first_chip(pair_sum(second_near, second_far)),
+            first_own,
+            first_chip(pair_sum(first_near, first_far)),
+            beside,
+        ]
         own_grad, rim_swap, rim_beside = normed_back(d_query, d_rest)
         rim_swap, rim_beside = core_move(rim_swap), beside_move(rim_beside)
         blocks = call(
@@ -926,7 +888,7 @@
             ],
             place=place,
             smem_out=1,
-        )(cond_own, blocks[0], *[move(block) for move, block in zip(z_moves, blocks[1:])])
+        )(cond_own, blocks[0], *[move(block) for move, block in reversed(list(zip(z_moves, blocks[1:])))])
     else:
         own_grad, rim_swap, rim_beside = normed_back(d_query, d_rest)
         grad_features = last_features(own_grad, core_move(rim_swap), beside_move(rim_beside))

time: 59.3 us -> 55.5 us (0.936)
  waiting for transfers between devices: 18.9 us -> 13.4 us
  starting transfers between devices: 22.6 us -> 25 us
  Pallas kernels: 14.6 us -> 13.8 us
    ppermute x17, waiting for transfers between devices: 12.7 us -> 9.97 us  [over(): lax.ppermute(value, axis, [(i, i ^ by) for i in range(size_of)])]
    ppermute x2 -> x3, waiting for transfers between devices: 3.91 us -> 2.43 us  [second_chip(): return lax.ppermute(value, 'rows', chip_pairs(1))]
    ppermute x2 -> x3, starting transfers between devices: 2.09 us -> 3.49 us  [second_chip(): return lax.ppermute(value, 'rows', chip_pairs(1))]
    ppermute x1 -> x2, waiting for transfers between devices: 2.29 us -> 1.04 us  [first_chip(): return lax.ppermute(value, 'rows', chip_pairs(0))]
    pallas_call x13 -> x15, Pallas kernels: 14.6 us -> 13.8 us  [run(): pl.pallas_call(kernel, out_shape=outs, in_specs=[pl.BlockSpec(memory_spac...]
    ppermute x1 -> x2, starting transfers between devices: 1.48 us -> 2.16 us  [first_chip(): return lax.ppermute(value, 'rows', chip_pairs(0))]
  transfers between devices with their start and end apart: 22 -> 24, of which waited for: 12 -> 8; matrix products, arithmetic and copies ran while one was open for 1% -> 1% of each run, Pallas kernels for 13% -> 13%
where the time goes in v2:
time: 55.5 us; the launch traced here: 55.2 us
  starting transfers between devices  25 us (45%)
  Pallas kernels  13.8 us (25%)
  waiting for transfers between devices  13.4 us (24%)
  local copies, waits for them, and re-layouts  1.76 us (3%)
  between operations  0.88 us (2%)
    ppermute x17, starting transfers between devices, over(): lax.ppermute(value, axis, [(i, i ^ by) for i in range(size_of)])  15.8 us
    pallas_call x15, Pallas kernels, run(): pl.pallas_call(kernel, out_shape=outs, in_specs=[pl.BlockSpec(memory_spac...  13.8 us
    ppermute x17, waiting for transfers between devices, over(): lax.ppermute(value, axis, [(i, i ^ by) for i in range(size_of)])  9.97 us
    ppermute x2, starting transfers between devices, beside_move(): return lax.ppermute(value, 'rows', beside_pairs)  3.55 us
    ppermute x3, starting transfers between devices, second_chip(): return lax.ppermute(value, 'rows', chip_pairs(1))  3.49 us
    ppermute x3, waiting for transfers between devices, second_chip(): return lax.ppermute(value, 'rows', chip_pairs(1))  2.43 us
    ppermute x2, starting transfers between devices, first_chip(): return lax.ppermute(value, 'rows', chip_pairs(0))  2.16 us
    unnamed x8, local copies, waits for them, and re-layouts  1.39 us
  transfers between devices with their start and end apart: 24, of which 8 were waited for; matrix products, arithmetic and copies ran while one was open for 1% of the time, Pallas kernels for 13%

profile of v2, /device:TPU:0, one launch (start us, length us, event | category | flops | bytes accessed | tf_op | source)
XLA Modules:
  0.0 55.2 jit_solution(9866689577002508752)
XLA Ops:
  0.7 1.1 %shard_map.179 = (bf16[8,3456]{1,0:T(8,128)(2,1)S(1)}, bf16[8,3456]{1,0:T(8,128)(2,1)S(1)}, f32[24,2]{1,0:T(8,128)S(1)}) custom-call(bf16[2,768]{1,0:T(2,128)(2,1)} %cond_ref.1, bf16[8,768]{1,0:T(8,128)(2,1)} %qkv_ref.1, bf16[8,1536]{1,0:T(8,128)(2,1)} %up_ref.1, bf16[8,256]{1,0:T(8,128)(2,1)} %out_ref.1, bf16[24,256]{1,0:T(8,128)(2,1)} %down_ref.1, ...), custom_call_target="tpu_custom_call" | custom-call | flops 1000000000 | bytes 4000000 | tf_op jit(solution)/shard_map/pallas_call | solution.py:597
  1.7 4.1 %collective-permute-start.4 = (bf16[8,3456]{1,0:T(8,128)(2,1)S(1)}, bf16[8,3456]{1,0:T(8,128)(2,1)S(1)}, u32[]{:S(2)}, u32[]{:S(2)}) collective-permute-start(bf16[8,3456]{1,0:T(8,128)(2,1)S(1)} %get-tuple-element.92), channel_id=1, source_target_pairs={{0,2},{1,3},{2,0},{3,1},{4,6},{5,7},{6,4},{7,5},{8,10},{9,11},{10,... | collective-permute-start | bytes 165896 | tf_op jit(solution)/shard_map/ppermute | solution.py:678
  5.8 1.3 %collective-permute-start.2 = (bf16[8,3456]{1,0:T(8,128)(2,1)S(1)}, bf16[8,3456]{1,0:T(8,128)(2,1)S(1)}, u32[]{:S(2)}, u32[]{:S(2)}) collective-permute-start(bf16[8,3456]{1,0:T(8,128)(2,1)S(1)} %get-tuple-element.92), channel_id=1, source_target_pairs={{0,3},{1,2},{2,1},{3,0},{4,7},{5,6},{6,5},{7,4},{8,11},{9,10},{10,... | collective-permute-start | bytes 165896 | tf_op jit(solution)/shard_map/ppermute | solution.py:678
  7.2 0.2 collective-permute-start.3
  7.4 1.4 %collective-permute-start.1 = (bf16[3,64,256]{2,1,0:T(8,128)(2,1)S(1)}, bf16[3,64,256]{2,1,0:T(8,128)(2,1)S(1)}, u32[]{:S(2)}, u32[]{:S(2)}) collective-permute-start(bf16[3,64,256]{2,1,0:T(8,128)(2,1)S(1)} %get-tuple-element.159), channel_id=1, source_target_pairs={{0,28},{4,8},{8,4},{12,16},{16,12},{20,24},{24,20},{28,0},{1,29},{... | collective-permute-start | bytes 294920 | tf_op jit(solution)/shard_map/ppermute | solution.py:740
  8.8 0.3 collective-permute-start
  9.2 0.1 fusion.3
  9.3 0.2 fusion.1
  9.6 0.7 %copy-done.3 = s32[64,64]{1,0:T(8,128)S(1)} copy-done((s32[64,64]{1,0:T(8,128)S(1)}, s32[64,64]{1,0:T(8,128)}, u32[]{:S(2)}) %copy-start.3) | copy-done | bytes 16408
  10.3 0.1 slice.11
  10.4 1.5 %collective-permute-done.3.p2 = bf16[8,3456]{1,0:T(8,128)(2,1)S(1)} collective-permute-done((bf16[8,3456]{1,0:T(8,128)(2,1)S(1)}, bf16[8,3456]{1,0:T(8,128)(2,1)S(1)}, u32[]{:S(2)}, u32[]{:S(2)}) %collective-permute-start.3) | collective-permute-done | bytes 55328 | tf_op jit(solution)/shard_map/ppermute | solution.py:678
  12.0 2.5 %collective-permute-start.6 = (bf16[4,8,3456]{2,1,0:T(8,128)(2,1)S(1)}, bf16[4,8,3456]{2,1,0:T(8,128)(2,1)S(1)}, u32[]{:S(2)}, u32[]{:S(2)}) collective-permute-start(bf16[4,8,3456]{2,1,0:T(8,128)(2,1)S(1)} %shard_map.180.p0), channel_id=1, source_target_pairs={{0,24},{4,28},{8,16},{12,20},{16,8},{20,12},{24,0},{28,4},{1,25},{... | collective-permute-start | bytes 663560 | tf_op jit(solution)/shard_map/ppermute | solution.py:678
  14.5 0.1 copy.20
  14.6 0.1 broadcast_in_dim.49
  14.7 0.1 reshape.363.id_key_ref
  14.8 0.6 %collective-permute-start.8 = (bf16[4,8,3456]{2,1,0:T(8,128)(2,1)S(1)}, bf16[4,8,3456]{2,1,0:T(8,128)(2,1)S(1)}, u32[]{:S(2)}, u32[]{:S(2)}) collective-permute-start(bf16[4,8,3456]{2,1,0:T(8,128)(2,1)S(1)} %shard_map.180.p0), channel_id=1, source_target_pairs={{0,16},{4,20},{8,24},{12,28},{16,0},{20,4},{24,8},{28,12},{1,17},{... | collective-permute-start | bytes 663560 | tf_op jit(solution)/shard_map/ppermute | solution.py:678
  15.3 0.5 collective-permute-start.5
  15.9 0.6 %copy-done.2 = f32[4]{0:T(128)S(1)} copy-done((f32[4]{0:T(128)S(1)}, f32[4]{0:T(128)}, u32[]{:S(2)}) %copy-start.2) | copy-done | bytes 40
  16.6 1.3 %shard_map.178 = (f32[1024,256]{1,0:T(8,128)S(1)}, bf16[256,1024]{1,0:T(8,128)(2,1)S(1)}, bf16[256,512]{1,0:T(8,128)(2,1)S(1)}, f32[1024,128]{1,0:T(8,128)S(1)},...) custom-call(f32[4]{0:T(128)S(1)} %copy-done.2, ...), custom_call_target="tpu_custom_call" | custom-call | flops 1000000000 | bytes 4000000 | tf_op jit(solution)/shard_map/pallas_call | solution.py:597
  17.9 3.5 %collective-permute-done.6.p3 = bf16[4,8,3456]{2,1,0:T(8,128)(2,1)S(1)} collective-permute-done((bf16[4,8,3456]{2,1,0:T(8,128)(2,1)S(1)}, bf16[4,8,3456]{2,1,0:T(8,128)(2,1)S(1)}, u32[]{:S(2)}, u32[]{:S(2)}) %collective-permute-start.6) | collective-permute-done | bytes 221216 | tf_op jit(solution)/shard_map/ppermute | solution.py:678
  21.3 0.5 collective-permute-start.9
  21.8 1.9 %collective-permute-done.8.p2 = bf16[4,8,3456]{2,1,0:T(8,128)(2,1)S(1)} collective-permute-done((bf16[4,8,3456]{2,1,0:T(8,128)(2,1)S(1)}, bf16[4,8,3456]{2,1,0:T(8,128)(2,1)S(1)}, u32[]{:S(2)}, u32[]{:S(2)}) %collective-permute-start.8) | collective-permute-done | bytes 221216 | tf_op jit(solution)/shard_map/ppermute | solution.py:678
  23.7 0.5 collective-permute-start.10
  24.3 1.0 %collective-permute-done.11.p6 = bf16[4,8,3456]{2,1,0:T(8,128)(2,1)S(1)} collective-permute-done((bf16[4,8,3456]{2,1,0:T(8,128)(2,1)S(1)}, bf16[4,8,3456]{2,1,0:T(8,128)(2,1)S(1)}, u32[]{:S(2)}, u32[]{:S(2)}) %collective-permute-start.11) | collective-permute-done | bytes 221216 | tf_op jit(solution)/shard_map/ppermute | solution.py:678
  25.2 0.3 collective-permute-done.10.p5
  25.5 4.7 %shard_map.181 = (bf16[1024,256]{1,0:T(8,128)(2,1)S(1)}, bf16[1024,256]{1,0:T(8,128)(2,1)S(1)}, bf16[1024,256]{1,0:T(8,128)(2,1)S(1)}, bf16[4,512,256]{2,1,0:T(8...) custom-call(f32[1,128]{1,0:T(1,128)S(1)} %get-tuple-element.84.root_, ...), custom_call_target="tpu_custom_call" | custom-call | flops 1000000000 | bytes 4000000 | tf_op jit(solution)/shard_map/pallas_call | solution.py:597
  30.2 0.3 collective-permute-start.12
  30.5 2.9 %shard_map.183 = (bf16[512,256]{1,0:T(8,128)(2,1)S(1)}, bf16[1024,512]{1,0:T(8,128)(2,1)S(1)}, bf16[4,4,8,896]{3,2,1,0:T(8,128)(2,1)S(1)}, bf16[4,4,8,896]{3,2,1,0:T(8,128)(2,1)S(1)}) custom-call(f32[1,128]{1,0:T(1,128)S(1)} %get-tuple-element.84.root_ref, bf16[512,256]{1,0:T(8,128)(2,1)S(1)} %get-tuple-element.106.shrunk_ref, ...), custom_call_target="tpu_custom_call" | custom-call | flops 1 | bytes 1 | tf_op jit(solution)/shard_map/pallas_call | solution.py:597
  33.4 0.4 collective-permute-start.14
  33.8 0.2 shard_map.182
  33.9 1.3 %collective-permute-start.13 = (bf16[4,8,2560]{2,1,0:T(8,128)(2,1)S(1)}, bf16[4,8,2560]{2,1,0:T(8,128)(2,1)S(1)}, u32[]{:S(2)}, u32[]{:S(2)}) collective-permute-start(bf16[4,8,2560]{2,1,0:T(8,128)(2,1)S(1)} %get-tuple-element.105), channel_id=1, source_target_pairs={{0,8},{4,20},{8,0},{12,28},{16,24},{20,4},{24,16},{28,12},{1,9},{5... | collective-permute-start | bytes 491528 | tf_op jit(solution)/shard_map/ppermute | solution.py:690
  35.3 1.0 %collective-permute-start.15 = (bf16[4,8,896]{2,1,0:T(8,128)(2,1)S(1)}, bf16[4,8,896]{2,1,0:T(8,128)(2,1)S(1)}, u32[]{:S(2)}, u32[]{:S(2)}) collective-permute-start(bf16[4,8,896]{2,1,0:T(8,128)(2,1)S(1)} %get-tuple-element.123), channel_id=1, source_target_pairs={{0,8},{4,20},{8,0},{12,28},{16,24},{20,4},{24,16},{28,12},{1,9},{5... | collective-permute-start | bytes 172040 | tf_op jit(solution)/shard_map/ppermute | solution.py:690
  36.3 1.2 %collective-permute-start.18 = (bf16[4,8,3456]{2,1,0:T(8,128)(2,1)S(1)}, bf16[4,8,3456]{2,1,0:T(8,128)(2,1)S(1)}, u32[]{:S(2)}, u32[]{:S(2)}) collective-permute-start(bf16[4,8,3456]{2,1,0:T(8,128)(2,1)S(1)} %shard_map.187), channel_id=1, source_target_pairs={{0,8},{4,20},{8,0},{12,28},{16,24},{20,4},{24,16},{28,12},{1,9},{5... | collective-permute-start | bytes 663560 | tf_op jit(solution)/shard_map/ppermute | solution.py:690
  37.5 2.4 %collective-permute-done.15.two_ref = bf16[4,8,896]{2,1,0:T(8,128)(2,1)S(1)} collective-permute-done((bf16[4,8,896]{2,1,0:T(8,128)(2,1)S(1)}, bf16[4,8,896]{2,1,0:T(8,128)(2,1)S(1)}, u32[]{:S(2)}, u32[]{:S(2)}) %collective-permute-start.15) | collective-permute-done | bytes 57376 | tf_op jit(solution)/shard_map/ppermute | solution.py:690
  40.0 1.4 %collective-permute-start.16 = (bf16[4,8,2560]{2,1,0:T(8,128)(2,1)S(1)}, bf16[4,8,2560]{2,1,0:T(8,128)(2,1)S(1)}, u32[]{:S(2)}, u32[]{:S(2)}) collective-permute-start(bf16[4,8,2560]{2,1,0:T(8,128)(2,1)S(1)} %shard_map.185), channel_id=1, source_target_pairs={{0,16},{4,12},{8,24},{12,4},{16,0},{20,28},{24,8},{28,20},{1,17},{... | collective-permute-start | bytes 491528 | tf_op jit(solution)/shard_map/ppermute | solution.py:687
  41.3 0.8 %collective-permute-start.17 = (bf16[4,8,896]{2,1,0:T(8,128)(2,1)S(1)}, bf16[4,8,896]{2,1,0:T(8,128)(2,1)S(1)}, u32[]{:S(2)}, u32[]{:S(2)}) collective-permute-start(bf16[4,8,896]{2,1,0:T(8,128)(2,1)S(1)} %shard_map.186), channel_id=1, source_target_pairs={{0,16},{4,12},{8,24},{12,4},{16,0},{20,28},{24,8},{28,20},{1,17},{... | collective-permute-start | bytes 172040 | tf_op jit(solution)/shard_map/ppermute | solution.py:687
  42.1 0.5 shard_map.189
  42.7 0.1 collective-permute-start.19
  42.8 2.2 %collective-permute-start.20 = (bf16[192,256]{1,0:T(8,128)(2,1)S(1)}, bf16[192,256]{1,0:T(8,128)(2,1)S(1)}, u32[]{:S(2)}, u32[]{:S(2)}) collective-permute-start(bf16[192,256]{1,0:T(8,128)(2,1)S(1)} %get-tuple-element.145), channel_id=1, source_target_pairs={{0,28},{4,8},{8,4},{12,16},{16,12},{20,24},{24,20},{28,0},{1,29},{... | collective-permute-start | bytes 294920 | tf_op jit(solution)/shard_map/ppermute | solution.py:740
  44.9 1.0 %collective-permute-done.17.q1 = bf16[4,8,896]{2,1,0:T(8,128)(2,1)S(1)} collective-permute-done((bf16[4,8,896]{2,1,0:T(8,128)(2,1)S(1)}, bf16[4,8,896]{2,1,0:T(8,128)(2,1)S(1)}, u32[]{:S(2)}, u32[]{:S(2)}) %collective-permute-start.17) | collective-permute-done | bytes 57376 | tf_op jit(solution)/shard_map/ppermute | solution.py:687
  46.0 0.1 shard_map.188
  46.1 2.9 %collective-permute-start.21 = (bf16[8,3456]{1,0:T(8,128)(2,1)S(1)}, bf16[8,3456]{1,0:T(8,128)(2,1)S(1)}, u32[]{:S(2)}, u32[]{:S(2)}) collective-permute-start(bf16[8,3456]{1,0:T(8,128)(2,1)S(1)} %get-tuple-element.149), channel_id=1, source_target_pairs={{0,3},{1,2},{2,1},{3,0},{4,7},{5,6},{6,5},{7,4},{8,11},{9,10},{10,... | collective-permute-start | bytes 165896 | tf_op jit(solution)/shard_map/ppermute | solution.py:678
  49.0 0.3 collective-permute-start.22
  49.3 1.3 %collective-permute-start.23 = (bf16[8,3456]{1,0:T(8,128)(2,1)S(1)}, bf16[8,3456]{1,0:T(8,128)(2,1)S(1)}, u32[]{:S(2)}, u32[]{:S(2)}) collective-permute-start(bf16[8,3456]{1,0:T(8,128)(2,1)S(1)} %get-tuple-element.151), channel_id=1, source_target_pairs={{0,1},{1,0},{2,3},{3,2},{4,5},{5,4},{6,7},{7,6},{8,9},{9,8},{10,11... | collective-permute-start | bytes 165896 | tf_op jit(solution)/shard_map/ppermute | solution.py:678
  50.6 1.1 %shard_map.190 = bf16[8,64,256]{2,1,0:T(8,128)(2,1)} custom-call(f32[512,256]{1,0:T(8,128)S(1)} %get-tuple-element.100.middle_ref, bf16[512,768]{1,0:T(8,128)(2,1)S(1)} %get-tuple-element.140.gated_ref, bf16[768,256]{1,0:T(8,128)(2,1)S(1)} %get-tuple-element.141.w_down_ref), custom_call_target="tpu_custom_call" | custom-call | flops 1000000000 | bytes 4000000 | tf_op jit(solution)/shard_map/pallas_call | solution.py:597
  51.6 1.1 %shard_map.191 = f32[8,64,256]{2,1,0:T(8,128)} custom-call(f32[512,256]{1,0:T(8,128)S(1)} %get-tuple-element.89.inputs_ref, f32[2,256]{1,0:T(2,128)S(1)} %get-tuple-element.142.gain_ref, f32[512,256]{1,0:T(8,128)S(1)} %get-tuple-element.143.own_ref, bf16[192,256]{1,0:T(8,128)(2,1)S(1)} %collective-permute-done.19.rim_swap_ref, ...), custom_call_target="tpu_custom_call" | custom-call | flops 1000000000 | bytes 4000000 | tf_op jit(solution)/shard_map/pallas_call | solution.py:597
  52.7 1.8 %collective-permute-done.22.two_ref = bf16[8,3456]{1,0:T(8,128)(2,1)S(1)} collective-permute-done((bf16[8,3456]{1,0:T(8,128)(2,1)S(1)}, bf16[8,3456]{1,0:T(8,128)(2,1)S(1)}, u32[]{:S(2)}, u32[]{:S(2)}) %collective-permute-start.22) | collective-permute-done | bytes 55328 | tf_op jit(solution)/shard_map/ppermute | solution.py:678
  54.5 0.7 %shard_map.192 = (f32[8,768]{1,0:T(8,128)}, f32[8,256]{1,0:T(8,128)}, f32[8,1536]{1,0:T(8,128)}, f32[24,256]{1,0:T(8,128)}, f32[24,256]{1,0:T(8,128)}, /*index=5*/f32[24,256]{1,0:T(8,128)}, f32[4]{0:T(128)}) custom-call(f32[24,2]{1,0:T(8,128)S(1)} %get-tuple-element.147.cond_ref, f32[8,3456]{1,0:T(8,128)S(1)} %get-tuple-element.148.own_ref, ...), custom_call_target="tpu_custom_call" | custom-call | flops 1000000000 | bytes 4000000 | tf_op jit(solution)/shard_map/pallas_call | solution.py:597
  (40 shorter events, 0.3 us)
Async XLA Ops:
  0.6 6.8 %copy-start = (bf16[8,64,256]{2,1,0:T(8,128)(2,1)S(1)}, bf16[8,64,256]{2,1,0:T(8,128)(2,1)}, u32[]{:S(2)}) copy-start(bf16[8,64,256]{2,1,0:T(8,128)(2,1)} %feat_ref.1) | copy-start | bytes 786436
  1.7 10.2 %collective-permute-start.4 = (bf16[8,3456]{1,0:T(8,128)(2,1)S(1)}, bf16[8,3456]{1,0:T(8,128)(2,1)S(1)}, u32[]{:S(2)}, u32[]{:S(2)}) collective-permute-start(bf16[8,3456]{1,0:T(8,128)(2,1)S(1)} %get-tuple-element.92), channel_id=1, source_target_pairs={{0,2},{1,3},{2,0},{3,1},{4,6},{5,7},{6,4},{7,5},{8,10},{9,11},{10,... | collective-permute-start | bytes 165896 | tf_op jit(solution)/shard_map/ppermute | solution.py:678
  5.8 6.1 %collective-permute-start.2 = (bf16[8,3456]{1,0:T(8,128)(2,1)S(1)}, bf16[8,3456]{1,0:T(8,128)(2,1)S(1)}, u32[]{:S(2)}, u32[]{:S(2)}) collective-permute-start(bf16[8,3456]{1,0:T(8,128)(2,1)S(1)} %get-tuple-element.92), channel_id=1, source_target_pairs={{0,3},{1,2},{2,1},{3,0},{4,7},{5,6},{6,5},{7,4},{8,11},{9,10},{10,... | collective-permute-start | bytes 165896 | tf_op jit(solution)/shard_map/ppermute | solution.py:678
  7.2 4.7 %collective-permute-start.3 = (bf16[8,3456]{1,0:T(8,128)(2,1)S(1)}, bf16[8,3456]{1,0:T(8,128)(2,1)S(1)}, u32[]{:S(2)}, u32[]{:S(2)}) collective-permute-start(bf16[8,3456]{1,0:T(8,128)(2,1)S(1)} %get-tuple-element.91.p0), channel_id=1, source_target_pairs={{0,1},{1,0},{2,3},{3,2},{4,5},{5,4},{6,7},{7,6},{8,9},{9,8},{10,11... | collective-permute-start | bytes 165896 | tf_op jit(solution)/shard_map/ppermute | solution.py:678
  7.4 8.4 %collective-permute-start.1 = (bf16[3,64,256]{2,1,0:T(8,128)(2,1)S(1)}, bf16[3,64,256]{2,1,0:T(8,128)(2,1)S(1)}, u32[]{:S(2)}, u32[]{:S(2)}) collective-permute-start(bf16[3,64,256]{2,1,0:T(8,128)(2,1)S(1)} %get-tuple-element.159), channel_id=1, source_target_pairs={{0,28},{4,8},{8,4},{12,16},{16,12},{20,24},{24,20},{28,0},{1,29},{... | collective-permute-start | bytes 294920 | tf_op jit(solution)/shard_map/ppermute | solution.py:740
  8.8 7.1 %collective-permute-start = (bf16[3,64,256]{2,1,0:T(8,128)(2,1)S(1)}, bf16[3,64,256]{2,1,0:T(8,128)(2,1)S(1)}, u32[]{:S(2)}, u32[]{:S(2)}) collective-permute-start(bf16[3,64,256]{2,1,0:T(8,128)(2,1)S(1)} %get-tuple-element.160), channel_id=1, source_target_pairs={{0,4},{4,0},{8,12},{12,8},{16,20},{20,16},{24,28},{28,24},{1,5},{5... | collective-permute-start | bytes 294920 | tf_op jit(solution)/shard_map/ppermute | solution.py:678
  9.5 0.8 %copy-start.3 = (s32[64,64]{1,0:T(8,128)S(1)}, s32[64,64]{1,0:T(8,128)}, u32[]{:S(2)}) copy-start(s32[64,64]{1,0:T(8,128)} %param.12) | copy-start | bytes 49156
  12.0 3.9 %copy-start.1 = (bf16[8,64,256]{2,1,0:T(8,128)(2,1)S(1)}, bf16[8,64,256]{2,1,0:T(8,128)(2,1)}, u32[]{:S(2)}) copy-start(bf16[8,64,256]{2,1,0:T(8,128)(2,1)} %cot_ref.1) | copy-start | bytes 786436
  12.0 9.3 %collective-permute-start.6 = (bf16[4,8,3456]{2,1,0:T(8,128)(2,1)S(1)}, bf16[4,8,3456]{2,1,0:T(8,128)(2,1)S(1)}, u32[]{:S(2)}, u32[]{:S(2)}) collective-permute-start(bf16[4,8,3456]{2,1,0:T(8,128)(2,1)S(1)} %shard_map.180.p0), channel_id=1, source_target_pairs={{0,24},{4,28},{8,16},{12,20},{16,8},{20,12},{24,0},{28,4},{1,25},{... | collective-permute-start | bytes 663560 | tf_op jit(solution)/shard_map/ppermute | solution.py:678
  14.8 9.0 %collective-permute-start.8 = (bf16[4,8,3456]{2,1,0:T(8,128)(2,1)S(1)}, bf16[4,8,3456]{2,1,0:T(8,128)(2,1)S(1)}, u32[]{:S(2)}, u32[]{:S(2)}) collective-permute-start(bf16[4,8,3456]{2,1,0:T(8,128)(2,1)S(1)} %shard_map.180.p0), channel_id=1, source_target_pairs={{0,16},{4,20},{8,24},{12,28},{16,0},{20,4},{24,8},{28,12},{1,17},{... | collective-permute-start | bytes 663560 | tf_op jit(solution)/shard_map/ppermute | solution.py:678
  15.3 8.4 %collective-permute-start.5 = (bf16[4,8,3456]{2,1,0:T(8,128)(2,1)S(1)}, bf16[4,8,3456]{2,1,0:T(8,128)(2,1)S(1)}, u32[]{:S(2)}, u32[]{:S(2)}) collective-permute-start(bf16[4,8,3456]{2,1,0:T(8,128)(2,1)S(1)} %shard_map.180.p0), channel_id=1, source_target_pairs={{0,8},{4,12},{8,0},{12,4},{16,24},{20,28},{24,16},{28,20},{1,9},{5... | collective-permute-start | bytes 663560 | tf_op jit(solution)/shard_map/ppermute | solution.py:678
  15.9 0.7 %copy-start.2 = (f32[4]{0:T(128)S(1)}, f32[4]{0:T(128)}, u32[]{:S(2)}) copy-start(f32[4]{0:T(128)} %scale_ref.1) | copy-start | bytes 52
  21.3 2.4 %collective-permute-start.7 = (bf16[4,8,3456]{2,1,0:T(8,128)(2,1)S(1)}, bf16[4,8,3456]{2,1,0:T(8,128)(2,1)S(1)}, u32[]{:S(2)}, u32[]{:S(2)}) collective-permute-start(bf16[4,8,3456]{2,1,0:T(8,128)(2,1)S(1)} %collective-permute-done.6.p3), channel_id=1, source_target_pairs={{0,4},{4,0},{8,12},{12,8},{16,20},{20,16},{24,28},{28,24},{1,5},{5... | collective-permute-start | bytes 663560 | tf_op jit(solution)/shard_map/ppermute | solution.py:678
  21.3 2.9 %collective-permute-start.9 = (bf16[4,8,3456]{2,1,0:T(8,128)(2,1)S(1)}, bf16[4,8,3456]{2,1,0:T(8,128)(2,1)S(1)}, u32[]{:S(2)}, u32[]{:S(2)}) collective-permute-start(bf16[4,8,3456]{2,1,0:T(8,128)(2,1)S(1)} %shard_map.180.p0), channel_id=1, source_target_pairs={{0,4},{4,0},{8,12},{12,8},{16,20},{20,16},{24,28},{28,24},{1,5},{5... | collective-permute-start | bytes 663560 | tf_op jit(solution)/shard_map/ppermute | solution.py:678
  23.7 1.5 %collective-permute-start.11 = (bf16[4,8,3456]{2,1,0:T(8,128)(2,1)S(1)}, bf16[4,8,3456]{2,1,0:T(8,128)(2,1)S(1)}, u32[]{:S(2)}, u32[]{:S(2)}) collective-permute-start(bf16[4,8,3456]{2,1,0:T(8,128)(2,1)S(1)} %collective-permute-done.8.p2), channel_id=1, source_target_pairs={{0,4},{4,0},{8,12},{12,8},{16,20},{20,16},{24,28},{28,24},{1,5},{5... | collective-permute-start | bytes 663560 | tf_op jit(solution)/shard_map/ppermute | solution.py:678
  23.7 1.8 %collective-permute-start.10 = (bf16[4,8,3456]{2,1,0:T(8,128)(2,1)S(1)}, bf16[4,8,3456]{2,1,0:T(8,128)(2,1)S(1)}, u32[]{:S(2)}, u32[]{:S(2)}) collective-permute-start(bf16[4,8,3456]{2,1,0:T(8,128)(2,1)S(1)} %collective-permute-done.5.p1), channel_id=1, source_target_pairs={{0,4},{4,0},{8,12},{12,8},{16,20},{20,16},{24,28},{28,24},{1,5},{5... | collective-permute-start | bytes 663560 | tf_op jit(solution)/shard_map/ppermute | solution.py:678
  30.2 3.5 %collective-permute-start.12 = (bf16[4,4,8,2560]{3,2,1,0:T(8,128)(2,1)S(1)}, bf16[4,4,8,2560]{3,2,1,0:T(8,128)(2,1)S(1)}, u32[]{:S(2)}, u32[]{:S(2)}) collective-permute-start(bf16[4,4,8,2560]{3,2,1,0:T(8,128)(2,1)S(1)} %get-tuple-element.102), channel_id=1, source_target_pairs={{0,4},{4,0},{8,12},{12,8},{16,20},{20,16},{24,28},{28,24},{1,5},{5... | collective-permute-start | bytes 1966088 | tf_op jit(solution)/shard_map/ppermute | solution.py:678
  33.4 1.9 %collective-permute-start.14 = (bf16[4,4,8,896]{3,2,1,0:T(8,128)(2,1)S(1)}, bf16[4,4,8,896]{3,2,1,0:T(8,128)(2,1)S(1)}, u32[]{:S(2)}, u32[]{:S(2)}) collective-permute-start(bf16[4,4,8,896]{3,2,1,0:T(8,128)(2,1)S(1)} %get-tuple-element.122), channel_id=1, source_target_pairs={{0,4},{4,0},{8,12},{12,8},{16,20},{20,16},{24,28},{28,24},{1,5},{5... | collective-permute-start | bytes 688136 | tf_op jit(solution)/shard_map/ppermute | solution.py:678
  33.9 6.0 %collective-permute-start.13 = (bf16[4,8,2560]{2,1,0:T(8,128)(2,1)S(1)}, bf16[4,8,2560]{2,1,0:T(8,128)(2,1)S(1)}, u32[]{:S(2)}, u32[]{:S(2)}) collective-permute-start(bf16[4,8,2560]{2,1,0:T(8,128)(2,1)S(1)} %get-tuple-element.105), channel_id=1, source_target_pairs={{0,8},{4,20},{8,0},{12,28},{16,24},{20,4},{24,16},{28,12},{1,9},{5... | collective-permute-start | bytes 491528 | tf_op jit(solution)/shard_map/ppermute | solution.py:690
  35.3 4.6 %collective-permute-start.15 = (bf16[4,8,896]{2,1,0:T(8,128)(2,1)S(1)}, bf16[4,8,896]{2,1,0:T(8,128)(2,1)S(1)}, u32[]{:S(2)}, u32[]{:S(2)}) collective-permute-start(bf16[4,8,896]{2,1,0:T(8,128)(2,1)S(1)} %get-tuple-element.123), channel_id=1, source_target_pairs={{0,8},{4,20},{8,0},{12,28},{16,24},{20,4},{24,16},{28,12},{1,9},{5... | collective-permute-start | bytes 172040 | tf_op jit(solution)/shard_map/ppermute | solution.py:690
  36.3 9.6 %collective-permute-start.18 = (bf16[4,8,3456]{2,1,0:T(8,128)(2,1)S(1)}, bf16[4,8,3456]{2,1,0:T(8,128)(2,1)S(1)}, u32[]{:S(2)}, u32[]{:S(2)}) collective-permute-start(bf16[4,8,3456]{2,1,0:T(8,128)(2,1)S(1)} %shard_map.187), channel_id=1, source_target_pairs={{0,8},{4,20},{8,0},{12,28},{16,24},{20,4},{24,16},{28,12},{1,9},{5... | collective-permute-start | bytes 663560 | tf_op jit(solution)/shard_map/ppermute | solution.py:690
  40.0 6.0 %collective-permute-start.16 = (bf16[4,8,2560]{2,1,0:T(8,128)(2,1)S(1)}, bf16[4,8,2560]{2,1,0:T(8,128)(2,1)S(1)}, u32[]{:S(2)}, u32[]{:S(2)}) collective-permute-start(bf16[4,8,2560]{2,1,0:T(8,128)(2,1)S(1)} %shard_map.185), channel_id=1, source_target_pairs={{0,16},{4,12},{8,24},{12,4},{16,0},{20,28},{24,8},{28,20},{1,17},{... | collective-permute-start | bytes 491528 | tf_op jit(solution)/shard_map/ppermute | solution.py:687
  41.3 4.6 %collective-permute-start.17 = (bf16[4,8,896]{2,1,0:T(8,128)(2,1)S(1)}, bf16[4,8,896]{2,1,0:T(8,128)(2,1)S(1)}, u32[]{:S(2)}, u32[]{:S(2)}) collective-permute-start(bf16[4,8,896]{2,1,0:T(8,128)(2,1)S(1)} %shard_map.186), channel_id=1, source_target_pairs={{0,16},{4,12},{8,24},{12,4},{16,0},{20,28},{24,8},{28,20},{1,17},{... | collective-permute-start | bytes 172040 | tf_op jit(solution)/shard_map/ppermute | solution.py:687
  42.7 9.0 %collective-permute-start.19 = (bf16[192,256]{1,0:T(8,128)(2,1)S(1)}, bf16[192,256]{1,0:T(8,128)(2,1)S(1)}, u32[]{:S(2)}, u32[]{:S(2)}) collective-permute-start(bf16[192,256]{1,0:T(8,128)(2,1)S(1)} %get-tuple-element.144), channel_id=1, source_target_pairs={{0,4},{4,0},{8,12},{12,8},{16,20},{20,16},{24,28},{28,24},{1,5},{5... | collective-permute-start | bytes 294920 | tf_op jit(solution)/shard_map/ppermute | solution.py:678
  42.8 8.9 %collective-permute-start.20 = (bf16[192,256]{1,0:T(8,128)(2,1)S(1)}, bf16[192,256]{1,0:T(8,128)(2,1)S(1)}, u32[]{:S(2)}, u32[]{:S(2)}) collective-permute-start(bf16[192,256]{1,0:T(8,128)(2,1)S(1)} %get-tuple-element.145), channel_id=1, source_target_pairs={{0,28},{4,8},{8,4},{12,16},{16,12},{20,24},{24,20},{28,0},{1,29},{... | collective-permute-start | bytes 294920 | tf_op jit(solution)/shard_map/ppermute | solution.py:740
  46.1 6.6 %collective-permute-start.21 = (bf16[8,3456]{1,0:T(8,128)(2,1)S(1)}, bf16[8,3456]{1,0:T(8,128)(2,1)S(1)}, u32[]{:S(2)}, u32[]{:S(2)}) collective-permute-start(bf16[8,3456]{1,0:T(8,128)(2,1)S(1)} %get-tuple-element.149), channel_id=1, source_target_pairs={{0,3},{1,2},{2,1},{3,0},{4,7},{5,6},{6,5},{7,4},{8,11},{9,10},{10,... | collective-permute-start | bytes 165896 | tf_op jit(solution)/shard_map/ppermute | solution.py:678
  49.0 5.5 %collective-permute-start.22 = (bf16[8,3456]{1,0:T(8,128)(2,1)S(1)}, bf16[8,3456]{1,0:T(8,128)(2,1)S(1)}, u32[]{:S(2)}, u32[]{:S(2)}) collective-permute-start(bf16[8,3456]{1,0:T(8,128)(2,1)S(1)} %get-tuple-element.150), channel_id=1, source_target_pairs={{0,2},{1,3},{2,0},{3,1},{4,6},{5,7},{6,4},{7,5},{8,10},{9,11},{10,... | collective-permute-start | bytes 165896 | tf_op jit(solution)/shard_map/ppermute | solution.py:678
  49.3 5.2 %collective-permute-start.23 = (bf16[8,3456]{1,0:T(8,128)(2,1)S(1)}, bf16[8,3456]{1,0:T(8,128)(2,1)S(1)}, u32[]{:S(2)}, u32[]{:S(2)}) collective-permute-start(bf16[8,3456]{1,0:T(8,128)(2,1)S(1)} %get-tuple-element.151), channel_id=1, source_target_pairs={{0,1},{1,0},{2,3},{3,2},{4,5},{5,4},{6,7},{7,6},{8,9},{9,8},{10,11... | collective-permute-start | bytes 165896 | tf_op jit(solution)/shard_map/ppermute | solution.py:678

commit v3 on v2

--- a/solution.py
+++ b/solution.py
@@ -162,7 +162,7 @@
 
 
 def pack_kernel(
-    per_canvas, place, cond_ref, qkv_ref, up_ref, out_ref, down_ref, attn_ref, feed_ref,
+    heads, per_canvas, place, cond_ref, qkv_ref, up_ref, out_ref, down_ref, attn_ref, feed_ref,
     near_ref, far_ref, cond_own_ref,
 ):
     own = attn_ref.shape[0]
@@ -186,12 +186,17 @@
     down = down_ref[...].astype(F32)
     parts = [up_ref[...], out_ref[...]] + [down[8 * i : 8 * i + 8].astype(BF16) for i in range(down.shape[0] // 8)]
     qkv = qkv_ref.shape[1]
+    turned = mm(
+        jnp.concatenate([qkv_ref[:, :width], qkv_ref[:, width : 2 * width]], axis=0).astype(F32).astype(BF16),
+        turned_order(width, heads),
+    ).astype(BF16)
     mine = place[0] == 0
     for ref, tail in (
         (near_ref, jnp.where(mine, tails[0], tails[1])),
         (far_ref, jnp.where(mine, tails[1], tails[0])),
     ):
-        ref[:, :qkv] = qkv_ref[...]
+        ref[:, :width], ref[:, width : 2 * width] = turned[:8], turned[8:]
+        ref[:, 2 * width : qkv] = qkv_ref[:, 2 * width :]
         ref[:, qkv : qkv + 128] = tail.astype(BF16)
         at = qkv + 128
         for part in parts:
@@ -307,21 +312,14 @@
 
 
 def attend_kernel(
-    heads, root_ref, unit_ref, cos_ref, sine_ref, mask_ref, sums, raw_ref,
+    heads, root_ref, unit_ref, cos_ref, sine_ref, mask_ref, sums, w_ref,
     query_ref, key_ref, value_ref, raised_ref, mixed_ref, inverse_ref, along_q_ref, length_q_ref, along_k_ref, length_k_ref,
-    gain_ref, gain_col_ref, w_ref,
+    gain_ref, gain_col_ref,
 ):
     bands, count = mask_ref.shape[:2]
     width = unit_ref.shape[1]
     size = width // heads
-    edge = REACH * BAND
-    weight = raw_ref[...]
-    order = turned_order(width, heads)
-    turned = mm(
-        jnp.concatenate([weight[:, :width], weight[:, width : 2 * width]], axis=0), order
-    ).astype(BF16)
-    w_ref[:, :width], w_ref[:, width : 2 * width] = turned[:width], turned[width:]
-    w_ref[:, 2 * width :] = weight[:, 2 * width :]
+    weight = w_ref[...]
     pairs = [sums[i : i + 2] + sums[i + 2 : i + 4] for i in (0, 4)]
     picked = 1.0 + jnp.concatenate(
         [jnp.concatenate([pair[0:1], pair[1:2]], axis=1) for pair in pairs], axis=0
@@ -334,27 +332,30 @@
     value_ref[...] = mm(normed, weight[:, 2 * width :]).astype(BF16)
     ones_head = same_head(width // 2, size // 2)
     cos, sine = cos_ref[...], sine_ref[...]
-    for i, ref in enumerate((query_ref, key_ref)):
-        first, second = halves(mm(normed, turned[i * width : (i + 1) * width]))
+    own = [own_rows(part, count) for part in (normed, cos, sine)]
+    for i, (ref, along_ref, length_ref, (rows, cos, sine)) in enumerate(
+        (
+            (query_ref, along_q_ref, length_q_ref, own),
+            (key_ref, along_k_ref, length_k_ref, (normed, cos, sine)),
+        )
+    ):
+        first, second = halves(mm(rows, weight[:, i * width : (i + 1) * width]))
         short = lax.rsqrt(mm((first * first + second * second).astype(BF16), ones_head) + EPS)
         length = short * root
         ref[...] = jnp.concatenate(
             [(first * cos - second * sine) * length, (second * cos + first * sine) * length], axis=1
         ).astype(BF16)
-        along = jnp.concatenate([first * short, second * short], axis=1)
-        if i == 0:
-            along_q_ref[...], length_q_ref[...] = own_rows(along, count), own_rows(length, count)
-        else:
-            along_k_ref[...], length_k_ref[...] = along, length
+        along_ref[...] = jnp.concatenate([first * short, second * short], axis=1)
+        length_ref[...] = length
     ones_half = jnp.ones((2 * count, 128), BF16)
     for band in range(bands):
         start = 2 * band * count
-        query = query_ref[start + edge : start + edge + count, :].astype(F32)
+        span = slice(band * count, (band + 1) * count)
+        query = query_ref[span, :].astype(F32)
         scores = mm_rt(stack_heads(query, heads), key_ref[start : start + 2 * count, :])
         raised = jnp.exp(scores).astype(BF16) * jnp.concatenate([mask_ref[band]] * heads, axis=0)
         raised_ref[band] = raised
         value = value_ref[start : start + 2 * count, :]
-        span = slice(band * count, (band + 1) * count)
         for pair in range(heads // 2):
             lanes = slice(128 * pair, 128 * pair + 128)
             both = mm(
@@ -493,22 +494,22 @@
     query_ref, key_ref, value_ref, raised_ref, mixed_ref, along_q_ref, length_q_ref, along_k_ref, length_k_ref,
     gain_ref, gain_col_ref, w_ref, middle_ref, middle_grad_ref, shrunk_ref, gain_grad_ref,
     w_down_ref, gated_ref, mine_ref, other_ref,
-    inverse_ref, raw_ref, w_up_ref, w_out_ref, mixed_low_ref, normed_ref, d_exp_ref, branch_ref,
+    inverse_ref, w_up_ref, w_out_ref, mixed_low_ref, normed_ref, d_exp_ref, branch_ref,
 ):
     width = inputs_ref.shape[1]
     first, ups = 3 * width + 128, w_up_ref.shape[1]
     sums = jnp.zeros((8, 128), F32)
     for start, rows in place_parts(place, (p0, p1, p2, p3, p4, p5, p6, p7)):
-        store_rows(raw_ref, start, rows[:, :, : 3 * width])
+        store_rows(w_ref, start, rows[:, :, : 3 * width])
         sums = sums + jnp.sum(rows[:, :, 3 * width : first], axis=0)
         store_rows(w_up_ref, start, rows[:, :, first : first + ups])
         store_rows(w_out_ref, start, rows[:, :, first + ups : first + ups + width])
         down = [rows[:, :, at : at + width] for at in range(first + ups + width, rows.shape[2], width)]
         store_rows(w_down_ref, start, jnp.concatenate(down, axis=1))
     attend_kernel(
-        heads, root_ref, unit_ref, cos_ref, sine_ref, mask_ref, sums, raw_ref,
+        heads, root_ref, unit_ref, cos_ref, sine_ref, mask_ref, sums, w_ref,
         query_ref, key_ref, value_ref, raised_ref, mixed_ref, inverse_ref,
-        along_q_ref, length_q_ref, along_k_ref, length_k_ref, gain_ref, gain_col_ref, w_ref,
+        along_q_ref, length_q_ref, along_k_ref, length_k_ref, gain_ref, gain_col_ref,
     )
     feed_kernel(
         heads, inputs_ref, cot_ref, w_up_ref, w_out_ref, gain_ref, mixed_ref, inverse_ref,
@@ -551,7 +552,7 @@
                 )
             )
         d_scores = (raised.astype(F32) * jnp.concatenate(parts, axis=0)).astype(BF16)
-        query = query_ref[own, :].astype(F32)
+        query = query_ref[span, :].astype(F32)
         d_key = mm_lt(d_scores, stack_heads(query, heads))
         d_query = fold_heads(mm(d_scores, key_ref[whole, :]), heads)
         for pair in range(heads // 2):
@@ -693,7 +694,7 @@
 
     if direct:
         near, far, cond_own = call(
-            functools.partial(pack_kernel, per_canvas),
+            functools.partial(pack_kernel, heads, per_canvas),
             [
                 low(8, first_lanes + second_lanes),
                 low(8, first_lanes + second_lanes),
@@ -728,9 +729,12 @@
             high = lax.reduce_precision(part, 8, 7)
             lines += [high, part - high]
         lines = jnp.pad(jnp.concatenate(lines).astype(BF16), ((0, width - 8), (0, 0)))
+        qkv = whole(qkv_weight)
+        turned = jnp.argmax(turned_order(width, heads), axis=0)
+        qkv = jnp.concatenate([qkv[:, :width][:, turned], qkv[:, width : 2 * width][:, turned], qkv[:, 2 * width :]], axis=1)
         down = whole(down_weight).reshape(chunks, -1, 8, width).transpose(0, 2, 1, 3).reshape(width, -1)
         parts = parts_of(
-            jnp.concatenate([whole(qkv_weight), lines, whole(up_weight), whole(out_weight), down], axis=1)
+            jnp.concatenate([qkv, lines, whole(up_weight), whole(out_weight), down], axis=1)
         )
 
     odd = row % 2 == 1
@@ -777,7 +781,7 @@
     ) = call(
         functools.partial(forward_kernel, heads),
         [
-            low(2 * tokens, width),
+            low(tokens, width),
             low(2 * tokens, width),
             low(2 * tokens, width),
             low(bands, heads * count, 2 * count),
@@ -800,7 +804,6 @@
         ],
         scratch=[
             pltpu.VMEM((tokens, width), F32),
-            pltpu.VMEM((width, 3 * width), BF16),
             pltpu.VMEM((width, 2 * hidden), BF16),
             pltpu.VMEM((width, width), BF16),
             pltpu.VMEM((tokens, width), BF16),

time: 55.5 us -> 55.1 us (level)
  no operation moved by 1% of the time
where the time goes in v3:
time: 55.1 us; the launch traced here: 54.9 us
  starting transfers between devices  24.9 us (45%)
  Pallas kernels  13.5 us (25%)
  waiting for transfers between devices  13.5 us (25%)
  local copies, waits for them, and re-layouts  1.76 us (3%)
  between operations  0.88 us (2%)
    ppermute x17, starting transfers between devices, over(): lax.ppermute(value, axis, [(i, i ^ by) for i in range(size_of)])  15.8 us
    pallas_call x15, Pallas kernels, run(): pl.pallas_call(kernel, out_shape=outs, in_specs=[pl.BlockSpec(memory_spac...  13.5 us
    ppermute x17, waiting for transfers between devices, over(): lax.ppermute(value, axis, [(i, i ^ by) for i in range(size_of)])  9.96 us
    ppermute x2, starting transfers between devices, beside_move(): return lax.ppermute(value, 'rows', beside_pairs)  3.54 us
    ppermute x3, starting transfers between devices, second_chip(): return lax.ppermute(value, 'rows', chip_pairs(1))  3.47 us
    ppermute x3, waiting for transfers between devices, second_chip(): return lax.ppermute(value, 'rows', chip_pairs(1))  2.44 us
    ppermute x2, starting transfers between devices, first_chip(): return lax.ppermute(value, 'rows', chip_pairs(0))  2.16 us
    unnamed x8, local copies, waits for them, and re-layouts  1.39 us
  transfers between devices with their start and end apart: 24, of which 8 were waited for; matrix products, arithmetic and copies ran while one was open for 1% of the time, Pallas kernels for 13%

profile of v3, /device:TPU:0, one launch (start us, length us, event | category | flops | bytes accessed | tf_op | source)
XLA Modules:
  0.0 54.9 jit_solution(6621778789567593571)
XLA Ops:
  0.7 1.1 %shard_map.179 = (bf16[8,3456]{1,0:T(8,128)(2,1)S(1)}, bf16[8,3456]{1,0:T(8,128)(2,1)S(1)}, f32[24,2]{1,0:T(8,128)S(1)}) custom-call(bf16[2,768]{1,0:T(2,128)(2,1)} %cond_ref.1, bf16[8,768]{1,0:T(8,128)(2,1)} %qkv_ref.1, bf16[8,1536]{1,0:T(8,128)(2,1)} %up_ref.1, bf16[8,256]{1,0:T(8,128)(2,1)} %out_ref.1, bf16[24,256]{1,0:T(8,128)(2,1)} %down_ref.1, ...), custom_call_target="tpu_custom_call" | custom-call | flops 1000000000 | bytes 4000000 | tf_op jit(solution)/shard_map/pallas_call | solution.py:598
  1.7 4.1 %collective-permute-start.4 = (bf16[8,3456]{1,0:T(8,128)(2,1)S(1)}, bf16[8,3456]{1,0:T(8,128)(2,1)S(1)}, u32[]{:S(2)}, u32[]{:S(2)}) collective-permute-start(bf16[8,3456]{1,0:T(8,128)(2,1)S(1)} %get-tuple-element.92), channel_id=1, source_target_pairs={{0,2},{1,3},{2,0},{3,1},{4,6},{5,7},{6,4},{7,5},{8,10},{9,11},{10,... | collective-permute-start | bytes 165896 | tf_op jit(solution)/shard_map/ppermute | solution.py:679
  5.8 1.3 %collective-permute-start.2 = (bf16[8,3456]{1,0:T(8,128)(2,1)S(1)}, bf16[8,3456]{1,0:T(8,128)(2,1)S(1)}, u32[]{:S(2)}, u32[]{:S(2)}) collective-permute-start(bf16[8,3456]{1,0:T(8,128)(2,1)S(1)} %get-tuple-element.92), channel_id=1, source_target_pairs={{0,3},{1,2},{2,1},{3,0},{4,7},{5,6},{6,5},{7,4},{8,11},{9,10},{10,... | collective-permute-start | bytes 165896 | tf_op jit(solution)/shard_map/ppermute | solution.py:679
  7.2 0.2 collective-permute-start.3
  7.5 1.4 %collective-permute-start.1 = (bf16[3,64,256]{2,1,0:T(8,128)(2,1)S(1)}, bf16[3,64,256]{2,1,0:T(8,128)(2,1)S(1)}, u32[]{:S(2)}, u32[]{:S(2)}) collective-permute-start(bf16[3,64,256]{2,1,0:T(8,128)(2,1)S(1)} %get-tuple-element.159), channel_id=1, source_target_pairs={{0,28},{4,8},{8,4},{12,16},{16,12},{20,24},{24,20},{28,0},{1,29},{... | collective-permute-start | bytes 294920 | tf_op jit(solution)/shard_map/ppermute | solution.py:744
  8.8 0.3 collective-permute-start
  9.2 0.1 fusion.3
  9.3 0.2 fusion.1
  9.6 0.7 %copy-done.3 = s32[64,64]{1,0:T(8,128)S(1)} copy-done((s32[64,64]{1,0:T(8,128)S(1)}, s32[64,64]{1,0:T(8,128)}, u32[]{:S(2)}) %copy-start.3) | copy-done | bytes 16408
  10.3 0.1 slice.11
  10.4 1.5 %collective-permute-done.3.p2 = bf16[8,3456]{1,0:T(8,128)(2,1)S(1)} collective-permute-done((bf16[8,3456]{1,0:T(8,128)(2,1)S(1)}, bf16[8,3456]{1,0:T(8,128)(2,1)S(1)}, u32[]{:S(2)}, u32[]{:S(2)}) %collective-permute-start.3) | collective-permute-done | bytes 55328 | tf_op jit(solution)/shard_map/ppermute | solution.py:679
  12.0 2.5 %collective-permute-start.6 = (bf16[4,8,3456]{2,1,0:T(8,128)(2,1)S(1)}, bf16[4,8,3456]{2,1,0:T(8,128)(2,1)S(1)}, u32[]{:S(2)}, u32[]{:S(2)}) collective-permute-start(bf16[4,8,3456]{2,1,0:T(8,128)(2,1)S(1)} %shard_map.180.p0), channel_id=1, source_target_pairs={{0,24},{4,28},{8,16},{12,20},{16,8},{20,12},{24,0},{28,4},{1,25},{... | collective-permute-start | bytes 663560 | tf_op jit(solution)/shard_map/ppermute | solution.py:679
  14.5 0.1 copy.20
  14.6 0.1 broadcast_in_dim.49
  14.7 0.1 reshape.363.id_key_ref
  14.8 0.6 %collective-permute-start.8 = (bf16[4,8,3456]{2,1,0:T(8,128)(2,1)S(1)}, bf16[4,8,3456]{2,1,0:T(8,128)(2,1)S(1)}, u32[]{:S(2)}, u32[]{:S(2)}) collective-permute-start(bf16[4,8,3456]{2,1,0:T(8,128)(2,1)S(1)} %shard_map.180.p0), channel_id=1, source_target_pairs={{0,16},{4,20},{8,24},{12,28},{16,0},{20,4},{24,8},{28,12},{1,17},{... | collective-permute-start | bytes 663560 | tf_op jit(solution)/shard_map/ppermute | solution.py:679
  15.4 0.5 collective-permute-start.5
  15.9 0.6 %copy-done.2 = f32[4]{0:T(128)S(1)} copy-done((f32[4]{0:T(128)S(1)}, f32[4]{0:T(128)}, u32[]{:S(2)}) %copy-start.2) | copy-done | bytes 40
  16.6 1.3 %shard_map.178 = (f32[1024,256]{1,0:T(8,128)S(1)}, bf16[256,1024]{1,0:T(8,128)(2,1)S(1)}, bf16[256,512]{1,0:T(8,128)(2,1)S(1)}, f32[1024,128]{1,0:T(8,128)S(1)},...) custom-call(f32[4]{0:T(128)S(1)} %copy-done.2, ...), custom_call_target="tpu_custom_call" | custom-call | flops 1000000000 | bytes 4000000 | tf_op jit(solution)/shard_map/pallas_call | solution.py:598
  17.9 3.5 %collective-permute-done.6.p3 = bf16[4,8,3456]{2,1,0:T(8,128)(2,1)S(1)} collective-permute-done((bf16[4,8,3456]{2,1,0:T(8,128)(2,1)S(1)}, bf16[4,8,3456]{2,1,0:T(8,128)(2,1)S(1)}, u32[]{:S(2)}, u32[]{:S(2)}) %collective-permute-start.6) | collective-permute-done | bytes 221216 | tf_op jit(solution)/shard_map/ppermute | solution.py:679
  21.3 0.5 collective-permute-start.9
  21.8 1.9 %collective-permute-done.8.p2 = bf16[4,8,3456]{2,1,0:T(8,128)(2,1)S(1)} collective-permute-done((bf16[4,8,3456]{2,1,0:T(8,128)(2,1)S(1)}, bf16[4,8,3456]{2,1,0:T(8,128)(2,1)S(1)}, u32[]{:S(2)}, u32[]{:S(2)}) %collective-permute-start.8) | collective-permute-done | bytes 221216 | tf_op jit(solution)/shard_map/ppermute | solution.py:679
  23.8 0.5 collective-permute-start.10
  24.3 1.0 %collective-permute-done.11.p6 = bf16[4,8,3456]{2,1,0:T(8,128)(2,1)S(1)} collective-permute-done((bf16[4,8,3456]{2,1,0:T(8,128)(2,1)S(1)}, bf16[4,8,3456]{2,1,0:T(8,128)(2,1)S(1)}, u32[]{:S(2)}, u32[]{:S(2)}) %collective-permute-start.11) | collective-permute-done | bytes 221216 | tf_op jit(solution)/shard_map/ppermute | solution.py:679
  25.2 0.3 collective-permute-done.10.p5
  25.5 4.3 %shard_map.181 = (bf16[512,256]{1,0:T(8,128)(2,1)S(1)}, bf16[1024,256]{1,0:T(8,128)(2,1)S(1)}, bf16[1024,256]{1,0:T(8,128)(2,1)S(1)}, bf16[4,512,256]{2,1,0:T(8,...) custom-call(f32[1,128]{1,0:T(1,128)S(1)} %get-tuple-element.84.root_, ...), custom_call_target="tpu_custom_call" | custom-call | flops 1000000000 | bytes 4000000 | tf_op jit(solution)/shard_map/pallas_call | solution.py:598
  29.9 0.2 collective-permute-start.12
  30.1 2.9 %shard_map.183 = (bf16[512,256]{1,0:T(8,128)(2,1)S(1)}, bf16[1024,512]{1,0:T(8,128)(2,1)S(1)}, bf16[4,4,8,896]{3,2,1,0:T(8,128)(2,1)S(1)}, bf16[4,4,8,896]{3,2,1,0:T(8,128)(2,1)S(1)}) custom-call(f32[1,128]{1,0:T(1,128)S(1)} %get-tuple-element.84.root_ref, bf16[512,256]{1,0:T(8,128)(2,1)S(1)} %get-tuple-element.106.shrunk_ref, ...), custom_call_target="tpu_custom_call" | custom-call | flops 1 | bytes 1 | tf_op jit(solution)/shard_map/pallas_call | solution.py:598
  33.0 0.4 collective-permute-start.14
  33.4 0.2 shard_map.182
  33.6 1.3 %collective-permute-start.13 = (bf16[4,8,2560]{2,1,0:T(8,128)(2,1)S(1)}, bf16[4,8,2560]{2,1,0:T(8,128)(2,1)S(1)}, u32[]{:S(2)}, u32[]{:S(2)}) collective-permute-start(bf16[4,8,2560]{2,1,0:T(8,128)(2,1)S(1)} %get-tuple-element.105), channel_id=1, source_target_pairs={{0,8},{4,20},{8,0},{12,28},{16,24},{20,4},{24,16},{28,12},{1,9},{5... | collective-permute-start | bytes 491528 | tf_op jit(solution)/shard_map/ppermute | solution.py:691
  35.0 1.0 %collective-permute-start.15 = (bf16[4,8,896]{2,1,0:T(8,128)(2,1)S(1)}, bf16[4,8,896]{2,1,0:T(8,128)(2,1)S(1)}, u32[]{:S(2)}, u32[]{:S(2)}) collective-permute-start(bf16[4,8,896]{2,1,0:T(8,128)(2,1)S(1)} %get-tuple-element.123), channel_id=1, source_target_pairs={{0,8},{4,20},{8,0},{12,28},{16,24},{20,4},{24,16},{28,12},{1,9},{5... | collective-permute-start | bytes 172040 | tf_op jit(solution)/shard_map/ppermute | solution.py:691
  36.0 1.1 %collective-permute-start.18 = (bf16[4,8,3456]{2,1,0:T(8,128)(2,1)S(1)}, bf16[4,8,3456]{2,1,0:T(8,128)(2,1)S(1)}, u32[]{:S(2)}, u32[]{:S(2)}) collective-permute-start(bf16[4,8,3456]{2,1,0:T(8,128)(2,1)S(1)} %shard_map.187), channel_id=1, source_target_pairs={{0,8},{4,20},{8,0},{12,28},{16,24},{20,4},{24,16},{28,12},{1,9},{5... | collective-permute-start | bytes 663560 | tf_op jit(solution)/shard_map/ppermute | solution.py:691
  37.1 2.4 %collective-permute-done.15.two_ref = bf16[4,8,896]{2,1,0:T(8,128)(2,1)S(1)} collective-permute-done((bf16[4,8,896]{2,1,0:T(8,128)(2,1)S(1)}, bf16[4,8,896]{2,1,0:T(8,128)(2,1)S(1)}, u32[]{:S(2)}, u32[]{:S(2)}) %collective-permute-start.15) | collective-permute-done | bytes 57376 | tf_op jit(solution)/shard_map/ppermute | solution.py:691
  39.6 1.3 %collective-permute-start.16 = (bf16[4,8,2560]{2,1,0:T(8,128)(2,1)S(1)}, bf16[4,8,2560]{2,1,0:T(8,128)(2,1)S(1)}, u32[]{:S(2)}, u32[]{:S(2)}) collective-permute-start(bf16[4,8,2560]{2,1,0:T(8,128)(2,1)S(1)} %shard_map.185), channel_id=1, source_target_pairs={{0,16},{4,12},{8,24},{12,4},{16,0},{20,28},{24,8},{28,20},{1,17},{... | collective-permute-start | bytes 491528 | tf_op jit(solution)/shard_map/ppermute | solution.py:688
  41.0 0.8 %collective-permute-start.17 = (bf16[4,8,896]{2,1,0:T(8,128)(2,1)S(1)}, bf16[4,8,896]{2,1,0:T(8,128)(2,1)S(1)}, u32[]{:S(2)}, u32[]{:S(2)}) collective-permute-start(bf16[4,8,896]{2,1,0:T(8,128)(2,1)S(1)} %shard_map.186), channel_id=1, source_target_pairs={{0,16},{4,12},{8,24},{12,4},{16,0},{20,28},{24,8},{28,20},{1,17},{... | collective-permute-start | bytes 172040 | tf_op jit(solution)/shard_map/ppermute | solution.py:688
  41.8 0.5 shard_map.189
  42.3 0.1 collective-permute-start.19
  42.4 2.1 %collective-permute-start.20 = (bf16[192,256]{1,0:T(8,128)(2,1)S(1)}, bf16[192,256]{1,0:T(8,128)(2,1)S(1)}, u32[]{:S(2)}, u32[]{:S(2)}) collective-permute-start(bf16[192,256]{1,0:T(8,128)(2,1)S(1)} %get-tuple-element.145), channel_id=1, source_target_pairs={{0,28},{4,8},{8,4},{12,16},{16,12},{20,24},{24,20},{28,0},{1,29},{... | collective-permute-start | bytes 294920 | tf_op jit(solution)/shard_map/ppermute | solution.py:744
  44.6 1.0 %collective-permute-done.17.q1 = bf16[4,8,896]{2,1,0:T(8,128)(2,1)S(1)} collective-permute-done((bf16[4,8,896]{2,1,0:T(8,128)(2,1)S(1)}, bf16[4,8,896]{2,1,0:T(8,128)(2,1)S(1)}, u32[]{:S(2)}, u32[]{:S(2)}) %collective-permute-start.17) | collective-permute-done | bytes 57376 | tf_op jit(solution)/shard_map/ppermute | solution.py:688
  45.6 0.1 shard_map.188
  45.8 2.8 %collective-permute-start.21 = (bf16[8,3456]{1,0:T(8,128)(2,1)S(1)}, bf16[8,3456]{1,0:T(8,128)(2,1)S(1)}, u32[]{:S(2)}, u32[]{:S(2)}) collective-permute-start(bf16[8,3456]{1,0:T(8,128)(2,1)S(1)} %get-tuple-element.149), channel_id=1, source_target_pairs={{0,3},{1,2},{2,1},{3,0},{4,7},{5,6},{6,5},{7,4},{8,11},{9,10},{10,... | collective-permute-start | bytes 165896 | tf_op jit(solution)/shard_map/ppermute | solution.py:679
  48.6 0.3 collective-permute-start.22
  48.9 1.3 %collective-permute-start.23 = (bf16[8,3456]{1,0:T(8,128)(2,1)S(1)}, bf16[8,3456]{1,0:T(8,128)(2,1)S(1)}, u32[]{:S(2)}, u32[]{:S(2)}) collective-permute-start(bf16[8,3456]{1,0:T(8,128)(2,1)S(1)} %get-tuple-element.151), channel_id=1, source_target_pairs={{0,1},{1,0},{2,3},{3,2},{4,5},{5,4},{6,7},{7,6},{8,9},{9,8},{10,11... | collective-permute-start | bytes 165896 | tf_op jit(solution)/shard_map/ppermute | solution.py:679
  50.2 1.1 %shard_map.190 = bf16[8,64,256]{2,1,0:T(8,128)(2,1)} custom-call(f32[512,256]{1,0:T(8,128)S(1)} %get-tuple-element.100.middle_ref, bf16[512,768]{1,0:T(8,128)(2,1)S(1)} %get-tuple-element.140.gated_ref, bf16[768,256]{1,0:T(8,128)(2,1)S(1)} %get-tuple-element.141.w_down_ref), custom_call_target="tpu_custom_call" | custom-call | flops 1000000000 | bytes 4000000 | tf_op jit(solution)/shard_map/pallas_call | solution.py:598
  51.3 1.1 %shard_map.191 = f32[8,64,256]{2,1,0:T(8,128)} custom-call(f32[512,256]{1,0:T(8,128)S(1)} %get-tuple-element.89.inputs_ref, f32[2,256]{1,0:T(2,128)S(1)} %get-tuple-element.142.gain_ref, f32[512,256]{1,0:T(8,128)S(1)} %get-tuple-element.143.own_ref, bf16[192,256]{1,0:T(8,128)(2,1)S(1)} %collective-permute-done.19.rim_swap_ref, ...), custom_call_target="tpu_custom_call" | custom-call | flops 1000000000 | bytes 4000000 | tf_op jit(solution)/shard_map/pallas_call | solution.py:598
  52.4 1.7 %collective-permute-done.22.two_ref = bf16[8,3456]{1,0:T(8,128)(2,1)S(1)} collective-permute-done((bf16[8,3456]{1,0:T(8,128)(2,1)S(1)}, bf16[8,3456]{1,0:T(8,128)(2,1)S(1)}, u32[]{:S(2)}, u32[]{:S(2)}) %collective-permute-start.22) | collective-permute-done | bytes 55328 | tf_op jit(solution)/shard_map/ppermute | solution.py:679
  54.1 0.7 %shard_map.192 = (f32[8,768]{1,0:T(8,128)}, f32[8,256]{1,0:T(8,128)}, f32[8,1536]{1,0:T(8,128)}, f32[24,256]{1,0:T(8,128)}, f32[24,256]{1,0:T(8,128)}, /*index=5*/f32[24,256]{1,0:T(8,128)}, f32[4]{0:T(128)}) custom-call(f32[24,2]{1,0:T(8,128)S(1)} %get-tuple-element.147.cond_ref, f32[8,3456]{1,0:T(8,128)S(1)} %get-tuple-element.148.own_ref, ...), custom_call_target="tpu_custom_call" | custom-call | flops 1000000000 | bytes 4000000 | tf_op jit(solution)/shard_map/pallas_call | solution.py:598
  (40 shorter events, 0.3 us)
Async XLA Ops:
  0.6 6.8 %copy-start = (bf16[8,64,256]{2,1,0:T(8,128)(2,1)S(1)}, bf16[8,64,256]{2,1,0:T(8,128)(2,1)}, u32[]{:S(2)}) copy-start(bf16[8,64,256]{2,1,0:T(8,128)(2,1)} %feat_ref.1) | copy-start | bytes 786436
  1.7 10.2 %collective-permute-start.4 = (bf16[8,3456]{1,0:T(8,128)(2,1)S(1)}, bf16[8,3456]{1,0:T(8,128)(2,1)S(1)}, u32[]{:S(2)}, u32[]{:S(2)}) collective-permute-start(bf16[8,3456]{1,0:T(8,128)(2,1)S(1)} %get-tuple-element.92), channel_id=1, source_target_pairs={{0,2},{1,3},{2,0},{3,1},{4,6},{5,7},{6,4},{7,5},{8,10},{9,11},{10,... | collective-permute-start | bytes 165896 | tf_op jit(solution)/shard_map/ppermute | solution.py:679
  5.8 6.1 %collective-permute-start.2 = (bf16[8,3456]{1,0:T(8,128)(2,1)S(1)}, bf16[8,3456]{1,0:T(8,128)(2,1)S(1)}, u32[]{:S(2)}, u32[]{:S(2)}) collective-permute-start(bf16[8,3456]{1,0:T(8,128)(2,1)S(1)} %get-tuple-element.92), channel_id=1, source_target_pairs={{0,3},{1,2},{2,1},{3,0},{4,7},{5,6},{6,5},{7,4},{8,11},{9,10},{10,... | collective-permute-start | bytes 165896 | tf_op jit(solution)/shard_map/ppermute | solution.py:679
  7.2 4.7 %collective-permute-start.3 = (bf16[8,3456]{1,0:T(8,128)(2,1)S(1)}, bf16[8,3456]{1,0:T(8,128)(2,1)S(1)}, u32[]{:S(2)}, u32[]{:S(2)}) collective-permute-start(bf16[8,3456]{1,0:T(8,128)(2,1)S(1)} %get-tuple-element.91.p0), channel_id=1, source_target_pairs={{0,1},{1,0},{2,3},{3,2},{4,5},{5,4},{6,7},{7,6},{8,9},{9,8},{10,11... | collective-permute-start | bytes 165896 | tf_op jit(solution)/shard_map/ppermute | solution.py:679
  7.5 8.4 %collective-permute-start.1 = (bf16[3,64,256]{2,1,0:T(8,128)(2,1)S(1)}, bf16[3,64,256]{2,1,0:T(8,128)(2,1)S(1)}, u32[]{:S(2)}, u32[]{:S(2)}) collective-permute-start(bf16[3,64,256]{2,1,0:T(8,128)(2,1)S(1)} %get-tuple-element.159), channel_id=1, source_target_pairs={{0,28},{4,8},{8,4},{12,16},{16,12},{20,24},{24,20},{28,0},{1,29},{... | collective-permute-start | bytes 294920 | tf_op jit(solution)/shard_map/ppermute | solution.py:744
  8.8 7.1 %collective-permute-start = (bf16[3,64,256]{2,1,0:T(8,128)(2,1)S(1)}, bf16[3,64,256]{2,1,0:T(8,128)(2,1)S(1)}, u32[]{:S(2)}, u32[]{:S(2)}) collective-permute-start(bf16[3,64,256]{2,1,0:T(8,128)(2,1)S(1)} %get-tuple-element.160), channel_id=1, source_target_pairs={{0,4},{4,0},{8,12},{12,8},{16,20},{20,16},{24,28},{28,24},{1,5},{5... | collective-permute-start | bytes 294920 | tf_op jit(solution)/shard_map/ppermute | solution.py:679
  9.5 0.8 %copy-start.3 = (s32[64,64]{1,0:T(8,128)S(1)}, s32[64,64]{1,0:T(8,128)}, u32[]{:S(2)}) copy-start(s32[64,64]{1,0:T(8,128)} %param.12) | copy-start | bytes 49156
  12.0 3.9 %copy-start.1 = (bf16[8,64,256]{2,1,0:T(8,128)(2,1)S(1)}, bf16[8,64,256]{2,1,0:T(8,128)(2,1)}, u32[]{:S(2)}) copy-start(bf16[8,64,256]{2,1,0:T(8,128)(2,1)} %cot_ref.1) | copy-start | bytes 786436
  12.0 9.3 %collective-permute-start.6 = (bf16[4,8,3456]{2,1,0:T(8,128)(2,1)S(1)}, bf16[4,8,3456]{2,1,0:T(8,128)(2,1)S(1)}, u32[]{:S(2)}, u32[]{:S(2)}) collective-permute-start(bf16[4,8,3456]{2,1,0:T(8,128)(2,1)S(1)} %shard_map.180.p0), channel_id=1, source_target_pairs={{0,24},{4,28},{8,16},{12,20},{16,8},{20,12},{24,0},{28,4},{1,25},{... | collective-permute-start | bytes 663560 | tf_op jit(solution)/shard_map/ppermute | solution.py:679
  14.8 9.0 %collective-permute-start.8 = (bf16[4,8,3456]{2,1,0:T(8,128)(2,1)S(1)}, bf16[4,8,3456]{2,1,0:T(8,128)(2,1)S(1)}, u32[]{:S(2)}, u32[]{:S(2)}) collective-permute-start(bf16[4,8,3456]{2,1,0:T(8,128)(2,1)S(1)} %shard_map.180.p0), channel_id=1, source_target_pairs={{0,16},{4,20},{8,24},{12,28},{16,0},{20,4},{24,8},{28,12},{1,17},{... | collective-permute-start | bytes 663560 | tf_op jit(solution)/shard_map/ppermute | solution.py:679
  15.4 8.4 %collective-permute-start.5 = (bf16[4,8,3456]{2,1,0:T(8,128)(2,1)S(1)}, bf16[4,8,3456]{2,1,0:T(8,128)(2,1)S(1)}, u32[]{:S(2)}, u32[]{:S(2)}) collective-permute-start(bf16[4,8,3456]{2,1,0:T(8,128)(2,1)S(1)} %shard_map.180.p0), channel_id=1, source_target_pairs={{0,8},{4,12},{8,0},{12,4},{16,24},{20,28},{24,16},{28,20},{1,9},{5... | collective-permute-start | bytes 663560 | tf_op jit(solution)/shard_map/ppermute | solution.py:679
  15.9 0.7 %copy-start.2 = (f32[4]{0:T(128)S(1)}, f32[4]{0:T(128)}, u32[]{:S(2)}) copy-start(f32[4]{0:T(128)} %scale_ref.1) | copy-start | bytes 52
  21.3 2.4 %collective-permute-start.7 = (bf16[4,8,3456]{2,1,0:T(8,128)(2,1)S(1)}, bf16[4,8,3456]{2,1,0:T(8,128)(2,1)S(1)}, u32[]{:S(2)}, u32[]{:S(2)}) collective-permute-start(bf16[4,8,3456]{2,1,0:T(8,128)(2,1)S(1)} %collective-permute-done.6.p3), channel_id=1, source_target_pairs={{0,4},{4,0},{8,12},{12,8},{16,20},{20,16},{24,28},{28,24},{1,5},{5... | collective-permute-start | bytes 663560 | tf_op jit(solution)/shard_map/ppermute | solution.py:679
  21.3 2.9 %collective-permute-start.9 = (bf16[4,8,3456]{2,1,0:T(8,128)(2,1)S(1)}, bf16[4,8,3456]{2,1,0:T(8,128)(2,1)S(1)}, u32[]{:S(2)}, u32[]{:S(2)}) collective-permute-start(bf16[4,8,3456]{2,1,0:T(8,128)(2,1)S(1)} %shard_map.180.p0), channel_id=1, source_target_pairs={{0,4},{4,0},{8,12},{12,8},{16,20},{20,16},{24,28},{28,24},{1,5},{5... | collective-permute-start | bytes 663560 | tf_op jit(solution)/shard_map/ppermute | solution.py:679
  23.8 1.5 %collective-permute-start.11 = (bf16[4,8,3456]{2,1,0:T(8,128)(2,1)S(1)}, bf16[4,8,3456]{2,1,0:T(8,128)(2,1)S(1)}, u32[]{:S(2)}, u32[]{:S(2)}) collective-permute-start(bf16[4,8,3456]{2,1,0:T(8,128)(2,1)S(1)} %collective-permute-done.8.p2), channel_id=1, source_target_pairs={{0,4},{4,0},{8,12},{12,8},{16,20},{20,16},{24,28},{28,24},{1,5},{5... | collective-permute-start | bytes 663560 | tf_op jit(solution)/shard_map/ppermute | solution.py:679
  23.8 1.8 %collective-permute-start.10 = (bf16[4,8,3456]{2,1,0:T(8,128)(2,1)S(1)}, bf16[4,8,3456]{2,1,0:T(8,128)(2,1)S(1)}, u32[]{:S(2)}, u32[]{:S(2)}) collective-permute-start(bf16[4,8,3456]{2,1,0:T(8,128)(2,1)S(1)} %collective-permute-done.5.p1), channel_id=1, source_target_pairs={{0,4},{4,0},{8,12},{12,8},{16,20},{20,16},{24,28},{28,24},{1,5},{5... | collective-permute-start | bytes 663560 | tf_op jit(solution)/shard_map/ppermute | solution.py:679
  29.9 3.5 %collective-permute-start.12 = (bf16[4,4,8,2560]{3,2,1,0:T(8,128)(2,1)S(1)}, bf16[4,4,8,2560]{3,2,1,0:T(8,128)(2,1)S(1)}, u32[]{:S(2)}, u32[]{:S(2)}) collective-permute-start(bf16[4,4,8,2560]{3,2,1,0:T(8,128)(2,1)S(1)} %get-tuple-element.102), channel_id=1, source_target_pairs={{0,4},{4,0},{8,12},{12,8},{16,20},{20,16},{24,28},{28,24},{1,5},{5... | collective-permute-start | bytes 1966088 | tf_op jit(solution)/shard_map/ppermute | solution.py:679
  33.0 1.9 %collective-permute-start.14 = (bf16[4,4,8,896]{3,2,1,0:T(8,128)(2,1)S(1)}, bf16[4,4,8,896]{3,2,1,0:T(8,128)(2,1)S(1)}, u32[]{:S(2)}, u32[]{:S(2)}) collective-permute-start(bf16[4,4,8,896]{3,2,1,0:T(8,128)(2,1)S(1)} %get-tuple-element.122), channel_id=1, source_target_pairs={{0,4},{4,0},{8,12},{12,8},{16,20},{20,16},{24,28},{28,24},{1,5},{5... | collective-permute-start | bytes 688136 | tf_op jit(solution)/shard_map/ppermute | solution.py:679
  33.6 6.0 %collective-permute-start.13 = (bf16[4,8,2560]{2,1,0:T(8,128)(2,1)S(1)}, bf16[4,8,2560]{2,1,0:T(8,128)(2,1)S(1)}, u32[]{:S(2)}, u32[]{:S(2)}) collective-permute-start(bf16[4,8,2560]{2,1,0:T(8,128)(2,1)S(1)} %get-tuple-element.105), channel_id=1, source_target_pairs={{0,8},{4,20},{8,0},{12,28},{16,24},{20,4},{24,16},{28,12},{1,9},{5... | collective-permute-start | bytes 491528 | tf_op jit(solution)/shard_map/ppermute | solution.py:691
  35.0 4.6 %collective-permute-start.15 = (bf16[4,8,896]{2,1,0:T(8,128)(2,1)S(1)}, bf16[4,8,896]{2,1,0:T(8,128)(2,1)S(1)}, u32[]{:S(2)}, u32[]{:S(2)}) collective-permute-start(bf16[4,8,896]{2,1,0:T(8,128)(2,1)S(1)} %get-tuple-element.123), channel_id=1, source_target_pairs={{0,8},{4,20},{8,0},{12,28},{16,24},{20,4},{24,16},{28,12},{1,9},{5... | collective-permute-start | bytes 172040 | tf_op jit(solution)/shard_map/ppermute | solution.py:691
  36.0 9.6 %collective-permute-start.18 = (bf16[4,8,3456]{2,1,0:T(8,128)(2,1)S(1)}, bf16[4,8,3456]{2,1,0:T(8,128)(2,1)S(1)}, u32[]{:S(2)}, u32[]{:S(2)}) collective-permute-start(bf16[4,8,3456]{2,1,0:T(8,128)(2,1)S(1)} %shard_map.187), channel_id=1, source_target_pairs={{0,8},{4,20},{8,0},{12,28},{16,24},{20,4},{24,16},{28,12},{1,9},{5... | collective-permute-start | bytes 663560 | tf_op jit(solution)/shard_map/ppermute | solution.py:691
  39.6 6.0 %collective-permute-start.16 = (bf16[4,8,2560]{2,1,0:T(8,128)(2,1)S(1)}, bf16[4,8,2560]{2,1,0:T(8,128)(2,1)S(1)}, u32[]{:S(2)}, u32[]{:S(2)}) collective-permute-start(bf16[4,8,2560]{2,1,0:T(8,128)(2,1)S(1)} %shard_map.185), channel_id=1, source_target_pairs={{0,16},{4,12},{8,24},{12,4},{16,0},{20,28},{24,8},{28,20},{1,17},{... | collective-permute-start | bytes 491528 | tf_op jit(solution)/shard_map/ppermute | solution.py:688
  41.0 4.6 %collective-permute-start.17 = (bf16[4,8,896]{2,1,0:T(8,128)(2,1)S(1)}, bf16[4,8,896]{2,1,0:T(8,128)(2,1)S(1)}, u32[]{:S(2)}, u32[]{:S(2)}) collective-permute-start(bf16[4,8,896]{2,1,0:T(8,128)(2,1)S(1)} %shard_map.186), channel_id=1, source_target_pairs={{0,16},{4,12},{8,24},{12,4},{16,0},{20,28},{24,8},{28,20},{1,17},{... | collective-permute-start | bytes 172040 | tf_op jit(solution)/shard_map/ppermute | solution.py:688
  42.3 9.0 %collective-permute-start.19 = (bf16[192,256]{1,0:T(8,128)(2,1)S(1)}, bf16[192,256]{1,0:T(8,128)(2,1)S(1)}, u32[]{:S(2)}, u32[]{:S(2)}) collective-permute-start(bf16[192,256]{1,0:T(8,128)(2,1)S(1)} %get-tuple-element.144), channel_id=1, source_target_pairs={{0,4},{4,0},{8,12},{12,8},{16,20},{20,16},{24,28},{28,24},{1,5},{5... | collective-permute-start | bytes 294920 | tf_op jit(solution)/shard_map/ppermute | solution.py:679
  42.4 8.9 %collective-permute-start.20 = (bf16[192,256]{1,0:T(8,128)(2,1)S(1)}, bf16[192,256]{1,0:T(8,128)(2,1)S(1)}, u32[]{:S(2)}, u32[]{:S(2)}) collective-permute-start(bf16[192,256]{1,0:T(8,128)(2,1)S(1)} %get-tuple-element.145), channel_id=1, source_target_pairs={{0,28},{4,8},{8,4},{12,16},{16,12},{20,24},{24,20},{28,0},{1,29},{... | collective-permute-start | bytes 294920 | tf_op jit(solution)/shard_map/ppermute | solution.py:744
  45.8 6.6 %collective-permute-start.21 = (bf16[8,3456]{1,0:T(8,128)(2,1)S(1)}, bf16[8,3456]{1,0:T(8,128)(2,1)S(1)}, u32[]{:S(2)}, u32[]{:S(2)}) collective-permute-start(bf16[8,3456]{1,0:T(8,128)(2,1)S(1)} %get-tuple-element.149), channel_id=1, source_target_pairs={{0,3},{1,2},{2,1},{3,0},{4,7},{5,6},{6,5},{7,4},{8,11},{9,10},{10,... | collective-permute-start | bytes 165896 | tf_op jit(solution)/shard_map/ppermute | solution.py:679
  48.6 5.5 %collective-permute-start.22 = (bf16[8,3456]{1,0:T(8,128)(2,1)S(1)}, bf16[8,3456]{1,0:T(8,128)(2,1)S(1)}, u32[]{:S(2)}, u32[]{:S(2)}) collective-permute-start(bf16[8,3456]{1,0:T(8,128)(2,1)S(1)} %get-tuple-element.150), channel_id=1, source_target_pairs={{0,2},{1,3},{2,0},{3,1},{4,6},{5,7},{6,4},{7,5},{8,10},{9,11},{10,... | collective-permute-start | bytes 165896 | tf_op jit(solution)/shard_map/ppermute | solution.py:679
  48.9 5.2 %collective-permute-start.23 = (bf16[8,3456]{1,0:T(8,128)(2,1)S(1)}, bf16[8,3456]{1,0:T(8,128)(2,1)S(1)}, u32[]{:S(2)}, u32[]{:S(2)}) collective-permute-start(bf16[8,3456]{1,0:T(8,128)(2,1)S(1)} %get-tuple-element.151), channel_id=1, source_target_pairs={{0,1},{1,0},{2,3},{3,2},{4,5},{5,4},{6,7},{7,6},{8,9},{9,8},{10,11... | collective-permute-start | bytes 165896 | tf_op jit(solution)/shard_map/ppermute | solution.py:679

commit v4 on v3

--- a/solution.py
+++ b/solution.py
@@ -209,10 +209,20 @@
         line_ref[place[3] ^ index] = part[...]
 
 
-def core_sum_kernel(place, mine_ref, got_ref, *outs):
+def carried(total):
+    tail = total[..., total.shape[-1] - 128 :]
+    value = tail[..., 4:5, :] + tail[..., 5:6, :]
+    high = value.astype(BF16).astype(F32)
+    row = lax.broadcasted_iota(jnp.int32, tail.shape, tail.ndim - 2)
+    tail = jnp.where(row == 4, high, jnp.where(row == 5, value - high, tail))
+    return jnp.concatenate([total[..., : total.shape[-1] - 128], tail], axis=-1)
+
+
+def core_sum_kernel(carry, place, mine_ref, got_ref, *outs):
     for index, out_ref in enumerate(outs):
         chip = place[1] ^ (0, place[6], place[6] ^ 3, 3)[index]
-        out_ref[...] = (mine_ref[chip].astype(F32) + got_ref[chip].astype(F32)).astype(BF16)
+        total = mine_ref[chip].astype(F32) + got_ref[chip].astype(F32)
+        out_ref[...] = (carried(total) if carry else total).astype(BF16)
 
 
 def join_kernel(one_ref, two_ref, out_ref):
@@ -221,14 +231,17 @@
     out_ref[:, :, split:] = two_ref[...]
 
 
-def pair_sum_kernel(one_ref, two_ref, out_ref):
-    out_ref[...] = (one_ref[...].astype(F32) + two_ref[...].astype(F32)).astype(BF16)
+def pair_sum_kernel(carry, one_ref, two_ref, out_ref):
+    total = one_ref[...].astype(F32) + two_ref[...].astype(F32)
+    out_ref[...] = (carried(total) if carry else total).astype(BF16)
 
 
 def chip_sum_kernel(place, p0, p1, q0, q1, both, o0, o1, o2, o3, keep_ref):
     split = p0.shape[-1]
     keep_ref[:, :, :split] = p0[...].astype(F32) + p1[...].astype(F32) + both[:, :, :split].astype(F32)
-    keep_ref[:, :, split:] = q0[...].astype(F32) + q1[...].astype(F32) + both[:, :, split:].astype(F32)
+    keep_ref[:, :, split:] = carried(
+        q0[...].astype(F32) + q1[...].astype(F32) + both[:, :, split:].astype(F32)
+    )
     for index, out_ref in enumerate((o0, o1, o2, o3)):
         out_ref[...] = keep_ref[place[3] ^ index].astype(out_ref.dtype)
 
@@ -313,7 +326,7 @@
 
 def attend_kernel(
     heads, root_ref, unit_ref, cos_ref, sine_ref, mask_ref, sums, w_ref,
-    query_ref, key_ref, value_ref, raised_ref, mixed_ref, inverse_ref, along_q_ref, length_q_ref, along_k_ref, length_k_ref,
+    query_ref, key_ref, value_ref, raised_ref, mixed_ref, inverse_ref, inverse_rows_ref, along_q_ref, length_q_ref, along_k_ref, length_k_ref,
     gain_ref, gain_col_ref,
 ):
     bands, count = mask_ref.shape[:2]
@@ -362,14 +375,16 @@
                 raised[2 * pair * count : 2 * (pair + 1) * count],
                 jnp.concatenate([value[:, lanes], ones_half], axis=1),
             )
-            inverse = 1.0 / merge_pair(both[:, 128:], size)
+            rows_inverse = 1.0 / both[:, 128:]
+            inverse_rows_ref[band, 2 * pair * count : 2 * (pair + 1) * count, :] = rows_inverse
+            inverse = merge_pair(rows_inverse, size)
             mixed_ref[span, lanes] = merge_pair(both[:, :128], size) * inverse
             inverse_ref[span, lanes] = inverse
 
 
 def feed_kernel(
     heads, inputs_ref, cot_ref, w_up_ref, w_out_ref, gain_ref, mixed_ref, inverse_ref,
-    middle_ref, middle_grad_ref, shrunk_ref, gain_grad_ref,
+    middle_ref, middle_grad_ref, shrunk_ref, d_mixed_ref, levels_ref, gain_grad_ref,
     w_down_ref, mixed_low_ref, normed_ref, gated_ref, d_exp_ref, branch_ref,
 ):
     width = inputs_ref.shape[1]
@@ -411,7 +426,19 @@
     middle_grad_ref[...] = d_middle
     branch = d_middle.astype(BF16)
     branch_ref[...] = branch
-    shrunk_ref[...] = (mm_rt(branch, w_out) * inverse_ref[...]).astype(BF16)
+    d_mixed = mm_rt(branch, w_out)
+    shrunk_ref[...] = (d_mixed * inverse_ref[...]).astype(BF16)
+    d_mixed = d_mixed.astype(BF16)
+    d_mixed_ref[...] = d_mixed
+    level_rows = d_mixed.astype(F32) * mixed
+    lane = lax.broadcasted_iota(jnp.int32, (width, 128), 1)
+    head = lax.broadcasted_iota(jnp.int32, (width, 128), 0) // (width // heads)
+    pick = jnp.where((lane % heads == head) & (lane < 2 * heads), 1.0, 0.0).astype(BF16)
+    high = level_rows.astype(BF16)
+    levels = mm(high, pick) + mm((level_rows - high.astype(F32)).astype(BF16), pick)
+    high = levels.astype(BF16).astype(F32)
+    lane = lax.broadcasted_iota(jnp.int32, levels.shape, 1)
+    levels_ref[...] = jnp.where(lane < heads, high, levels - high).astype(BF16)
 
 
 def weights_kernel(place, cot_ref, mixed_low_ref, normed_ref, gated_ref, d_exp_ref, branch_ref, mine_ref, other_ref):
@@ -491,8 +518,8 @@
 def forward_kernel(
     heads, place, root_ref, unit_ref, cos_ref, sine_ref, mask_ref, inputs_ref, cot_ref,
     p0, p1, p2, p3, p4, p5, p6, p7,
-    query_ref, key_ref, value_ref, raised_ref, mixed_ref, along_q_ref, length_q_ref, along_k_ref, length_k_ref,
-    gain_ref, gain_col_ref, w_ref, middle_ref, middle_grad_ref, shrunk_ref, gain_grad_ref,
+    query_ref, key_ref, value_ref, raised_ref, inverse_rows_ref, mixed_ref, along_q_ref, length_q_ref, along_k_ref, length_k_ref,
+    gain_ref, gain_col_ref, w_ref, middle_ref, middle_grad_ref, shrunk_ref, d_mixed_ref, levels_ref, gain_grad_ref,
     w_down_ref, gated_ref, mine_ref, other_ref,
     inverse_ref, w_up_ref, w_out_ref, mixed_low_ref, normed_ref, d_exp_ref, branch_ref,
 ):
@@ -508,12 +535,12 @@
         store_rows(w_down_ref, start, jnp.concatenate(down, axis=1))
     attend_kernel(
         heads, root_ref, unit_ref, cos_ref, sine_ref, mask_ref, sums, w_ref,
-        query_ref, key_ref, value_ref, raised_ref, mixed_ref, inverse_ref,
+        query_ref, key_ref, value_ref, raised_ref, mixed_ref, inverse_ref, inverse_rows_ref,
         along_q_ref, length_q_ref, along_k_ref, length_k_ref, gain_ref, gain_col_ref,
     )
     feed_kernel(
         heads, inputs_ref, cot_ref, w_up_ref, w_out_ref, gain_ref, mixed_ref, inverse_ref,
-        middle_ref, middle_grad_ref, shrunk_ref, gain_grad_ref,
+        middle_ref, middle_grad_ref, shrunk_ref, d_mixed_ref, levels_ref, gain_grad_ref,
         w_down_ref, mixed_low_ref, normed_ref, gated_ref, d_exp_ref, branch_ref,
     )
     weights_kernel(
@@ -522,7 +549,7 @@
 
 
 def backward_kernel(
-    heads, rows, place, root_ref, shrunk_ref, mixed_ref, raised_ref, query_ref, key_ref, value_ref,
+    heads, rows, place, root_ref, shrunk_ref, d_mixed_ref, levels_ref, raised_ref, inverse_rows_ref, query_ref, key_ref, value_ref,
     cos_ref, sine_ref, w_ref, gain_col_ref, unit_turned_ref, own_turned_ref, along_q_ref, length_q_ref,
     along_k_ref, length_k_ref, gain_grad_ref,
     d_query_ref, d_rest_ref, mine_ref, other_ref,
@@ -538,22 +565,29 @@
         whole = slice(start, start + keys)
         own = slice(start + edge, start + edge + count)
         shrunk = shrunk_ref[span].astype(F32)
-        level_rows = -(shrunk * mixed_ref[span])
+        d_mixed = d_mixed_ref[span].astype(F32)
+        levels = levels_ref[span].astype(F32)
+        lane = lax.broadcasted_iota(jnp.int32, levels.shape, 1)
         value = value_ref[whole, :]
         raised = raised_ref[band]
         parts, stacks = [], []
         for pair in range(heads // 2):
             lanes = slice(128 * pair, 128 * pair + 128)
             stacks.append(pair_lanes(shrunk, heads, pair))
+            terms = jnp.concatenate(
+                [jnp.where(lane % heads == h, -levels, 0.0) for h in (2 * pair, 2 * pair + 1)], axis=0
+            ).astype(BF16)
             parts.append(
                 mm_rt(
-                    jnp.concatenate([stacks[-1], pair_lanes(level_rows, heads, pair)], axis=1),
+                    jnp.concatenate([pair_lanes(d_mixed, heads, pair), terms], axis=1),
                     jnp.concatenate([value[:, lanes], ones_half], axis=1),
                 )
             )
-        d_scores = (raised.astype(F32) * jnp.concatenate(parts, axis=0)).astype(BF16)
-        query = query_ref[span, :].astype(F32)
-        d_key = mm_lt(d_scores, stack_heads(query, heads))
+        query = stack_heads(query_ref[span, :].astype(F32), heads)
+        inverse = jnp.concatenate([inverse_rows_ref[band]] * (keys // 128), axis=1)
+        probs = jnp.where(raised > 0, jnp.exp(mm_rt(query, key_ref[whole, :])) * inverse, 0.0)
+        d_scores = (probs * jnp.concatenate(parts, axis=0)).astype(BF16)
+        d_key = mm_lt(d_scores, query)
         d_query = fold_heads(mm(d_scores, key_ref[whole, :]), heads)
         for pair in range(heads // 2):
             lanes = slice(width + 128 * pair, width + 128 * pair + 128)
@@ -776,8 +810,8 @@
         parts = mine + [core_move(part) for part in mine[:3]] + [far]
 
     (
-        query, key, value, raised, mixed, along_q, length_q, along_k, length_k, gain, gain_col, w_qkv,
-        middle, middle_grad, shrunk, gain_grad, w_down, gated, mine_second, other_second,
+        query, key, value, raised, inverse_rows, mixed, along_q, length_q, along_k, length_k, gain, gain_col, w_qkv,
+        middle, middle_grad, shrunk, d_mixed, levels, gain_grad, w_down, gated, mine_second, other_second,
     ) = call(
         functools.partial(forward_kernel, heads),
         [
@@ -785,6 +819,7 @@
             low(2 * tokens, width),
             low(2 * tokens, width),
             low(bands, heads * count, 2 * count),
+            shape(bands, heads * count, 128),
             shape(tokens, width),
             shape(tokens, width),
             shape(tokens, width // 2),
@@ -796,6 +831,8 @@
             shape(tokens, width),
             shape(tokens, width),
             low(tokens, width),
+            low(tokens, width),
+            low(tokens, 128),
             shape(1, width),
             low(hidden, width),
             low(tokens, hidden),
@@ -825,7 +862,7 @@
         place=place,
         flops=1,
     )(
-        root, shrunk, mixed, raised, query, key, value, cos, sine, w_qkv, gain_col, unit_turned, own_turned,
+        root, shrunk, d_mixed, levels, raised, inverse_rows, query, key, value, cos, sine, w_qkv, gain_col, unit_turned, own_turned,
         along_q, length_q, along_k, length_k, gain_grad,
     )
 
@@ -846,25 +883,25 @@
 
     if direct:
         all_lanes = second_lanes + first_lanes
-        def core_sum(mine, got):
-            return call(core_sum_kernel, [low(group, 8, mine.shape[-1]) for _ in range(chips)], place=place)(mine, got)
-
-        def pair_sum(one, two):
-            return call(pair_sum_kernel, [low(*one.shape)], flops=1)(one, two)[0]
+        def core_sum(carry, mine, got):
+            return call(functools.partial(core_sum_kernel, carry), [low(group, 8, mine.shape[-1]) for _ in range(chips)], place=place)(mine, got)
+
+        def pair_sum(carry, one, two):
+            return call(functools.partial(pair_sum_kernel, carry), [low(*one.shape)], flops=1)(one, two)[0]
 
         first_got = core_move(other_first)
-        second_own, second_near, second_beside, second_far = core_sum(mine_second, core_move(other_second))
+        second_own, second_near, second_beside, second_far = core_sum(False, mine_second, core_move(other_second))
         second_far = second_chip(second_far)
-        first_own, first_near, first_beside, first_far = core_sum(mine_first, first_got)
+        first_own, first_near, first_beside, first_far = core_sum(True, mine_first, first_got)
         first_far = second_chip(first_far)
         second_far, first_far = lax.optimization_barrier((second_far, first_far))
         first_own, d_rest = lax.optimization_barrier((first_own, d_rest))
         beside = second_chip(call(join_kernel, [low(group, 8, all_lanes)], flops=1)(second_beside, first_beside)[0])
         sums = [
             second_own,
-            first_chip(pair_sum(second_near, second_far)),
+            first_chip(pair_sum(False, second_near, second_far)),
             first_own,
-            first_chip(pair_sum(first_near, first_far)),
+            first_chip(pair_sum(True, first_near, first_far)),
             beside,
         ]
         own_grad, rim_swap, rim_beside = normed_back(d_query, d_rest)

time: 55.1 us -> 55.7 us (1.011)
  transfers between devices with their start and end apart: 24 -> 24, of which waited for: 8 -> 8; matrix products, arithmetic and copies ran while one was open for 1% -> 1% of each run, Pallas kernels for 13% -> 14%
where the time goes in v4:
time: 55.7 us; the launch traced here: 55.4 us
  starting transfers between devices  25 us (45%)
  Pallas kernels  14 us (25%)
  waiting for transfers between devices  13.4 us (24%)
  local copies, waits for them, and re-layouts  1.76 us (3%)
  between operations  0.87 us (2%)
    ppermute x17, starting transfers between devices, over(): lax.ppermute(value, axis, [(i, i ^ by) for i in range(size_of)])  15.8 us
    pallas_call x15, Pallas kernels, run(): pl.pallas_call(kernel, out_shape=outs, in_specs=[pl.BlockSpec(memory_spac...  14 us
    ppermute x17, waiting for transfers between devices, over(): lax.ppermute(value, axis, [(i, i ^ by) for i in range(size_of)])  10 us
    ppermute x2, starting transfers between devices, beside_move(): return lax.ppermute(value, 'rows', beside_pairs)  3.54 us
    ppermute x3, starting transfers between devices, second_chip(): return lax.ppermute(value, 'rows', chip_pairs(1))  3.5 us
    ppermute x3, waiting for transfers between devices, second_chip(): return lax.ppermute(value, 'rows', chip_pairs(1))  2.39 us
    ppermute x2, starting transfers between devices, first_chip(): return lax.ppermute(value, 'rows', chip_pairs(0))  2.16 us
    unnamed x8, local copies, waits for them, and re-layouts  1.39 us
  transfers between devices with their start and end apart: 24, of which 8 were waited for; matrix products, arithmetic and copies ran while one was open for 1% of the time, Pallas kernels for 14%

profile of v4, /device:TPU:0, one launch (start us, length us, event | category | flops | bytes accessed | tf_op | source)
XLA Modules:
  0.0 55.4 jit_solution(10373695670329489071)
XLA Ops:
  0.7 1.1 %shard_map.179 = (bf16[8,3456]{1,0:T(8,128)(2,1)S(1)}, bf16[8,3456]{1,0:T(8,128)(2,1)S(1)}, f32[24,2]{1,0:T(8,128)S(1)}) custom-call(bf16[2,768]{1,0:T(2,128)(2,1)} %cond_ref.1, bf16[8,768]{1,0:T(8,128)(2,1)} %qkv_ref.1, bf16[8,1536]{1,0:T(8,128)(2,1)} %up_ref.1, bf16[8,256]{1,0:T(8,128)(2,1)} %out_ref.1, bf16[24,256]{1,0:T(8,128)(2,1)} %down_ref.1, ...), custom_call_target="tpu_custom_call" | custom-call | flops 1000000000 | bytes 4000000 | tf_op jit(solution)/shard_map/pallas_call | solution.py:632
  1.7 4.1 %collective-permute-start.4 = (bf16[8,3456]{1,0:T(8,128)(2,1)S(1)}, bf16[8,3456]{1,0:T(8,128)(2,1)S(1)}, u32[]{:S(2)}, u32[]{:S(2)}) collective-permute-start(bf16[8,3456]{1,0:T(8,128)(2,1)S(1)} %get-tuple-element.94), channel_id=1, source_target_pairs={{0,2},{1,3},{2,0},{3,1},{4,6},{5,7},{6,4},{7,5},{8,10},{9,11},{10,... | collective-permute-start | bytes 165896 | tf_op jit(solution)/shard_map/ppermute | solution.py:713
  5.8 1.3 %collective-permute-start.2 = (bf16[8,3456]{1,0:T(8,128)(2,1)S(1)}, bf16[8,3456]{1,0:T(8,128)(2,1)S(1)}, u32[]{:S(2)}, u32[]{:S(2)}) collective-permute-start(bf16[8,3456]{1,0:T(8,128)(2,1)S(1)} %get-tuple-element.94), channel_id=1, source_target_pairs={{0,3},{1,2},{2,1},{3,0},{4,7},{5,6},{6,5},{7,4},{8,11},{9,10},{10,... | collective-permute-start | bytes 165896 | tf_op jit(solution)/shard_map/ppermute | solution.py:713
  7.2 0.2 collective-permute-start.3
  7.5 1.4 %collective-permute-start.1 = (bf16[3,64,256]{2,1,0:T(8,128)(2,1)S(1)}, bf16[3,64,256]{2,1,0:T(8,128)(2,1)S(1)}, u32[]{:S(2)}, u32[]{:S(2)}) collective-permute-start(bf16[3,64,256]{2,1,0:T(8,128)(2,1)S(1)} %get-tuple-element.163), channel_id=1, source_target_pairs={{0,28},{4,8},{8,4},{12,16},{16,12},{20,24},{24,20},{28,0},{1,29},{... | collective-permute-start | bytes 294920 | tf_op jit(solution)/shard_map/ppermute | solution.py:778
  8.8 0.3 collective-permute-start
  9.2 0.1 fusion.3
  9.3 0.2 fusion.1
  9.6 0.7 %copy-done.3 = s32[64,64]{1,0:T(8,128)S(1)} copy-done((s32[64,64]{1,0:T(8,128)S(1)}, s32[64,64]{1,0:T(8,128)}, u32[]{:S(2)}) %copy-start.3) | copy-done | bytes 16408
  10.3 0.1 slice.11
  10.4 1.5 %collective-permute-done.3.p2 = bf16[8,3456]{1,0:T(8,128)(2,1)S(1)} collective-permute-done((bf16[8,3456]{1,0:T(8,128)(2,1)S(1)}, bf16[8,3456]{1,0:T(8,128)(2,1)S(1)}, u32[]{:S(2)}, u32[]{:S(2)}) %collective-permute-start.3) | collective-permute-done | bytes 55328 | tf_op jit(solution)/shard_map/ppermute | solution.py:713
  12.0 2.5 %collective-permute-start.6 = (bf16[4,8,3456]{2,1,0:T(8,128)(2,1)S(1)}, bf16[4,8,3456]{2,1,0:T(8,128)(2,1)S(1)}, u32[]{:S(2)}, u32[]{:S(2)}) collective-permute-start(bf16[4,8,3456]{2,1,0:T(8,128)(2,1)S(1)} %shard_map.180.p0), channel_id=1, source_target_pairs={{0,24},{4,28},{8,16},{12,20},{16,8},{20,12},{24,0},{28,4},{1,25},{... | collective-permute-start | bytes 663560 | tf_op jit(solution)/shard_map/ppermute | solution.py:713
  14.5 0.1 copy.20
  14.6 0.1 broadcast_in_dim.49
  14.7 0.1 reshape.363.id_key_ref
  14.8 0.6 %collective-permute-start.8 = (bf16[4,8,3456]{2,1,0:T(8,128)(2,1)S(1)}, bf16[4,8,3456]{2,1,0:T(8,128)(2,1)S(1)}, u32[]{:S(2)}, u32[]{:S(2)}) collective-permute-start(bf16[4,8,3456]{2,1,0:T(8,128)(2,1)S(1)} %shard_map.180.p0), channel_id=1, source_target_pairs={{0,16},{4,20},{8,24},{12,28},{16,0},{20,4},{24,8},{28,12},{1,17},{... | collective-permute-start | bytes 663560 | tf_op jit(solution)/shard_map/ppermute | solution.py:713
  15.4 0.5 collective-permute-start.5
  15.9 0.6 %copy-done.2 = f32[4]{0:T(128)S(1)} copy-done((f32[4]{0:T(128)S(1)}, f32[4]{0:T(128)}, u32[]{:S(2)}) %copy-start.2) | copy-done | bytes 40
  16.6 1.3 %shard_map.178 = (f32[1024,256]{1,0:T(8,128)S(1)}, bf16[256,1024]{1,0:T(8,128)(2,1)S(1)}, bf16[256,512]{1,0:T(8,128)(2,1)S(1)}, f32[1024,128]{1,0:T(8,128)S(1)},...) custom-call(f32[4]{0:T(128)S(1)} %copy-done.2, ...), custom_call_target="tpu_custom_call" | custom-call | flops 1000000000 | bytes 4000000 | tf_op jit(solution)/shard_map/pallas_call | solution.py:632
  17.9 3.5 %collective-permute-done.6.p3 = bf16[4,8,3456]{2,1,0:T(8,128)(2,1)S(1)} collective-permute-done((bf16[4,8,3456]{2,1,0:T(8,128)(2,1)S(1)}, bf16[4,8,3456]{2,1,0:T(8,128)(2,1)S(1)}, u32[]{:S(2)}, u32[]{:S(2)}) %collective-permute-start.6) | collective-permute-done | bytes 221216 | tf_op jit(solution)/shard_map/ppermute | solution.py:713
  21.3 0.5 collective-permute-start.9
  21.8 1.9 %collective-permute-done.8.p2 = bf16[4,8,3456]{2,1,0:T(8,128)(2,1)S(1)} collective-permute-done((bf16[4,8,3456]{2,1,0:T(8,128)(2,1)S(1)}, bf16[4,8,3456]{2,1,0:T(8,128)(2,1)S(1)}, u32[]{:S(2)}, u32[]{:S(2)}) %collective-permute-start.8) | collective-permute-done | bytes 221216 | tf_op jit(solution)/shard_map/ppermute | solution.py:713
  23.8 0.5 collective-permute-start.10
  24.3 1.0 %collective-permute-done.11.p6 = bf16[4,8,3456]{2,1,0:T(8,128)(2,1)S(1)} collective-permute-done((bf16[4,8,3456]{2,1,0:T(8,128)(2,1)S(1)}, bf16[4,8,3456]{2,1,0:T(8,128)(2,1)S(1)}, u32[]{:S(2)}, u32[]{:S(2)}) %collective-permute-start.11) | collective-permute-done | bytes 221216 | tf_op jit(solution)/shard_map/ppermute | solution.py:713
  25.2 0.3 collective-permute-done.10.p5
  25.5 4.5 %shard_map.181 = (bf16[512,256]{1,0:T(8,128)(2,1)S(1)}, bf16[1024,256]{1,0:T(8,128)(2,1)S(1)}, bf16[1024,256]{1,0:T(8,128)(2,1)S(1)}, bf16[4,512,256]{2,1,0:T(8,...) custom-call(f32[1,128]{1,0:T(1,128)S(1)} %get-tuple-element.86.root_, ...), custom_call_target="tpu_custom_call" | custom-call | flops 1000000000 | bytes 4000000 | tf_op jit(solution)/shard_map/pallas_call | solution.py:632
  30.1 0.3 collective-permute-start.12
  30.3 3.2 %shard_map.183 = (bf16[512,256]{1,0:T(8,128)(2,1)S(1)}, bf16[1024,512]{1,0:T(8,128)(2,1)S(1)}, bf16[4,4,8,896]{3,2,1,0:T(8,128)(2,1)S(1)}, bf16[4,4,8,896]{3,2,1,0:T(8,128)(2,1)S(1)}) custom-call(f32[1,128]{1,0:T(1,128)S(1)} %get-tuple-element.86.root_ref, bf16[512,256]{1,0:T(8,128)(2,1)S(1)} %get-tuple-element.108.shrunk_ref, ...), custom_call_target="tpu_custom_call" | custom-call | flops 1 | bytes 1 | tf_op jit(solution)/shard_map/pallas_call | solution.py:632
  33.6 0.4 collective-permute-start.14
  33.9 0.2 shard_map.182
  34.1 1.3 %collective-permute-start.13 = (bf16[4,8,2560]{2,1,0:T(8,128)(2,1)S(1)}, bf16[4,8,2560]{2,1,0:T(8,128)(2,1)S(1)}, u32[]{:S(2)}, u32[]{:S(2)}) collective-permute-start(bf16[4,8,2560]{2,1,0:T(8,128)(2,1)S(1)} %get-tuple-element.107), channel_id=1, source_target_pairs={{0,8},{4,20},{8,0},{12,28},{16,24},{20,4},{24,16},{28,12},{1,9},{5... | collective-permute-start | bytes 491528 | tf_op jit(solution)/shard_map/ppermute | solution.py:725
  35.4 0.1 shard_map.184
  35.5 1.0 %collective-permute-start.15 = (bf16[4,8,896]{2,1,0:T(8,128)(2,1)S(1)}, bf16[4,8,896]{2,1,0:T(8,128)(2,1)S(1)}, u32[]{:S(2)}, u32[]{:S(2)}) collective-permute-start(bf16[4,8,896]{2,1,0:T(8,128)(2,1)S(1)} %get-tuple-element.127), channel_id=1, source_target_pairs={{0,8},{4,20},{8,0},{12,28},{16,24},{20,4},{24,16},{28,12},{1,9},{5... | collective-permute-start | bytes 172040 | tf_op jit(solution)/shard_map/ppermute | solution.py:725
  36.5 1.2 %collective-permute-start.18 = (bf16[4,8,3456]{2,1,0:T(8,128)(2,1)S(1)}, bf16[4,8,3456]{2,1,0:T(8,128)(2,1)S(1)}, u32[]{:S(2)}, u32[]{:S(2)}) collective-permute-start(bf16[4,8,3456]{2,1,0:T(8,128)(2,1)S(1)} %shard_map.187), channel_id=1, source_target_pairs={{0,8},{4,20},{8,0},{12,28},{16,24},{20,4},{24,16},{28,12},{1,9},{5... | collective-permute-start | bytes 663560 | tf_op jit(solution)/shard_map/ppermute | solution.py:725
  37.7 2.4 %collective-permute-done.15.two_ref = bf16[4,8,896]{2,1,0:T(8,128)(2,1)S(1)} collective-permute-done((bf16[4,8,896]{2,1,0:T(8,128)(2,1)S(1)}, bf16[4,8,896]{2,1,0:T(8,128)(2,1)S(1)}, u32[]{:S(2)}, u32[]{:S(2)}) %collective-permute-start.15) | collective-permute-done | bytes 57376 | tf_op jit(solution)/shard_map/ppermute | solution.py:725
  40.1 1.4 %collective-permute-start.16 = (bf16[4,8,2560]{2,1,0:T(8,128)(2,1)S(1)}, bf16[4,8,2560]{2,1,0:T(8,128)(2,1)S(1)}, u32[]{:S(2)}, u32[]{:S(2)}) collective-permute-start(bf16[4,8,2560]{2,1,0:T(8,128)(2,1)S(1)} %shard_map.185), channel_id=1, source_target_pairs={{0,16},{4,12},{8,24},{12,4},{16,0},{20,28},{24,8},{28,20},{1,17},{... | collective-permute-start | bytes 491528 | tf_op jit(solution)/shard_map/ppermute | solution.py:722
  41.5 0.8 %collective-permute-start.17 = (bf16[4,8,896]{2,1,0:T(8,128)(2,1)S(1)}, bf16[4,8,896]{2,1,0:T(8,128)(2,1)S(1)}, u32[]{:S(2)}, u32[]{:S(2)}) collective-permute-start(bf16[4,8,896]{2,1,0:T(8,128)(2,1)S(1)} %shard_map.186), channel_id=1, source_target_pairs={{0,16},{4,12},{8,24},{12,4},{16,0},{20,28},{24,8},{28,20},{1,17},{... | collective-permute-start | bytes 172040 | tf_op jit(solution)/shard_map/ppermute | solution.py:722
  42.3 0.5 shard_map.189
  42.9 2.1 %collective-permute-start.20 = (bf16[192,256]{1,0:T(8,128)(2,1)S(1)}, bf16[192,256]{1,0:T(8,128)(2,1)S(1)}, u32[]{:S(2)}, u32[]{:S(2)}) collective-permute-start(bf16[192,256]{1,0:T(8,128)(2,1)S(1)} %get-tuple-element.149), channel_id=1, source_target_pairs={{0,28},{4,8},{8,4},{12,16},{16,12},{20,24},{24,20},{28,0},{1,29},{... | collective-permute-start | bytes 294920 | tf_op jit(solution)/shard_map/ppermute | solution.py:778
  45.1 1.0 %collective-permute-done.17.q1 = bf16[4,8,896]{2,1,0:T(8,128)(2,1)S(1)} collective-permute-done((bf16[4,8,896]{2,1,0:T(8,128)(2,1)S(1)}, bf16[4,8,896]{2,1,0:T(8,128)(2,1)S(1)}, u32[]{:S(2)}, u32[]{:S(2)}) %collective-permute-start.17) | collective-permute-done | bytes 57376 | tf_op jit(solution)/shard_map/ppermute | solution.py:722
  46.1 0.1 shard_map.188
  46.3 2.9 %collective-permute-start.21 = (bf16[8,3456]{1,0:T(8,128)(2,1)S(1)}, bf16[8,3456]{1,0:T(8,128)(2,1)S(1)}, u32[]{:S(2)}, u32[]{:S(2)}) collective-permute-start(bf16[8,3456]{1,0:T(8,128)(2,1)S(1)} %get-tuple-element.153), channel_id=1, source_target_pairs={{0,3},{1,2},{2,1},{3,0},{4,7},{5,6},{6,5},{7,4},{8,11},{9,10},{10,... | collective-permute-start | bytes 165896 | tf_op jit(solution)/shard_map/ppermute | solution.py:713
  49.2 0.3 collective-permute-start.22
  49.5 1.2 %collective-permute-start.23 = (bf16[8,3456]{1,0:T(8,128)(2,1)S(1)}, bf16[8,3456]{1,0:T(8,128)(2,1)S(1)}, u32[]{:S(2)}, u32[]{:S(2)}) collective-permute-start(bf16[8,3456]{1,0:T(8,128)(2,1)S(1)} %get-tuple-element.155), channel_id=1, source_target_pairs={{0,1},{1,0},{2,3},{3,2},{4,5},{5,4},{6,7},{7,6},{8,9},{9,8},{10,11... | collective-permute-start | bytes 165896 | tf_op jit(solution)/shard_map/ppermute | solution.py:713
  50.7 1.1 %shard_map.190 = bf16[8,64,256]{2,1,0:T(8,128)(2,1)} custom-call(f32[512,256]{1,0:T(8,128)S(1)} %get-tuple-element.102.middle_ref, bf16[512,768]{1,0:T(8,128)(2,1)S(1)} %get-tuple-element.144.gated_ref, bf16[768,256]{1,0:T(8,128)(2,1)S(1)} %get-tuple-element.145.w_down_ref), custom_call_target="tpu_custom_call" | custom-call | flops 1000000000 | bytes 4000000 | tf_op jit(solution)/shard_map/pallas_call | solution.py:632
  51.8 1.1 %shard_map.191 = f32[8,64,256]{2,1,0:T(8,128)} custom-call(f32[512,256]{1,0:T(8,128)S(1)} %get-tuple-element.91.inputs_ref, f32[2,256]{1,0:T(2,128)S(1)} %get-tuple-element.146.gain_ref, f32[512,256]{1,0:T(8,128)S(1)} %get-tuple-element.147.own_ref, bf16[192,256]{1,0:T(8,128)(2,1)S(1)} %collective-permute-done.19.rim_swap_ref, ...), custom_call_target="tpu_custom_call" | custom-call | flops 1000000000 | bytes 4000000 | tf_op jit(solution)/shard_map/pallas_call | solution.py:632
  52.9 1.8 %collective-permute-done.22.two_ref = bf16[8,3456]{1,0:T(8,128)(2,1)S(1)} collective-permute-done((bf16[8,3456]{1,0:T(8,128)(2,1)S(1)}, bf16[8,3456]{1,0:T(8,128)(2,1)S(1)}, u32[]{:S(2)}, u32[]{:S(2)}) %collective-permute-start.22) | collective-permute-done | bytes 55328 | tf_op jit(solution)/shard_map/ppermute | solution.py:713
  54.7 0.7 %shard_map.192 = (f32[8,768]{1,0:T(8,128)}, f32[8,256]{1,0:T(8,128)}, f32[8,1536]{1,0:T(8,128)}, f32[24,256]{1,0:T(8,128)}, f32[24,256]{1,0:T(8,128)}, /*index=5*/f32[24,256]{1,0:T(8,128)}, f32[4]{0:T(128)}) custom-call(f32[24,2]{1,0:T(8,128)S(1)} %get-tuple-element.151.cond_ref, f32[8,3456]{1,0:T(8,128)S(1)} %get-tuple-element.152.own_ref, ...), custom_call_target="tpu_custom_call" | custom-call | flops 1000000000 | bytes 4000000 | tf_op jit(solution)/shard_map/pallas_call | solution.py:632
  (40 shorter events, 0.4 us)
Async XLA Ops:
  0.6 6.8 %copy-start = (bf16[8,64,256]{2,1,0:T(8,128)(2,1)S(1)}, bf16[8,64,256]{2,1,0:T(8,128)(2,1)}, u32[]{:S(2)}) copy-start(bf16[8,64,256]{2,1,0:T(8,128)(2,1)} %feat_ref.1) | copy-start | bytes 786436
  1.7 10.2 %collective-permute-start.4 = (bf16[8,3456]{1,0:T(8,128)(2,1)S(1)}, bf16[8,3456]{1,0:T(8,128)(2,1)S(1)}, u32[]{:S(2)}, u32[]{:S(2)}) collective-permute-start(bf16[8,3456]{1,0:T(8,128)(2,1)S(1)} %get-tuple-element.94), channel_id=1, source_target_pairs={{0,2},{1,3},{2,0},{3,1},{4,6},{5,7},{6,4},{7,5},{8,10},{9,11},{10,... | collective-permute-start | bytes 165896 | tf_op jit(solution)/shard_map/ppermute | solution.py:713
  5.8 6.1 %collective-permute-start.2 = (bf16[8,3456]{1,0:T(8,128)(2,1)S(1)}, bf16[8,3456]{1,0:T(8,128)(2,1)S(1)}, u32[]{:S(2)}, u32[]{:S(2)}) collective-permute-start(bf16[8,3456]{1,0:T(8,128)(2,1)S(1)} %get-tuple-element.94), channel_id=1, source_target_pairs={{0,3},{1,2},{2,1},{3,0},{4,7},{5,6},{6,5},{7,4},{8,11},{9,10},{10,... | collective-permute-start | bytes 165896 | tf_op jit(solution)/shard_map/ppermute | solution.py:713
  7.2 4.7 %collective-permute-start.3 = (bf16[8,3456]{1,0:T(8,128)(2,1)S(1)}, bf16[8,3456]{1,0:T(8,128)(2,1)S(1)}, u32[]{:S(2)}, u32[]{:S(2)}) collective-permute-start(bf16[8,3456]{1,0:T(8,128)(2,1)S(1)} %get-tuple-element.93.p0), channel_id=1, source_target_pairs={{0,1},{1,0},{2,3},{3,2},{4,5},{5,4},{6,7},{7,6},{8,9},{9,8},{10,11... | collective-permute-start | bytes 165896 | tf_op jit(solution)/shard_map/ppermute | solution.py:713
  7.5 8.4 %collective-permute-start.1 = (bf16[3,64,256]{2,1,0:T(8,128)(2,1)S(1)}, bf16[3,64,256]{2,1,0:T(8,128)(2,1)S(1)}, u32[]{:S(2)}, u32[]{:S(2)}) collective-permute-start(bf16[3,64,256]{2,1,0:T(8,128)(2,1)S(1)} %get-tuple-element.163), channel_id=1, source_target_pairs={{0,28},{4,8},{8,4},{12,16},{16,12},{20,24},{24,20},{28,0},{1,29},{... | collective-permute-start | bytes 294920 | tf_op jit(solution)/shard_map/ppermute | solution.py:778
  8.8 7.1 %collective-permute-start = (bf16[3,64,256]{2,1,0:T(8,128)(2,1)S(1)}, bf16[3,64,256]{2,1,0:T(8,128)(2,1)S(1)}, u32[]{:S(2)}, u32[]{:S(2)}) collective-permute-start(bf16[3,64,256]{2,1,0:T(8,128)(2,1)S(1)} %get-tuple-element.164), channel_id=1, source_target_pairs={{0,4},{4,0},{8,12},{12,8},{16,20},{20,16},{24,28},{28,24},{1,5},{5... | collective-permute-start | bytes 294920 | tf_op jit(solution)/shard_map/ppermute | solution.py:713
  9.5 0.8 %copy-start.3 = (s32[64,64]{1,0:T(8,128)S(1)}, s32[64,64]{1,0:T(8,128)}, u32[]{:S(2)}) copy-start(s32[64,64]{1,0:T(8,128)} %param.12) | copy-start | bytes 49156
  12.0 3.9 %copy-start.1 = (bf16[8,64,256]{2,1,0:T(8,128)(2,1)S(1)}, bf16[8,64,256]{2,1,0:T(8,128)(2,1)}, u32[]{:S(2)}) copy-start(bf16[8,64,256]{2,1,0:T(8,128)(2,1)} %cot_ref.1) | copy-start | bytes 786436
  12.0 9.3 %collective-permute-start.6 = (bf16[4,8,3456]{2,1,0:T(8,128)(2,1)S(1)}, bf16[4,8,3456]{2,1,0:T(8,128)(2,1)S(1)}, u32[]{:S(2)}, u32[]{:S(2)}) collective-permute-start(bf16[4,8,3456]{2,1,0:T(8,128)(2,1)S(1)} %shard_map.180.p0), channel_id=1, source_target_pairs={{0,24},{4,28},{8,16},{12,20},{16,8},{20,12},{24,0},{28,4},{1,25},{... | collective-permute-start | bytes 663560 | tf_op jit(solution)/shard_map/ppermute | solution.py:713
  14.8 9.0 %collective-permute-start.8 = (bf16[4,8,3456]{2,1,0:T(8,128)(2,1)S(1)}, bf16[4,8,3456]{2,1,0:T(8,128)(2,1)S(1)}, u32[]{:S(2)}, u32[]{:S(2)}) collective-permute-start(bf16[4,8,3456]{2,1,0:T(8,128)(2,1)S(1)} %shard_map.180.p0), channel_id=1, source_target_pairs={{0,16},{4,20},{8,24},{12,28},{16,0},{20,4},{24,8},{28,12},{1,17},{... | collective-permute-start | bytes 663560 | tf_op jit(solution)/shard_map/ppermute | solution.py:713
  15.4 8.4 %collective-permute-start.5 = (bf16[4,8,3456]{2,1,0:T(8,128)(2,1)S(1)}, bf16[4,8,3456]{2,1,0:T(8,128)(2,1)S(1)}, u32[]{:S(2)}, u32[]{:S(2)}) collective-permute-start(bf16[4,8,3456]{2,1,0:T(8,128)(2,1)S(1)} %shard_map.180.p0), channel_id=1, source_target_pairs={{0,8},{4,12},{8,0},{12,4},{16,24},{20,28},{24,16},{28,20},{1,9},{5... | collective-permute-start | bytes 663560 | tf_op jit(solution)/shard_map/ppermute | solution.py:713
  15.9 0.7 %copy-start.2 = (f32[4]{0:T(128)S(1)}, f32[4]{0:T(128)}, u32[]{:S(2)}) copy-start(f32[4]{0:T(128)} %scale_ref.1) | copy-start | bytes 52
  21.3 2.4 %collective-permute-start.7 = (bf16[4,8,3456]{2,1,0:T(8,128)(2,1)S(1)}, bf16[4,8,3456]{2,1,0:T(8,128)(2,1)S(1)}, u32[]{:S(2)}, u32[]{:S(2)}) collective-permute-start(bf16[4,8,3456]{2,1,0:T(8,128)(2,1)S(1)} %collective-permute-done.6.p3), channel_id=1, source_target_pairs={{0,4},{4,0},{8,12},{12,8},{16,20},{20,16},{24,28},{28,24},{1,5},{5... | collective-permute-start | bytes 663560 | tf_op jit(solution)/shard_map/ppermute | solution.py:713
  21.3 2.9 %collective-permute-start.9 = (bf16[4,8,3456]{2,1,0:T(8,128)(2,1)S(1)}, bf16[4,8,3456]{2,1,0:T(8,128)(2,1)S(1)}, u32[]{:S(2)}, u32[]{:S(2)}) collective-permute-start(bf16[4,8,3456]{2,1,0:T(8,128)(2,1)S(1)} %shard_map.180.p0), channel_id=1, source_target_pairs={{0,4},{4,0},{8,12},{12,8},{16,20},{20,16},{24,28},{28,24},{1,5},{5... | collective-permute-start | bytes 663560 | tf_op jit(solution)/shard_map/ppermute | solution.py:713
  23.8 1.5 %collective-permute-start.11 = (bf16[4,8,3456]{2,1,0:T(8,128)(2,1)S(1)}, bf16[4,8,3456]{2,1,0:T(8,128)(2,1)S(1)}, u32[]{:S(2)}, u32[]{:S(2)}) collective-permute-start(bf16[4,8,3456]{2,1,0:T(8,128)(2,1)S(1)} %collective-permute-done.8.p2), channel_id=1, source_target_pairs={{0,4},{4,0},{8,12},{12,8},{16,20},{20,16},{24,28},{28,24},{1,5},{5... | collective-permute-start | bytes 663560 | tf_op jit(solution)/shard_map/ppermute | solution.py:713
  23.8 1.8 %collective-permute-start.10 = (bf16[4,8,3456]{2,1,0:T(8,128)(2,1)S(1)}, bf16[4,8,3456]{2,1,0:T(8,128)(2,1)S(1)}, u32[]{:S(2)}, u32[]{:S(2)}) collective-permute-start(bf16[4,8,3456]{2,1,0:T(8,128)(2,1)S(1)} %collective-permute-done.5.p1), channel_id=1, source_target_pairs={{0,4},{4,0},{8,12},{12,8},{16,20},{20,16},{24,28},{28,24},{1,5},{5... | collective-permute-start | bytes 663560 | tf_op jit(solution)/shard_map/ppermute | solution.py:713
  30.1 3.9 %collective-permute-start.12 = (bf16[4,4,8,2560]{3,2,1,0:T(8,128)(2,1)S(1)}, bf16[4,4,8,2560]{3,2,1,0:T(8,128)(2,1)S(1)}, u32[]{:S(2)}, u32[]{:S(2)}) collective-permute-start(bf16[4,4,8,2560]{3,2,1,0:T(8,128)(2,1)S(1)} %get-tuple-element.104), channel_id=1, source_target_pairs={{0,4},{4,0},{8,12},{12,8},{16,20},{20,16},{24,28},{28,24},{1,5},{5... | collective-permute-start | bytes 1966088 | tf_op jit(solution)/shard_map/ppermute | solution.py:713
  33.6 1.9 %collective-permute-start.14 = (bf16[4,4,8,896]{3,2,1,0:T(8,128)(2,1)S(1)}, bf16[4,4,8,896]{3,2,1,0:T(8,128)(2,1)S(1)}, u32[]{:S(2)}, u32[]{:S(2)}) collective-permute-start(bf16[4,4,8,896]{3,2,1,0:T(8,128)(2,1)S(1)} %get-tuple-element.126), channel_id=1, source_target_pairs={{0,4},{4,0},{8,12},{12,8},{16,20},{20,16},{24,28},{28,24},{1,5},{5... | collective-permute-start | bytes 688136 | tf_op jit(solution)/shard_map/ppermute | solution.py:713
  34.1 6.0 %collective-permute-start.13 = (bf16[4,8,2560]{2,1,0:T(8,128)(2,1)S(1)}, bf16[4,8,2560]{2,1,0:T(8,128)(2,1)S(1)}, u32[]{:S(2)}, u32[]{:S(2)}) collective-permute-start(bf16[4,8,2560]{2,1,0:T(8,128)(2,1)S(1)} %get-tuple-element.107), channel_id=1, source_target_pairs={{0,8},{4,20},{8,0},{12,28},{16,24},{20,4},{24,16},{28,12},{1,9},{5... | collective-permute-start | bytes 491528 | tf_op jit(solution)/shard_map/ppermute | solution.py:725
  35.5 4.6 %collective-permute-start.15 = (bf16[4,8,896]{2,1,0:T(8,128)(2,1)S(1)}, bf16[4,8,896]{2,1,0:T(8,128)(2,1)S(1)}, u32[]{:S(2)}, u32[]{:S(2)}) collective-permute-start(bf16[4,8,896]{2,1,0:T(8,128)(2,1)S(1)} %get-tuple-element.127), channel_id=1, source_target_pairs={{0,8},{4,20},{8,0},{12,28},{16,24},{20,4},{24,16},{28,12},{1,9},{5... | collective-permute-start | bytes 172040 | tf_op jit(solution)/shard_map/ppermute | solution.py:725
  36.5 9.6 %collective-permute-start.18 = (bf16[4,8,3456]{2,1,0:T(8,128)(2,1)S(1)}, bf16[4,8,3456]{2,1,0:T(8,128)(2,1)S(1)}, u32[]{:S(2)}, u32[]{:S(2)}) collective-permute-start(bf16[4,8,3456]{2,1,0:T(8,128)(2,1)S(1)} %shard_map.187), channel_id=1, source_target_pairs={{0,8},{4,20},{8,0},{12,28},{16,24},{20,4},{24,16},{28,12},{1,9},{5... | collective-permute-start | bytes 663560 | tf_op jit(solution)/shard_map/ppermute | solution.py:725
  40.1 6.0 %collective-permute-start.16 = (bf16[4,8,2560]{2,1,0:T(8,128)(2,1)S(1)}, bf16[4,8,2560]{2,1,0:T(8,128)(2,1)S(1)}, u32[]{:S(2)}, u32[]{:S(2)}) collective-permute-start(bf16[4,8,2560]{2,1,0:T(8,128)(2,1)S(1)} %shard_map.185), channel_id=1, source_target_pairs={{0,16},{4,12},{8,24},{12,4},{16,0},{20,28},{24,8},{28,20},{1,17},{... | collective-permute-start | bytes 491528 | tf_op jit(solution)/shard_map/ppermute | solution.py:722
  41.5 4.6 %collective-permute-start.17 = (bf16[4,8,896]{2,1,0:T(8,128)(2,1)S(1)}, bf16[4,8,896]{2,1,0:T(8,128)(2,1)S(1)}, u32[]{:S(2)}, u32[]{:S(2)}) collective-permute-start(bf16[4,8,896]{2,1,0:T(8,128)(2,1)S(1)} %shard_map.186), channel_id=1, source_target_pairs={{0,16},{4,12},{8,24},{12,4},{16,0},{20,28},{24,8},{28,20},{1,17},{... | collective-permute-start | bytes 172040 | tf_op jit(solution)/shard_map/ppermute | solution.py:722
  42.9 9.0 %collective-permute-start.19 = (bf16[192,256]{1,0:T(8,128)(2,1)S(1)}, bf16[192,256]{1,0:T(8,128)(2,1)S(1)}, u32[]{:S(2)}, u32[]{:S(2)}) collective-permute-start(bf16[192,256]{1,0:T(8,128)(2,1)S(1)} %get-tuple-element.148), channel_id=1, source_target_pairs={{0,4},{4,0},{8,12},{12,8},{16,20},{20,16},{24,28},{28,24},{1,5},{5... | collective-permute-start | bytes 294920 | tf_op jit(solution)/shard_map/ppermute | solution.py:713
  42.9 8.9 %collective-permute-start.20 = (bf16[192,256]{1,0:T(8,128)(2,1)S(1)}, bf16[192,256]{1,0:T(8,128)(2,1)S(1)}, u32[]{:S(2)}, u32[]{:S(2)}) collective-permute-start(bf16[192,256]{1,0:T(8,128)(2,1)S(1)} %get-tuple-element.149), channel_id=1, source_target_pairs={{0,28},{4,8},{8,4},{12,16},{16,12},{20,24},{24,20},{28,0},{1,29},{... | collective-permute-start | bytes 294920 | tf_op jit(solution)/shard_map/ppermute | solution.py:778
  46.3 6.6 %collective-permute-start.21 = (bf16[8,3456]{1,0:T(8,128)(2,1)S(1)}, bf16[8,3456]{1,0:T(8,128)(2,1)S(1)}, u32[]{:S(2)}, u32[]{:S(2)}) collective-permute-start(bf16[8,3456]{1,0:T(8,128)(2,1)S(1)} %get-tuple-element.153), channel_id=1, source_target_pairs={{0,3},{1,2},{2,1},{3,0},{4,7},{5,6},{6,5},{7,4},{8,11},{9,10},{10,... | collective-permute-start | bytes 165896 | tf_op jit(solution)/shard_map/ppermute | solution.py:713
  49.2 5.5 %collective-permute-start.22 = (bf16[8,3456]{1,0:T(8,128)(2,1)S(1)}, bf16[8,3456]{1,0:T(8,128)(2,1)S(1)}, u32[]{:S(2)}, u32[]{:S(2)}) collective-permute-start(bf16[8,3456]{1,0:T(8,128)(2,1)S(1)} %get-tuple-element.154), channel_id=1, source_target_pairs={{0,2},{1,3},{2,0},{3,1},{4,6},{5,7},{6,4},{7,5},{8,10},{9,11},{10,... | collective-permute-start | bytes 165896 | tf_op jit(solution)/shard_map/ppermute | solution.py:713
  49.5 5.2 %collective-permute-start.23 = (bf16[8,3456]{1,0:T(8,128)(2,1)S(1)}, bf16[8,3456]{1,0:T(8,128)(2,1)S(1)}, u32[]{:S(2)}, u32[]{:S(2)}) collective-permute-start(bf16[8,3456]{1,0:T(8,128)(2,1)S(1)} %get-tuple-element.155), channel_id=1, source_target_pairs={{0,1},{1,0},{2,3},{3,2},{4,5},{5,4},{6,7},{7,6},{8,9},{9,8},{10,11... | collective-permute-start | bytes 165896 | tf_op jit(solution)/shard_map/ppermute | solution.py:713

commit v5 on v4

--- a/solution.py
+++ b/solution.py
@@ -163,7 +163,7 @@
 
 def pack_kernel(
     heads, per_canvas, place, cond_ref, qkv_ref, up_ref, out_ref, down_ref, attn_ref, feed_ref,
-    near_ref, far_ref, cond_own_ref,
+    near_ref, far_ref, both_ref, cond_own_ref,
 ):
     own = attn_ref.shape[0]
     canvases, total = cond_ref.shape
@@ -191,10 +191,9 @@
         turned_order(width, heads),
     ).astype(BF16)
     mine = place[0] == 0
-    for ref, tail in (
-        (near_ref, jnp.where(mine, tails[0], tails[1])),
-        (far_ref, jnp.where(mine, tails[1], tails[0])),
-    ):
+    near, far = jnp.where(mine, tails[0], tails[1]), jnp.where(mine, tails[1], tails[0])
+    both_ref[:, both_ref.shape[1] - 128 :] = far.astype(BF16)
+    for ref, tail in ((near_ref, near), (far_ref, far), (both_ref, near)):
         ref[:, :width], ref[:, width : 2 * width] = turned[:8], turned[8:]
         ref[:, 2 * width : qkv] = qkv_ref[:, 2 * width :]
         ref[:, qkv : qkv + 128] = tail.astype(BF16)
@@ -202,6 +201,13 @@
         for part in parts:
             ref[:, at : at + part.shape[1]] = part
             at += part.shape[1]
+
+
+def again_kernel(at, both_ref, near_ref, far_ref):
+    lanes = near_ref.shape[1]
+    near_ref[...] = both_ref[:, :lanes]
+    far_ref[...] = both_ref[:, :lanes]
+    far_ref[:, at : at + 128] = both_ref[:, lanes:]
 
 
 def line_kernel(order, place, p0, p1, p2, p3, line_ref):
@@ -326,7 +332,7 @@
 
 def attend_kernel(
     heads, root_ref, unit_ref, cos_ref, sine_ref, mask_ref, sums, w_ref,
-    query_ref, key_ref, value_ref, raised_ref, mixed_ref, inverse_ref, inverse_rows_ref, along_q_ref, length_q_ref, along_k_ref, length_k_ref,
+    query_ref, key_ref, value_ref, raised_ref, exact_ref, mixed_ref, inverse_ref, inverse_rows_ref, along_q_ref, length_q_ref, along_k_ref, length_k_ref,
     gain_ref, gain_col_ref,
 ):
     bands, count = mask_ref.shape[:2]
@@ -366,7 +372,9 @@
         span = slice(band * count, (band + 1) * count)
         query = query_ref[span, :].astype(F32)
         scores = mm_rt(stack_heads(query, heads), key_ref[start : start + 2 * count, :])
-        raised = jnp.exp(scores).astype(BF16) * jnp.concatenate([mask_ref[band]] * heads, axis=0)
+        exact = jnp.exp(scores)
+        exact_ref[band] = exact
+        raised = exact.astype(BF16) * jnp.concatenate([mask_ref[band]] * heads, axis=0)
         raised_ref[band] = raised
         value = value_ref[start : start + 2 * count, :]
         for pair in range(heads // 2):
@@ -518,7 +526,7 @@
 def forward_kernel(
     heads, place, root_ref, unit_ref, cos_ref, sine_ref, mask_ref, inputs_ref, cot_ref,
     p0, p1, p2, p3, p4, p5, p6, p7,
-    query_ref, key_ref, value_ref, raised_ref, inverse_rows_ref, mixed_ref, along_q_ref, length_q_ref, along_k_ref, length_k_ref,
+    query_ref, key_ref, value_ref, raised_ref, exact_ref, inverse_rows_ref, mixed_ref, along_q_ref, length_q_ref, along_k_ref, length_k_ref,
     gain_ref, gain_col_ref, w_ref, middle_ref, middle_grad_ref, shrunk_ref, d_mixed_ref, levels_ref, gain_grad_ref,
     w_down_ref, gated_ref, mine_ref, other_ref,
     inverse_ref, w_up_ref, w_out_ref, mixed_low_ref, normed_ref, d_exp_ref, branch_ref,
@@ -535,7 +543,7 @@
         store_rows(w_down_ref, start, jnp.concatenate(down, axis=1))
     attend_kernel(
         heads, root_ref, unit_ref, cos_ref, sine_ref, mask_ref, sums, w_ref,
-        query_ref, key_ref, value_ref, raised_ref, mixed_ref, inverse_ref, inverse_rows_ref,
+        query_ref, key_ref, value_ref, raised_ref, exact_ref, mixed_ref, inverse_ref, inverse_rows_ref,
         along_q_ref, length_q_ref, along_k_ref, length_k_ref, gain_ref, gain_col_ref,
     )
     feed_kernel(
@@ -549,7 +557,7 @@
 
 
 def backward_kernel(
-    heads, rows, place, root_ref, shrunk_ref, d_mixed_ref, levels_ref, raised_ref, inverse_rows_ref, query_ref, key_ref, value_ref,
+    heads, rows, place, root_ref, shrunk_ref, d_mixed_ref, levels_ref, raised_ref, exact_ref, inverse_rows_ref, query_ref, key_ref, value_ref,
     cos_ref, sine_ref, w_ref, gain_col_ref, unit_turned_ref, own_turned_ref, along_q_ref, length_q_ref,
     along_k_ref, length_k_ref, gain_grad_ref,
     d_query_ref, d_rest_ref, mine_ref, other_ref,
@@ -585,7 +593,7 @@
             )
         query = stack_heads(query_ref[span, :].astype(F32), heads)
         inverse = jnp.concatenate([inverse_rows_ref[band]] * (keys // 128), axis=1)
-        probs = jnp.where(raised > 0, jnp.exp(mm_rt(query, key_ref[whole, :])) * inverse, 0.0)
+        probs = jnp.where(raised > 0, exact_ref[band] * inverse, 0.0)
         d_scores = (probs * jnp.concatenate(parts, axis=0)).astype(BF16)
         d_key = mm_lt(d_scores, query)
         d_query = fold_heads(mm(d_scores, key_ref[whole, :]), heads)
@@ -727,22 +735,33 @@
     core_move = over("rows", 1)
 
     if direct:
-        near, far, cond_own = call(
+        near, far, both, cond_own = call(
             functools.partial(pack_kernel, heads, per_canvas),
             [
                 low(8, first_lanes + second_lanes),
                 low(8, first_lanes + second_lanes),
+                low(8, first_lanes + second_lanes + 128),
                 shape(own_cond, canvases),
             ],
             place=place,
             pin=False,
         )(conditioning, qkv_weight, up_weight, out_weight, down_weight, attn_cond_weight, feed_cond_weight)
         z_order = (3, 1, 2)
-        line = call(functools.partial(line_kernel, z_order), [low(group, 8, first_lanes + second_lanes)], place=place)(
-            near,
-            *[z_moves[k - 1](near if k // per_canvas == 0 else far) for k in z_order],
-        )[0]
-        mine = [line] + [move(line) for move in xy_moves]
+
+        def gather_line(near, far):
+            return call(
+                functools.partial(line_kernel, z_order), [low(group, 8, first_lanes + second_lanes)], place=place
+            )(near, *[z_moves[k - 1](near if k // per_canvas == 0 else far) for k in z_order])[0]
+
+        both = xy_moves[2](both)
+        line = gather_line(near, far)
+        across = gather_line(
+            *call(
+                functools.partial(again_kernel, 3 * width),
+                [low(8, first_lanes + second_lanes), low(8, first_lanes + second_lanes)],
+            )(both)
+        )
+        mine = [line, xy_moves[0](line), xy_moves[1](line), across]
     else:
         def parts_of(full):
             full = full.reshape(chips, 2, group, 8, full.shape[-1])
@@ -804,13 +823,10 @@
     )(attention_scale, features, cotangent, halo_swap, halo_beside, row_table, col_table, id_query, id_key)
     if direct:
         mine = mine[:1] + [lax.optimization_barrier((part, unit))[0] for part in mine[1:]]
-        far = core_move(mine[3])
-        for i in (1, 2):
-            mine[i], far = lax.optimization_barrier((mine[i], far))
-        parts = mine + [core_move(part) for part in mine[:3]] + [far]
+        parts = mine + [core_move(part) for part in mine]
 
     (
-        query, key, value, raised, inverse_rows, mixed, along_q, length_q, along_k, length_k, gain, gain_col, w_qkv,
+        query, key, value, raised, exact, inverse_rows, mixed, along_q, length_q, along_k, length_k, gain, gain_col, w_qkv,
         middle, middle_grad, shrunk, d_mixed, levels, gain_grad, w_down, gated, mine_second, other_second,
     ) = call(
         functools.partial(forward_kernel, heads),
@@ -819,6 +835,7 @@
             low(2 * tokens, width),
             low(2 * tokens, width),
             low(bands, heads * count, 2 * count),
+            shape(bands, heads * count, 2 * count),
             shape(bands, heads * count, 128),
             shape(tokens, width),
             shape(tokens, width),
@@ -862,7 +879,7 @@
         place=place,
         flops=1,
     )(
-        root, shrunk, d_mixed, levels, raised, inverse_rows, query, key, value, cos, sine, w_qkv, gain_col, unit_turned, own_turned,
+        root, shrunk, d_mixed, levels, raised, exact, inverse_rows, query, key, value, cos, sine, w_qkv, gain_col, unit_turned, own_turned,
         along_q, length_q, along_k, length_k, gain_grad,
     )
 

time: 55.7 us -> 55.3 us (level)
  starting transfers between devices: 25 us -> 27 us
  local copies, waits for them, and re-layouts: 1.76 us -> 0.4 us
  waiting for transfers between devices: 13.4 us -> 12.4 us
    ppermute x17 -> x20, starting transfers between devices: 15.8 us -> 21.2 us  [over(): lax.ppermute(value, axis, [(i, i ^ by) for i in range(size_of)])]
    ppermute x2, starting transfers between devices: 3.54 us -> 1.09 us  [beside_move(): return lax.ppermute(value, 'rows', beside_pairs)]
    ppermute x17 -> x20, waiting for transfers between devices: 10 us -> 7.6 us  [over(): lax.ppermute(value, axis, [(i, i ^ by) for i in range(size_of)])]
    unnamed x8, local copies, waits for them, and re-layouts: 1.39 us -> 0.02 us
    ppermute x2, waiting for transfers between devices: 1.04 us -> 2.17 us  [first_chip(): return lax.ppermute(value, 'rows', chip_pairs(0))]
    ppermute x3, starting transfers between devices: 3.5 us -> 2.55 us  [second_chip(): return lax.ppermute(value, 'rows', chip_pairs(1))]
    pallas_call x15 -> x17, Pallas kernels: 14 us -> 13.9 us  [run(): pl.pallas_call(kernel, out_shape=outs, in_specs=[pl.BlockSpec(memory_spac...]
  transfers between devices with their start and end apart: 24 -> 27, of which waited for: 8 -> 10; matrix products, arithmetic and copies ran while one was open for 1% -> 1% of each run, Pallas kernels for 14% -> 14%
where the time goes in v5:
time: 55.3 us; the launch traced here: 55 us
  starting transfers between devices  27 us (49%)
  Pallas kernels  13.9 us (25%)
  waiting for transfers between devices  12.4 us (22%)
  between operations  0.92 us (2%)
    ppermute x20, starting transfers between devices, over(): lax.ppermute(value, axis, [(i, i ^ by) for i in range(size_of)])  21.2 us
    pallas_call x17, Pallas kernels, run(): pl.pallas_call(kernel, out_shape=outs, in_specs=[pl.BlockSpec(memory_spac...  13.9 us
    ppermute x20, waiting for transfers between devices, over(): lax.ppermute(value, axis, [(i, i ^ by) for i in range(size_of)])  7.6 us
    ppermute x3, waiting for transfers between devices, second_chip(): return lax.ppermute(value, 'rows', chip_pairs(1))  2.61 us
    ppermute x3, starting transfers between devices, second_chip(): return lax.ppermute(value, 'rows', chip_pairs(1))  2.55 us
    ppermute x2, waiting for transfers between devices, first_chip(): return lax.ppermute(value, 'rows', chip_pairs(0))  2.17 us
    ppermute x2, starting transfers between devices, first_chip(): return lax.ppermute(value, 'rows', chip_pairs(0))  2.16 us
  transfers between devices with their start and end apart: 27, of which 10 were waited for; matrix products, arithmetic and copies ran while one was open for 1% of the time, Pallas kernels for 14%

profile of v5, /device:TPU:0, one launch (start us, length us, event | category | flops | bytes accessed | tf_op | source)
XLA Modules:
  0.0 55.0 jit_solution(9699063565210046106)
XLA Ops:
  0.7 1.1 %shard_map.179 = (bf16[8,3456]{1,0:T(8,128)(2,1)S(1)}, bf16[8,3456]{1,0:T(8,128)(2,1)S(1)}, bf16[8,3584]{1,0:T(8,128)(2,1)S(1)}, f32[24,2]{1,0:T(8,128)S(1)}) custom-call(bf16[2,768]{1,0:T(2,128)(2,1)} %cond_ref.1, bf16[8,768]{1,0:T(8,128)(2,1)} %qkv_ref.1, bf16[8,1536]{1,0:T(8,128)(2,1)} %up_ref.1, bf16[8,256]{1,0:T(8,128)(2,1)} %out_ref.1, ...), custom_call_target="tpu_custom_call" | custom-call | flops 1000000000 | bytes 4000000 | tf_op jit(solution)/shard_map/pallas_call | solution.py:640
  1.8 4.1 %collective-permute-start.4 = (bf16[8,3456]{1,0:T(8,128)(2,1)S(1)}, bf16[8,3456]{1,0:T(8,128)(2,1)S(1)}, u32[]{:S(2)}, u32[]{:S(2)}) collective-permute-start(bf16[8,3456]{1,0:T(8,128)(2,1)S(1)} %get-tuple-element.94), channel_id=1, source_target_pairs={{0,2},{1,3},{2,0},{3,1},{4,6},{5,7},{6,4},{7,5},{8,10},{9,11},{10,... | collective-permute-start | bytes 165896 | tf_op jit(solution)/shard_map/ppermute | solution.py:721
  5.9 1.3 %collective-permute-start.2 = (bf16[8,3456]{1,0:T(8,128)(2,1)S(1)}, bf16[8,3456]{1,0:T(8,128)(2,1)S(1)}, u32[]{:S(2)}, u32[]{:S(2)}) collective-permute-start(bf16[8,3456]{1,0:T(8,128)(2,1)S(1)} %get-tuple-element.94), channel_id=1, source_target_pairs={{0,3},{1,2},{2,1},{3,0},{4,7},{5,6},{6,5},{7,4},{8,11},{9,10},{10,... | collective-permute-start | bytes 165896 | tf_op jit(solution)/shard_map/ppermute | solution.py:721
  7.2 0.2 collective-permute-start.3
  7.4 2.4 %collective-permute-start.7 = (bf16[8,3584]{1,0:T(8,128)(2,1)S(1)}, bf16[8,3584]{1,0:T(8,128)(2,1)S(1)}, u32[]{:S(2)}, u32[]{:S(2)}) collective-permute-start(bf16[8,3584]{1,0:T(8,128)(2,1)S(1)} %get-tuple-element.97), channel_id=1, source_target_pairs={{0,24},{4,28},{8,16},{12,20},{16,8},{20,12},{24,0},{28,4},{1,25},{... | collective-permute-start | bytes 172040 | tf_op jit(solution)/shard_map/ppermute | solution.py:721
  10.1 0.1 slice.11
  10.2 0.1 fusion.3
  10.3 0.2 fusion.1
  10.6 0.1 copy.20
  10.7 0.1 broadcast_in_dim.49
  10.7 0.1 reshape.363.id_key_ref
  10.8 1.1 %collective-permute-done.3.p2 = bf16[8,3456]{1,0:T(8,128)(2,1)S(1)} collective-permute-done((bf16[8,3456]{1,0:T(8,128)(2,1)S(1)}, bf16[8,3456]{1,0:T(8,128)(2,1)S(1)}, u32[]{:S(2)}, u32[]{:S(2)}) %collective-permute-start.3) | collective-permute-done | bytes 55328 | tf_op jit(solution)/shard_map/ppermute | solution.py:721
  12.0 1.6 %collective-permute-start.6 = (bf16[4,8,3456]{2,1,0:T(8,128)(2,1)S(1)}, bf16[4,8,3456]{2,1,0:T(8,128)(2,1)S(1)}, u32[]{:S(2)}, u32[]{:S(2)}) collective-permute-start(bf16[4,8,3456]{2,1,0:T(8,128)(2,1)S(1)} %shard_map.180.p0), channel_id=1, source_target_pairs={{0,16},{4,20},{8,24},{12,28},{16,0},{20,4},{24,8},{28,12},{1,17},{... | collective-permute-start | bytes 663560 | tf_op jit(solution)/shard_map/ppermute | solution.py:721
  13.6 1.5 %collective-permute-start.5 = (bf16[4,8,3456]{2,1,0:T(8,128)(2,1)S(1)}, bf16[4,8,3456]{2,1,0:T(8,128)(2,1)S(1)}, u32[]{:S(2)}, u32[]{:S(2)}) collective-permute-start(bf16[4,8,3456]{2,1,0:T(8,128)(2,1)S(1)} %shard_map.180.p0), channel_id=1, source_target_pairs={{0,8},{4,12},{8,0},{12,4},{16,24},{20,28},{24,16},{28,20},{1,9},{5... | collective-permute-start | bytes 663560 | tf_op jit(solution)/shard_map/ppermute | solution.py:721
  15.1 2.4 %collective-permute-start.10 = (bf16[8,3456]{1,0:T(8,128)(2,1)S(1)}, bf16[8,3456]{1,0:T(8,128)(2,1)S(1)}, u32[]{:S(2)}, u32[]{:S(2)}) collective-permute-start(bf16[8,3456]{1,0:T(8,128)(2,1)S(1)} %get-tuple-element.99), channel_id=1, source_target_pairs={{0,2},{1,3},{2,0},{3,1},{4,6},{5,7},{6,4},{7,5},{8,10},{9,11},{10,... | collective-permute-start | bytes 165896 | tf_op jit(solution)/shard_map/ppermute | solution.py:721
  17.5 1.3 %collective-permute-start.8 = (bf16[8,3456]{1,0:T(8,128)(2,1)S(1)}, bf16[8,3456]{1,0:T(8,128)(2,1)S(1)}, u32[]{:S(2)}, u32[]{:S(2)}) collective-permute-start(bf16[8,3456]{1,0:T(8,128)(2,1)S(1)} %get-tuple-element.99), channel_id=1, source_target_pairs={{0,3},{1,2},{2,1},{3,0},{4,7},{5,6},{6,5},{7,4},{8,11},{9,10},{10,... | collective-permute-start | bytes 165896 | tf_op jit(solution)/shard_map/ppermute | solution.py:721
  18.9 1.3 %shard_map.178 = (f32[1024,256]{1,0:T(8,128)S(1)}, bf16[256,1024]{1,0:T(8,128)(2,1)S(1)}, bf16[256,512]{1,0:T(8,128)(2,1)S(1)}, f32[1024,128]{1,0:T(8,128)S(1)},...) custom-call(f32[4]{0:T(128)S(1)} %copy-done.2, ...), custom_call_target="tpu_custom_call" | custom-call | flops 1000000000 | bytes 4000000 | tf_op jit(solution)/shard_map/pallas_call | solution.py:640
  20.2 3.4 %collective-permute-done.9.p2 = bf16[8,3456]{1,0:T(8,128)(2,1)S(1)} collective-permute-done((bf16[8,3456]{1,0:T(8,128)(2,1)S(1)}, bf16[8,3456]{1,0:T(8,128)(2,1)S(1)}, u32[]{:S(2)}, u32[]{:S(2)}) %collective-permute-start.9) | collective-permute-done | bytes 55328 | tf_op jit(solution)/shard_map/ppermute | solution.py:721
  23.7 0.6 %collective-permute-start.14 = (bf16[4,8,3456]{2,1,0:T(8,128)(2,1)S(1)}, bf16[4,8,3456]{2,1,0:T(8,128)(2,1)S(1)}, u32[]{:S(2)}, u32[]{:S(2)}) collective-permute-start(bf16[4,8,3456]{2,1,0:T(8,128)(2,1)S(1)} %shard_map.182.p3), channel_id=1, source_target_pairs={{0,4},{4,0},{8,12},{12,8},{16,20},{20,16},{24,28},{28,24},{1,5},{5... | collective-permute-start | bytes 663560 | tf_op jit(solution)/shard_map/ppermute | solution.py:721
  24.2 0.1 collective-permute-start.12
  24.3 0.4 collective-permute-start.13
  24.7 0.3 collective-permute-done.11.p4
  25.1 0.3 collective-permute-done.14.p7
  25.4 0.3 collective-permute-done.12.p5
  25.7 0.3 collective-permute-done.13.p6
  26.0 4.5 %shard_map.183 = (bf16[512,256]{1,0:T(8,128)(2,1)S(1)}, bf16[1024,256]{1,0:T(8,128)(2,1)S(1)}, bf16[1024,256]{1,0:T(8,128)(2,1)S(1)}, bf16[4,512,256]{2,1,0:T(8,...) custom-call(f32[1,128]{1,0:T(1,128)S(1)} %get-tuple-element.86.root_, ...), custom_call_target="tpu_custom_call" | custom-call | flops 1000000000 | bytes 4000000 | tf_op jit(solution)/shard_map/pallas_call | solution.py:640
  30.6 0.4 collective-permute-start.15
  31.0 3.1 %shard_map.185 = (bf16[512,256]{1,0:T(8,128)(2,1)S(1)}, bf16[1024,512]{1,0:T(8,128)(2,1)S(1)}, bf16[4,4,8,896]{3,2,1,0:T(8,128)(2,1)S(1)}, bf16[4,4,8,896]{3,2,1,0:T(8,128)(2,1)S(1)}) custom-call(f32[1,128]{1,0:T(1,128)S(1)} %get-tuple-element.86.root_ref, bf16[512,256]{1,0:T(8,128)(2,1)S(1)} %get-tuple-element.107.shrunk_ref, ...), custom_call_target="tpu_custom_call" | custom-call | flops 1 | bytes 1 | tf_op jit(solution)/shard_map/pallas_call | solution.py:640
  34.0 0.3 collective-permute-start.17
  34.3 0.2 shard_map.184
  34.4 0.4 collective-permute-start.16
  34.8 0.7 %collective-permute-done.17.got_ref = bf16[4,4,8,896]{3,2,1,0:T(8,128)(2,1)S(1)} collective-permute-done((bf16[4,4,8,896]{3,2,1,0:T(8,128)(2,1)S(1)}, bf16[4,4,8,896]{3,2,1,0:T(8,128)(2,1)S(1)}, u32[]{:S(2)}, u32[]{:S(2)}) %collective-permute-start.17) | collective-permute-done | bytes 229408 | tf_op jit(solution)/shard_map/ppermute | solution.py:721
  35.6 0.1 shard_map.186
  35.7 1.0 %collective-permute-start.18 = (bf16[4,8,896]{2,1,0:T(8,128)(2,1)S(1)}, bf16[4,8,896]{2,1,0:T(8,128)(2,1)S(1)}, u32[]{:S(2)}, u32[]{:S(2)}) collective-permute-start(bf16[4,8,896]{2,1,0:T(8,128)(2,1)S(1)} %get-tuple-element.127), channel_id=1, source_target_pairs={{0,8},{4,20},{8,0},{12,28},{16,24},{20,4},{24,16},{28,12},{1,9},{5... | collective-permute-start | bytes 172040 | tf_op jit(solution)/shard_map/ppermute | solution.py:733
  36.7 1.1 %collective-permute-start.21 = (bf16[4,8,3456]{2,1,0:T(8,128)(2,1)S(1)}, bf16[4,8,3456]{2,1,0:T(8,128)(2,1)S(1)}, u32[]{:S(2)}, u32[]{:S(2)}) collective-permute-start(bf16[4,8,3456]{2,1,0:T(8,128)(2,1)S(1)} %shard_map.189), channel_id=1, source_target_pairs={{0,8},{4,20},{8,0},{12,28},{16,24},{20,4},{24,16},{28,12},{1,9},{5... | collective-permute-start | bytes 663560 | tf_op jit(solution)/shard_map/ppermute | solution.py:733
  37.8 2.6 %collective-permute-done.18.two_ref = bf16[4,8,896]{2,1,0:T(8,128)(2,1)S(1)} collective-permute-done((bf16[4,8,896]{2,1,0:T(8,128)(2,1)S(1)}, bf16[4,8,896]{2,1,0:T(8,128)(2,1)S(1)}, u32[]{:S(2)}, u32[]{:S(2)}) %collective-permute-start.18) | collective-permute-done | bytes 57376 | tf_op jit(solution)/shard_map/ppermute | solution.py:733
  40.5 0.6 %collective-permute-start.19 = (bf16[4,8,2560]{2,1,0:T(8,128)(2,1)S(1)}, bf16[4,8,2560]{2,1,0:T(8,128)(2,1)S(1)}, u32[]{:S(2)}, u32[]{:S(2)}) collective-permute-start(bf16[4,8,2560]{2,1,0:T(8,128)(2,1)S(1)} %shard_map.187), channel_id=1, source_target_pairs={{0,16},{4,12},{8,24},{12,4},{16,0},{20,28},{24,8},{28,20},{1,17},{... | collective-permute-start | bytes 491528 | tf_op jit(solution)/shard_map/ppermute | solution.py:730
  41.1 1.6 %collective-permute-start.20 = (bf16[4,8,896]{2,1,0:T(8,128)(2,1)S(1)}, bf16[4,8,896]{2,1,0:T(8,128)(2,1)S(1)}, u32[]{:S(2)}, u32[]{:S(2)}) collective-permute-start(bf16[4,8,896]{2,1,0:T(8,128)(2,1)S(1)} %shard_map.188), channel_id=1, source_target_pairs={{0,16},{4,12},{8,24},{12,4},{16,0},{20,28},{24,8},{28,20},{1,17},{... | collective-permute-start | bytes 172040 | tf_op jit(solution)/shard_map/ppermute | solution.py:730
  42.7 0.5 shard_map.191
  43.3 1.0 %collective-permute-start.23 = (bf16[192,256]{1,0:T(8,128)(2,1)S(1)}, bf16[192,256]{1,0:T(8,128)(2,1)S(1)}, u32[]{:S(2)}, u32[]{:S(2)}) collective-permute-start(bf16[192,256]{1,0:T(8,128)(2,1)S(1)} %get-tuple-element.149), channel_id=1, source_target_pairs={{0,28},{4,8},{8,4},{12,16},{16,12},{20,24},{24,20},{28,0},{1,29},{... | collective-permute-start | bytes 294920 | tf_op jit(solution)/shard_map/ppermute | solution.py:797
  44.3 2.2 %collective-permute-done.20.q1 = bf16[4,8,896]{2,1,0:T(8,128)(2,1)S(1)} collective-permute-done((bf16[4,8,896]{2,1,0:T(8,128)(2,1)S(1)}, bf16[4,8,896]{2,1,0:T(8,128)(2,1)S(1)}, u32[]{:S(2)}, u32[]{:S(2)}) %collective-permute-start.20) | collective-permute-done | bytes 57376 | tf_op jit(solution)/shard_map/ppermute | solution.py:730
  46.5 0.1 shard_map.190
  46.6 2.1 %collective-permute-start.24 = (bf16[8,3456]{1,0:T(8,128)(2,1)S(1)}, bf16[8,3456]{1,0:T(8,128)(2,1)S(1)}, u32[]{:S(2)}, u32[]{:S(2)}) collective-permute-start(bf16[8,3456]{1,0:T(8,128)(2,1)S(1)} %get-tuple-element.153), channel_id=1, source_target_pairs={{0,3},{1,2},{2,1},{3,0},{4,7},{5,6},{6,5},{7,4},{8,11},{9,10},{10,... | collective-permute-start | bytes 165896 | tf_op jit(solution)/shard_map/ppermute | solution.py:721
  48.7 2.4 %collective-permute-start.26 = (bf16[8,3456]{1,0:T(8,128)(2,1)S(1)}, bf16[8,3456]{1,0:T(8,128)(2,1)S(1)}, u32[]{:S(2)}, u32[]{:S(2)}) collective-permute-start(bf16[8,3456]{1,0:T(8,128)(2,1)S(1)} %get-tuple-element.155), channel_id=1, source_target_pairs={{0,1},{1,0},{2,3},{3,2},{4,5},{5,4},{6,7},{7,6},{8,9},{9,8},{10,11... | collective-permute-start | bytes 165896 | tf_op jit(solution)/shard_map/ppermute | solution.py:721
  51.1 1.1 %shard_map.192 = bf16[8,64,256]{2,1,0:T(8,128)(2,1)} custom-call(f32[512,256]{1,0:T(8,128)S(1)} %get-tuple-element.101.middle_ref, bf16[512,768]{1,0:T(8,128)(2,1)S(1)} %get-tuple-element.144.gated_ref, bf16[768,256]{1,0:T(8,128)(2,1)S(1)} %get-tuple-element.145.w_down_ref), custom_call_target="tpu_custom_call" | custom-call | flops 1000000000 | bytes 4000000 | tf_op jit(solution)/shard_map/pallas_call | solution.py:640
  52.2 1.1 %shard_map.193 = f32[8,64,256]{2,1,0:T(8,128)} custom-call(f32[512,256]{1,0:T(8,128)S(1)} %get-tuple-element.91.inputs_ref, f32[2,256]{1,0:T(2,128)S(1)} %get-tuple-element.146.gain_ref, f32[512,256]{1,0:T(8,128)S(1)} %get-tuple-element.147.own_ref, bf16[192,256]{1,0:T(8,128)(2,1)S(1)} %collective-permute-done.22.rim_swap_ref, ...), custom_call_target="tpu_custom_call" | custom-call | flops 1000000000 | bytes 4000000 | tf_op jit(solution)/shard_map/pallas_call | solution.py:640
  53.3 1.0 %collective-permute-done.25.two_ref = bf16[8,3456]{1,0:T(8,128)(2,1)S(1)} collective-permute-done((bf16[8,3456]{1,0:T(8,128)(2,1)S(1)}, bf16[8,3456]{1,0:T(8,128)(2,1)S(1)}, u32[]{:S(2)}, u32[]{:S(2)}) %collective-permute-start.25) | collective-permute-done | bytes 55328 | tf_op jit(solution)/shard_map/ppermute | solution.py:721
  54.3 0.7 %shard_map.194 = (f32[8,768]{1,0:T(8,128)}, f32[8,256]{1,0:T(8,128)}, f32[8,1536]{1,0:T(8,128)}, f32[24,256]{1,0:T(8,128)}, f32[24,256]{1,0:T(8,128)}, /*index=5*/f32[24,256]{1,0:T(8,128)}, f32[4]{0:T(128)}) custom-call(f32[24,2]{1,0:T(8,128)S(1)} %get-tuple-element.151.cond_ref, f32[8,3456]{1,0:T(8,128)S(1)} %get-tuple-element.152.own_ref, ...), custom_call_target="tpu_custom_call" | custom-call | flops 1000000000 | bytes 4000000 | tf_op jit(solution)/shard_map/pallas_call | solution.py:640
  (48 shorter events, 0.5 us)
Async XLA Ops:
  0.6 9.2 %copy-start = (bf16[8,64,256]{2,1,0:T(8,128)(2,1)S(1)}, bf16[8,64,256]{2,1,0:T(8,128)(2,1)}, u32[]{:S(2)}) copy-start(bf16[8,64,256]{2,1,0:T(8,128)(2,1)} %feat_ref.1) | copy-start | bytes 786436
  0.7 9.4 %copy-start.3 = (s32[64,64]{1,0:T(8,128)S(1)}, s32[64,64]{1,0:T(8,128)}, u32[]{:S(2)}) copy-start(s32[64,64]{1,0:T(8,128)} %param.12) | copy-start | bytes 49156
  1.8 10.2 %collective-permute-start.4 = (bf16[8,3456]{1,0:T(8,128)(2,1)S(1)}, bf16[8,3456]{1,0:T(8,128)(2,1)S(1)}, u32[]{:S(2)}, u32[]{:S(2)}) collective-permute-start(bf16[8,3456]{1,0:T(8,128)(2,1)S(1)} %get-tuple-element.94), channel_id=1, source_target_pairs={{0,2},{1,3},{2,0},{3,1},{4,6},{5,7},{6,4},{7,5},{8,10},{9,11},{10,... | collective-permute-start | bytes 165896 | tf_op jit(solution)/shard_map/ppermute | solution.py:721
  5.9 6.1 %collective-permute-start.2 = (bf16[8,3456]{1,0:T(8,128)(2,1)S(1)}, bf16[8,3456]{1,0:T(8,128)(2,1)S(1)}, u32[]{:S(2)}, u32[]{:S(2)}) collective-permute-start(bf16[8,3456]{1,0:T(8,128)(2,1)S(1)} %get-tuple-element.94), channel_id=1, source_target_pairs={{0,3},{1,2},{2,1},{3,0},{4,7},{5,6},{6,5},{7,4},{8,11},{9,10},{10,... | collective-permute-start | bytes 165896 | tf_op jit(solution)/shard_map/ppermute | solution.py:721
  7.2 4.7 %collective-permute-start.3 = (bf16[8,3456]{1,0:T(8,128)(2,1)S(1)}, bf16[8,3456]{1,0:T(8,128)(2,1)S(1)}, u32[]{:S(2)}, u32[]{:S(2)}) collective-permute-start(bf16[8,3456]{1,0:T(8,128)(2,1)S(1)} %get-tuple-element.93.p0), channel_id=1, source_target_pairs={{0,1},{1,0},{2,3},{3,2},{4,5},{5,4},{6,7},{7,6},{8,9},{9,8},{10,11... | collective-permute-start | bytes 165896 | tf_op jit(solution)/shard_map/ppermute | solution.py:721
  7.4 7.7 %collective-permute-start.7 = (bf16[8,3584]{1,0:T(8,128)(2,1)S(1)}, bf16[8,3584]{1,0:T(8,128)(2,1)S(1)}, u32[]{:S(2)}, u32[]{:S(2)}) collective-permute-start(bf16[8,3584]{1,0:T(8,128)(2,1)S(1)} %get-tuple-element.97), channel_id=1, source_target_pairs={{0,24},{4,28},{8,16},{12,20},{16,8},{20,12},{24,0},{28,4},{1,25},{... | collective-permute-start | bytes 172040 | tf_op jit(solution)/shard_map/ppermute | solution.py:721
  9.9 7.6 %collective-permute-start.1 = (bf16[3,64,256]{2,1,0:T(8,128)(2,1)S(1)}, bf16[3,64,256]{2,1,0:T(8,128)(2,1)S(1)}, u32[]{:S(2)}, u32[]{:S(2)}) collective-permute-start(bf16[3,64,256]{2,1,0:T(8,128)(2,1)S(1)} %get-tuple-element.163), channel_id=1, source_target_pairs={{0,28},{4,8},{8,4},{12,16},{16,12},{20,24},{24,20},{28,0},{1,29},{... | collective-permute-start | bytes 294920 | tf_op jit(solution)/shard_map/ppermute | solution.py:797
  12.0 6.9 %collective-permute-start = (bf16[3,64,256]{2,1,0:T(8,128)(2,1)S(1)}, bf16[3,64,256]{2,1,0:T(8,128)(2,1)S(1)}, u32[]{:S(2)}, u32[]{:S(2)}) collective-permute-start(bf16[3,64,256]{2,1,0:T(8,128)(2,1)S(1)} %get-tuple-element.164), channel_id=1, source_target_pairs={{0,4},{4,0},{8,12},{12,8},{16,20},{20,16},{24,28},{28,24},{1,5},{5... | collective-permute-start | bytes 294920 | tf_op jit(solution)/shard_map/ppermute | solution.py:721
  12.0 6.9 %copy-start.1 = (bf16[8,64,256]{2,1,0:T(8,128)(2,1)S(1)}, bf16[8,64,256]{2,1,0:T(8,128)(2,1)}, u32[]{:S(2)}) copy-start(bf16[8,64,256]{2,1,0:T(8,128)(2,1)} %cot_ref.1) | copy-start | bytes 786436
  12.0 6.9 %copy-start.2 = (f32[4]{0:T(128)S(1)}, f32[4]{0:T(128)}, u32[]{:S(2)}) copy-start(f32[4]{0:T(128)} %scale_ref.1) | copy-start | bytes 52
  12.0 12.2 %collective-permute-start.6 = (bf16[4,8,3456]{2,1,0:T(8,128)(2,1)S(1)}, bf16[4,8,3456]{2,1,0:T(8,128)(2,1)S(1)}, u32[]{:S(2)}, u32[]{:S(2)}) collective-permute-start(bf16[4,8,3456]{2,1,0:T(8,128)(2,1)S(1)} %shard_map.180.p0), channel_id=1, source_target_pairs={{0,16},{4,20},{8,24},{12,28},{16,0},{20,4},{24,8},{28,12},{1,17},{... | collective-permute-start | bytes 663560 | tf_op jit(solution)/shard_map/ppermute | solution.py:721
  13.6 10.6 %collective-permute-start.5 = (bf16[4,8,3456]{2,1,0:T(8,128)(2,1)S(1)}, bf16[4,8,3456]{2,1,0:T(8,128)(2,1)S(1)}, u32[]{:S(2)}, u32[]{:S(2)}) collective-permute-start(bf16[4,8,3456]{2,1,0:T(8,128)(2,1)S(1)} %shard_map.180.p0), channel_id=1, source_target_pairs={{0,8},{4,12},{8,0},{12,4},{16,24},{20,28},{24,16},{28,20},{1,9},{5... | collective-permute-start | bytes 663560 | tf_op jit(solution)/shard_map/ppermute | solution.py:721
  15.1 8.5 %collective-permute-start.10 = (bf16[8,3456]{1,0:T(8,128)(2,1)S(1)}, bf16[8,3456]{1,0:T(8,128)(2,1)S(1)}, u32[]{:S(2)}, u32[]{:S(2)}) collective-permute-start(bf16[8,3456]{1,0:T(8,128)(2,1)S(1)} %get-tuple-element.99), channel_id=1, source_target_pairs={{0,2},{1,3},{2,0},{3,1},{4,6},{5,7},{6,4},{7,5},{8,10},{9,11},{10,... | collective-permute-start | bytes 165896 | tf_op jit(solution)/shard_map/ppermute | solution.py:721
  17.5 6.1 %collective-permute-start.8 = (bf16[8,3456]{1,0:T(8,128)(2,1)S(1)}, bf16[8,3456]{1,0:T(8,128)(2,1)S(1)}, u32[]{:S(2)}, u32[]{:S(2)}) collective-permute-start(bf16[8,3456]{1,0:T(8,128)(2,1)S(1)} %get-tuple-element.99), channel_id=1, source_target_pairs={{0,3},{1,2},{2,1},{3,0},{4,7},{5,6},{6,5},{7,4},{8,11},{9,10},{10,... | collective-permute-start | bytes 165896 | tf_op jit(solution)/shard_map/ppermute | solution.py:721
  18.9 4.7 %collective-permute-start.9 = (bf16[8,3456]{1,0:T(8,128)(2,1)S(1)}, bf16[8,3456]{1,0:T(8,128)(2,1)S(1)}, u32[]{:S(2)}, u32[]{:S(2)}) collective-permute-start(bf16[8,3456]{1,0:T(8,128)(2,1)S(1)} %get-tuple-element.98.p0), channel_id=1, source_target_pairs={{0,1},{1,0},{2,3},{3,2},{4,5},{5,4},{6,7},{7,6},{8,9},{9,8},{10,11... | collective-permute-start | bytes 165896 | tf_op jit(solution)/shard_map/ppermute | solution.py:721
  23.6 1.5 %collective-permute-start.11 = (bf16[4,8,3456]{2,1,0:T(8,128)(2,1)S(1)}, bf16[4,8,3456]{2,1,0:T(8,128)(2,1)S(1)}, u32[]{:S(2)}, u32[]{:S(2)}) collective-permute-start(bf16[4,8,3456]{2,1,0:T(8,128)(2,1)S(1)} %shard_map.180.p0), channel_id=1, source_target_pairs={{0,4},{4,0},{8,12},{12,8},{16,20},{20,16},{24,28},{28,24},{1,5},{5... | collective-permute-start | bytes 663560 | tf_op jit(solution)/shard_map/ppermute | solution.py:721
  23.7 1.7 %collective-permute-start.14 = (bf16[4,8,3456]{2,1,0:T(8,128)(2,1)S(1)}, bf16[4,8,3456]{2,1,0:T(8,128)(2,1)S(1)}, u32[]{:S(2)}, u32[]{:S(2)}) collective-permute-start(bf16[4,8,3456]{2,1,0:T(8,128)(2,1)S(1)} %shard_map.182.p3), channel_id=1, source_target_pairs={{0,4},{4,0},{8,12},{12,8},{16,20},{20,16},{24,28},{28,24},{1,5},{5... | collective-permute-start | bytes 663560 | tf_op jit(solution)/shard_map/ppermute | solution.py:721
  24.2 1.5 %collective-permute-start.12 = (bf16[4,8,3456]{2,1,0:T(8,128)(2,1)S(1)}, bf16[4,8,3456]{2,1,0:T(8,128)(2,1)S(1)}, u32[]{:S(2)}, u32[]{:S(2)}) collective-permute-start(bf16[4,8,3456]{2,1,0:T(8,128)(2,1)S(1)} %collective-permute-done.5.p1), channel_id=1, source_target_pairs={{0,4},{4,0},{8,12},{12,8},{16,20},{20,16},{24,28},{28,24},{1,5},{5... | collective-permute-start | bytes 663560 | tf_op jit(solution)/shard_map/ppermute | solution.py:721
  24.3 1.7 %collective-permute-start.13 = (bf16[4,8,3456]{2,1,0:T(8,128)(2,1)S(1)}, bf16[4,8,3456]{2,1,0:T(8,128)(2,1)S(1)}, u32[]{:S(2)}, u32[]{:S(2)}) collective-permute-start(bf16[4,8,3456]{2,1,0:T(8,128)(2,1)S(1)} %collective-permute-done.6.p2), channel_id=1, source_target_pairs={{0,4},{4,0},{8,12},{12,8},{16,20},{20,16},{24,28},{28,24},{1,5},{5... | collective-permute-start | bytes 663560 | tf_op jit(solution)/shard_map/ppermute | solution.py:721
  30.6 3.7 %collective-permute-start.15 = (bf16[4,4,8,2560]{3,2,1,0:T(8,128)(2,1)S(1)}, bf16[4,4,8,2560]{3,2,1,0:T(8,128)(2,1)S(1)}, u32[]{:S(2)}, u32[]{:S(2)}) collective-permute-start(bf16[4,4,8,2560]{3,2,1,0:T(8,128)(2,1)S(1)} %get-tuple-element.103), channel_id=1, source_target_pairs={{0,4},{4,0},{8,12},{12,8},{16,20},{20,16},{24,28},{28,24},{1,5},{5... | collective-permute-start | bytes 1966088 | tf_op jit(solution)/shard_map/ppermute | solution.py:721
  34.0 1.6 %collective-permute-start.17 = (bf16[4,4,8,896]{3,2,1,0:T(8,128)(2,1)S(1)}, bf16[4,4,8,896]{3,2,1,0:T(8,128)(2,1)S(1)}, u32[]{:S(2)}, u32[]{:S(2)}) collective-permute-start(bf16[4,4,8,896]{3,2,1,0:T(8,128)(2,1)S(1)} %get-tuple-element.126), channel_id=1, source_target_pairs={{0,4},{4,0},{8,12},{12,8},{16,20},{20,16},{24,28},{28,24},{1,5},{5... | collective-permute-start | bytes 688136 | tf_op jit(solution)/shard_map/ppermute | solution.py:721
  34.4 6.0 %collective-permute-start.16 = (bf16[4,8,2560]{2,1,0:T(8,128)(2,1)S(1)}, bf16[4,8,2560]{2,1,0:T(8,128)(2,1)S(1)}, u32[]{:S(2)}, u32[]{:S(2)}) collective-permute-start(bf16[4,8,2560]{2,1,0:T(8,128)(2,1)S(1)} %get-tuple-element.106), channel_id=1, source_target_pairs={{0,8},{4,20},{8,0},{12,28},{16,24},{20,4},{24,16},{28,12},{1,9},{5... | collective-permute-start | bytes 491528 | tf_op jit(solution)/shard_map/ppermute | solution.py:733
  35.7 4.8 %collective-permute-start.18 = (bf16[4,8,896]{2,1,0:T(8,128)(2,1)S(1)}, bf16[4,8,896]{2,1,0:T(8,128)(2,1)S(1)}, u32[]{:S(2)}, u32[]{:S(2)}) collective-permute-start(bf16[4,8,896]{2,1,0:T(8,128)(2,1)S(1)} %get-tuple-element.127), channel_id=1, source_target_pairs={{0,8},{4,20},{8,0},{12,28},{16,24},{20,4},{24,16},{28,12},{1,9},{5... | collective-permute-start | bytes 172040 | tf_op jit(solution)/shard_map/ppermute | solution.py:733
  36.7 9.8 %collective-permute-start.21 = (bf16[4,8,3456]{2,1,0:T(8,128)(2,1)S(1)}, bf16[4,8,3456]{2,1,0:T(8,128)(2,1)S(1)}, u32[]{:S(2)}, u32[]{:S(2)}) collective-permute-start(bf16[4,8,3456]{2,1,0:T(8,128)(2,1)S(1)} %shard_map.189), channel_id=1, source_target_pairs={{0,8},{4,20},{8,0},{12,28},{16,24},{20,4},{24,16},{28,12},{1,9},{5... | collective-permute-start | bytes 663560 | tf_op jit(solution)/shard_map/ppermute | solution.py:733
  40.5 6.0 %collective-permute-start.19 = (bf16[4,8,2560]{2,1,0:T(8,128)(2,1)S(1)}, bf16[4,8,2560]{2,1,0:T(8,128)(2,1)S(1)}, u32[]{:S(2)}, u32[]{:S(2)}) collective-permute-start(bf16[4,8,2560]{2,1,0:T(8,128)(2,1)S(1)} %shard_map.187), channel_id=1, source_target_pairs={{0,16},{4,12},{8,24},{12,4},{16,0},{20,28},{24,8},{28,20},{1,17},{... | collective-permute-start | bytes 491528 | tf_op jit(solution)/shard_map/ppermute | solution.py:730
  41.1 5.4 %collective-permute-start.20 = (bf16[4,8,896]{2,1,0:T(8,128)(2,1)S(1)}, bf16[4,8,896]{2,1,0:T(8,128)(2,1)S(1)}, u32[]{:S(2)}, u32[]{:S(2)}) collective-permute-start(bf16[4,8,896]{2,1,0:T(8,128)(2,1)S(1)} %shard_map.188), channel_id=1, source_target_pairs={{0,16},{4,12},{8,24},{12,4},{16,0},{20,28},{24,8},{28,20},{1,17},{... | collective-permute-start | bytes 172040 | tf_op jit(solution)/shard_map/ppermute | solution.py:730
  43.2 9.0 %collective-permute-start.22 = (bf16[192,256]{1,0:T(8,128)(2,1)S(1)}, bf16[192,256]{1,0:T(8,128)(2,1)S(1)}, u32[]{:S(2)}, u32[]{:S(2)}) collective-permute-start(bf16[192,256]{1,0:T(8,128)(2,1)S(1)} %get-tuple-element.148), channel_id=1, source_target_pairs={{0,4},{4,0},{8,12},{12,8},{16,20},{20,16},{24,28},{28,24},{1,5},{5... | collective-permute-start | bytes 294920 | tf_op jit(solution)/shard_map/ppermute | solution.py:721
  43.3 8.9 %collective-permute-start.23 = (bf16[192,256]{1,0:T(8,128)(2,1)S(1)}, bf16[192,256]{1,0:T(8,128)(2,1)S(1)}, u32[]{:S(2)}, u32[]{:S(2)}) collective-permute-start(bf16[192,256]{1,0:T(8,128)(2,1)S(1)} %get-tuple-element.149), channel_id=1, source_target_pairs={{0,28},{4,8},{8,4},{12,16},{16,12},{20,24},{24,20},{28,0},{1,29},{... | collective-permute-start | bytes 294920 | tf_op jit(solution)/shard_map/ppermute | solution.py:797
  46.6 6.6 %collective-permute-start.24 = (bf16[8,3456]{1,0:T(8,128)(2,1)S(1)}, bf16[8,3456]{1,0:T(8,128)(2,1)S(1)}, u32[]{:S(2)}, u32[]{:S(2)}) collective-permute-start(bf16[8,3456]{1,0:T(8,128)(2,1)S(1)} %get-tuple-element.153), channel_id=1, source_target_pairs={{0,3},{1,2},{2,1},{3,0},{4,7},{5,6},{6,5},{7,4},{8,11},{9,10},{10,... | collective-permute-start | bytes 165896 | tf_op jit(solution)/shard_map/ppermute | solution.py:721
  48.7 5.6 %collective-permute-start.25 = (bf16[8,3456]{1,0:T(8,128)(2,1)S(1)}, bf16[8,3456]{1,0:T(8,128)(2,1)S(1)}, u32[]{:S(2)}, u32[]{:S(2)}) collective-permute-start(bf16[8,3456]{1,0:T(8,128)(2,1)S(1)} %get-tuple-element.154), channel_id=1, source_target_pairs={{0,2},{1,3},{2,0},{3,1},{4,6},{5,7},{6,4},{7,5},{8,10},{9,11},{10,... | collective-permute-start | bytes 165896 | tf_op jit(solution)/shard_map/ppermute | solution.py:721
  48.7 5.6 %collective-permute-start.26 = (bf16[8,3456]{1,0:T(8,128)(2,1)S(1)}, bf16[8,3456]{1,0:T(8,128)(2,1)S(1)}, u32[]{:S(2)}, u32[]{:S(2)}) collective-permute-start(bf16[8,3456]{1,0:T(8,128)(2,1)S(1)} %get-tuple-element.155), channel_id=1, source_target_pairs={{0,1},{1,0},{2,3},{3,2},{4,5},{5,4},{6,7},{7,6},{8,9},{9,8},{10,11... | collective-permute-start | bytes 165896 | tf_op jit(solution)/shard_map/ppermute | solution.py:721

commit v6 on v5

--- a/solution.py
+++ b/solution.py
@@ -372,9 +372,9 @@
         span = slice(band * count, (band + 1) * count)
         query = query_ref[span, :].astype(F32)
         scores = mm_rt(stack_heads(query, heads), key_ref[start : start + 2 * count, :])
-        exact = jnp.exp(scores)
+        exact = jnp.exp(scores) * jnp.concatenate([mask_ref[band].astype(F32)] * heads, axis=0)
         exact_ref[band] = exact
-        raised = exact.astype(BF16) * jnp.concatenate([mask_ref[band]] * heads, axis=0)
+        raised = exact.astype(BF16)
         raised_ref[band] = raised
         value = value_ref[start : start + 2 * count, :]
         for pair in range(heads // 2):
@@ -593,7 +593,7 @@
             )
         query = stack_heads(query_ref[span, :].astype(F32), heads)
         inverse = jnp.concatenate([inverse_rows_ref[band]] * (keys // 128), axis=1)
-        probs = jnp.where(raised > 0, exact_ref[band] * inverse, 0.0)
+        probs = exact_ref[band] * inverse
         d_scores = (probs * jnp.concatenate(parts, axis=0)).astype(BF16)
         d_key = mm_lt(d_scores, query)
         d_query = fold_heads(mm(d_scores, key_ref[whole, :]), heads)

time: 55.3 us -> 55.1 us (level)
  no operation moved by 1% of the time
where the time goes in v6:
time: 55.1 us; the launch traced here: 54.9 us
  starting transfers between devices  27 us (49%)
  Pallas kernels  13.8 us (25%)
  waiting for transfers between devices  12.4 us (23%)
  between operations  0.92 us (2%)
    ppermute x20, starting transfers between devices, over(): lax.ppermute(value, axis, [(i, i ^ by) for i in range(size_of)])  21.2 us
    pallas_call x17, Pallas kernels, run(): pl.pallas_call(kernel, out_shape=outs, in_specs=[pl.BlockSpec(memory_spac...  13.8 us
    ppermute x20, waiting for transfers between devices, over(): lax.ppermute(value, axis, [(i, i ^ by) for i in range(size_of)])  7.59 us
    ppermute x3, waiting for transfers between devices, second_chip(): return lax.ppermute(value, 'rows', chip_pairs(1))  2.61 us
    ppermute x3, starting transfers between devices, second_chip(): return lax.ppermute(value, 'rows', chip_pairs(1))  2.55 us
    ppermute x2, waiting for transfers between devices, first_chip(): return lax.ppermute(value, 'rows', chip_pairs(0))  2.17 us
    ppermute x2, starting transfers between devices, first_chip(): return lax.ppermute(value, 'rows', chip_pairs(0))  2.16 us
  transfers between devices with their start and end apart: 27, of which 10 were waited for; matrix products, arithmetic and copies ran while one was open for 1% of the time, Pallas kernels for 14%

profile of v6, /device:TPU:0, one launch (start us, length us, event | category | flops | bytes accessed | tf_op | source)
XLA Modules:
  0.0 54.9 jit_solution(5396236279254591405)
XLA Ops:
  0.7 1.1 %shard_map.179 = (bf16[8,3456]{1,0:T(8,128)(2,1)S(1)}, bf16[8,3456]{1,0:T(8,128)(2,1)S(1)}, bf16[8,3584]{1,0:T(8,128)(2,1)S(1)}, f32[24,2]{1,0:T(8,128)S(1)}) custom-call(bf16[2,768]{1,0:T(2,128)(2,1)} %cond_ref.1, bf16[8,768]{1,0:T(8,128)(2,1)} %qkv_ref.1, bf16[8,1536]{1,0:T(8,128)(2,1)} %up_ref.1, bf16[8,256]{1,0:T(8,128)(2,1)} %out_ref.1, ...), custom_call_target="tpu_custom_call" | custom-call | flops 1000000000 | bytes 4000000 | tf_op jit(solution)/shard_map/pallas_call | solution.py:640
  1.8 4.1 %collective-permute-start.4 = (bf16[8,3456]{1,0:T(8,128)(2,1)S(1)}, bf16[8,3456]{1,0:T(8,128)(2,1)S(1)}, u32[]{:S(2)}, u32[]{:S(2)}) collective-permute-start(bf16[8,3456]{1,0:T(8,128)(2,1)S(1)} %get-tuple-element.94), channel_id=1, source_target_pairs={{0,2},{1,3},{2,0},{3,1},{4,6},{5,7},{6,4},{7,5},{8,10},{9,11},{10,... | collective-permute-start | bytes 165896 | tf_op jit(solution)/shard_map/ppermute | solution.py:721
  5.9 1.3 %collective-permute-start.2 = (bf16[8,3456]{1,0:T(8,128)(2,1)S(1)}, bf16[8,3456]{1,0:T(8,128)(2,1)S(1)}, u32[]{:S(2)}, u32[]{:S(2)}) collective-permute-start(bf16[8,3456]{1,0:T(8,128)(2,1)S(1)} %get-tuple-element.94), channel_id=1, source_target_pairs={{0,3},{1,2},{2,1},{3,0},{4,7},{5,6},{6,5},{7,4},{8,11},{9,10},{10,... | collective-permute-start | bytes 165896 | tf_op jit(solution)/shard_map/ppermute | solution.py:721
  7.2 0.2 collective-permute-start.3
  7.4 2.4 %collective-permute-start.7 = (bf16[8,3584]{1,0:T(8,128)(2,1)S(1)}, bf16[8,3584]{1,0:T(8,128)(2,1)S(1)}, u32[]{:S(2)}, u32[]{:S(2)}) collective-permute-start(bf16[8,3584]{1,0:T(8,128)(2,1)S(1)} %get-tuple-element.97), channel_id=1, source_target_pairs={{0,24},{4,28},{8,16},{12,20},{16,8},{20,12},{24,0},{28,4},{1,25},{... | collective-permute-start | bytes 172040 | tf_op jit(solution)/shard_map/ppermute | solution.py:721
  10.1 0.1 slice.11
  10.2 0.1 fusion.3
  10.3 0.2 fusion.1
  10.6 0.1 copy.20
  10.7 0.1 broadcast_in_dim.49
  10.7 0.1 reshape.363.id_key_ref
  10.8 1.1 %collective-permute-done.3.p2 = bf16[8,3456]{1,0:T(8,128)(2,1)S(1)} collective-permute-done((bf16[8,3456]{1,0:T(8,128)(2,1)S(1)}, bf16[8,3456]{1,0:T(8,128)(2,1)S(1)}, u32[]{:S(2)}, u32[]{:S(2)}) %collective-permute-start.3) | collective-permute-done | bytes 55328 | tf_op jit(solution)/shard_map/ppermute | solution.py:721
  12.0 1.6 %collective-permute-start.6 = (bf16[4,8,3456]{2,1,0:T(8,128)(2,1)S(1)}, bf16[4,8,3456]{2,1,0:T(8,128)(2,1)S(1)}, u32[]{:S(2)}, u32[]{:S(2)}) collective-permute-start(bf16[4,8,3456]{2,1,0:T(8,128)(2,1)S(1)} %shard_map.180.p0), channel_id=1, source_target_pairs={{0,16},{4,20},{8,24},{12,28},{16,0},{20,4},{24,8},{28,12},{1,17},{... | collective-permute-start | bytes 663560 | tf_op jit(solution)/shard_map/ppermute | solution.py:721
  13.6 1.5 %collective-permute-start.5 = (bf16[4,8,3456]{2,1,0:T(8,128)(2,1)S(1)}, bf16[4,8,3456]{2,1,0:T(8,128)(2,1)S(1)}, u32[]{:S(2)}, u32[]{:S(2)}) collective-permute-start(bf16[4,8,3456]{2,1,0:T(8,128)(2,1)S(1)} %shard_map.180.p0), channel_id=1, source_target_pairs={{0,8},{4,12},{8,0},{12,4},{16,24},{20,28},{24,16},{28,20},{1,9},{5... | collective-permute-start | bytes 663560 | tf_op jit(solution)/shard_map/ppermute | solution.py:721
  15.1 2.4 %collective-permute-start.10 = (bf16[8,3456]{1,0:T(8,128)(2,1)S(1)}, bf16[8,3456]{1,0:T(8,128)(2,1)S(1)}, u32[]{:S(2)}, u32[]{:S(2)}) collective-permute-start(bf16[8,3456]{1,0:T(8,128)(2,1)S(1)} %get-tuple-element.99), channel_id=1, source_target_pairs={{0,2},{1,3},{2,0},{3,1},{4,6},{5,7},{6,4},{7,5},{8,10},{9,11},{10,... | collective-permute-start | bytes 165896 | tf_op jit(solution)/shard_map/ppermute | solution.py:721
  17.5 1.3 %collective-permute-start.8 = (bf16[8,3456]{1,0:T(8,128)(2,1)S(1)}, bf16[8,3456]{1,0:T(8,128)(2,1)S(1)}, u32[]{:S(2)}, u32[]{:S(2)}) collective-permute-start(bf16[8,3456]{1,0:T(8,128)(2,1)S(1)} %get-tuple-element.99), channel_id=1, source_target_pairs={{0,3},{1,2},{2,1},{3,0},{4,7},{5,6},{6,5},{7,4},{8,11},{9,10},{10,... | collective-permute-start | bytes 165896 | tf_op jit(solution)/shard_map/ppermute | solution.py:721
  18.9 1.3 %shard_map.178 = (f32[1024,256]{1,0:T(8,128)S(1)}, bf16[256,1024]{1,0:T(8,128)(2,1)S(1)}, bf16[256,512]{1,0:T(8,128)(2,1)S(1)}, f32[1024,128]{1,0:T(8,128)S(1)},...) custom-call(f32[4]{0:T(128)S(1)} %copy-done.2, ...), custom_call_target="tpu_custom_call" | custom-call | flops 1000000000 | bytes 4000000 | tf_op jit(solution)/shard_map/pallas_call | solution.py:640
  20.2 3.4 %collective-permute-done.9.p2 = bf16[8,3456]{1,0:T(8,128)(2,1)S(1)} collective-permute-done((bf16[8,3456]{1,0:T(8,128)(2,1)S(1)}, bf16[8,3456]{1,0:T(8,128)(2,1)S(1)}, u32[]{:S(2)}, u32[]{:S(2)}) %collective-permute-start.9) | collective-permute-done | bytes 55328 | tf_op jit(solution)/shard_map/ppermute | solution.py:721
  23.7 0.6 %collective-permute-start.14 = (bf16[4,8,3456]{2,1,0:T(8,128)(2,1)S(1)}, bf16[4,8,3456]{2,1,0:T(8,128)(2,1)S(1)}, u32[]{:S(2)}, u32[]{:S(2)}) collective-permute-start(bf16[4,8,3456]{2,1,0:T(8,128)(2,1)S(1)} %shard_map.182.p3), channel_id=1, source_target_pairs={{0,4},{4,0},{8,12},{12,8},{16,20},{20,16},{24,28},{28,24},{1,5},{5... | collective-permute-start | bytes 663560 | tf_op jit(solution)/shard_map/ppermute | solution.py:721
  24.2 0.1 collective-permute-start.12
  24.3 0.4 collective-permute-start.13
  24.7 0.3 collective-permute-done.11.p4
  25.1 0.3 collective-permute-done.14.p7
  25.4 0.3 collective-permute-done.12.p5
  25.7 0.3 collective-permute-done.13.p6
  26.0 4.6 %shard_map.183 = (bf16[512,256]{1,0:T(8,128)(2,1)S(1)}, bf16[1024,256]{1,0:T(8,128)(2,1)S(1)}, bf16[1024,256]{1,0:T(8,128)(2,1)S(1)}, bf16[4,512,256]{2,1,0:T(8,...) custom-call(f32[1,128]{1,0:T(1,128)S(1)} %get-tuple-element.86.root_, ...), custom_call_target="tpu_custom_call" | custom-call | flops 1000000000 | bytes 4000000 | tf_op jit(solution)/shard_map/pallas_call | solution.py:640
  30.6 0.4 collective-permute-start.15
  31.0 2.9 %shard_map.185 = (bf16[512,256]{1,0:T(8,128)(2,1)S(1)}, bf16[1024,512]{1,0:T(8,128)(2,1)S(1)}, bf16[4,4,8,896]{3,2,1,0:T(8,128)(2,1)S(1)}, bf16[4,4,8,896]{3,2,1,0:T(8,128)(2,1)S(1)}) custom-call(f32[1,128]{1,0:T(1,128)S(1)} %get-tuple-element.86.root_ref, bf16[512,256]{1,0:T(8,128)(2,1)S(1)} %get-tuple-element.107.shrunk_ref, ...), custom_call_target="tpu_custom_call" | custom-call | flops 1 | bytes 1 | tf_op jit(solution)/shard_map/pallas_call | solution.py:640
  33.9 0.3 collective-permute-start.17
  34.2 0.2 shard_map.184
  34.3 0.4 collective-permute-start.16
  34.7 0.7 %collective-permute-done.17.got_ref = bf16[4,4,8,896]{3,2,1,0:T(8,128)(2,1)S(1)} collective-permute-done((bf16[4,4,8,896]{3,2,1,0:T(8,128)(2,1)S(1)}, bf16[4,4,8,896]{3,2,1,0:T(8,128)(2,1)S(1)}, u32[]{:S(2)}, u32[]{:S(2)}) %collective-permute-start.17) | collective-permute-done | bytes 229408 | tf_op jit(solution)/shard_map/ppermute | solution.py:721
  35.4 0.1 shard_map.186
  35.5 1.0 %collective-permute-start.18 = (bf16[4,8,896]{2,1,0:T(8,128)(2,1)S(1)}, bf16[4,8,896]{2,1,0:T(8,128)(2,1)S(1)}, u32[]{:S(2)}, u32[]{:S(2)}) collective-permute-start(bf16[4,8,896]{2,1,0:T(8,128)(2,1)S(1)} %get-tuple-element.127), channel_id=1, source_target_pairs={{0,8},{4,20},{8,0},{12,28},{16,24},{20,4},{24,16},{28,12},{1,9},{5... | collective-permute-start | bytes 172040 | tf_op jit(solution)/shard_map/ppermute | solution.py:733
  36.6 1.1 %collective-permute-start.21 = (bf16[4,8,3456]{2,1,0:T(8,128)(2,1)S(1)}, bf16[4,8,3456]{2,1,0:T(8,128)(2,1)S(1)}, u32[]{:S(2)}, u32[]{:S(2)}) collective-permute-start(bf16[4,8,3456]{2,1,0:T(8,128)(2,1)S(1)} %shard_map.189), channel_id=1, source_target_pairs={{0,8},{4,20},{8,0},{12,28},{16,24},{20,4},{24,16},{28,12},{1,9},{5... | collective-permute-start | bytes 663560 | tf_op jit(solution)/shard_map/ppermute | solution.py:733
  37.7 2.6 %collective-permute-done.18.two_ref = bf16[4,8,896]{2,1,0:T(8,128)(2,1)S(1)} collective-permute-done((bf16[4,8,896]{2,1,0:T(8,128)(2,1)S(1)}, bf16[4,8,896]{2,1,0:T(8,128)(2,1)S(1)}, u32[]{:S(2)}, u32[]{:S(2)}) %collective-permute-start.18) | collective-permute-done | bytes 57376 | tf_op jit(solution)/shard_map/ppermute | solution.py:733
  40.4 0.6 %collective-permute-start.19 = (bf16[4,8,2560]{2,1,0:T(8,128)(2,1)S(1)}, bf16[4,8,2560]{2,1,0:T(8,128)(2,1)S(1)}, u32[]{:S(2)}, u32[]{:S(2)}) collective-permute-start(bf16[4,8,2560]{2,1,0:T(8,128)(2,1)S(1)} %shard_map.187), channel_id=1, source_target_pairs={{0,16},{4,12},{8,24},{12,4},{16,0},{20,28},{24,8},{28,20},{1,17},{... | collective-permute-start | bytes 491528 | tf_op jit(solution)/shard_map/ppermute | solution.py:730
  41.0 1.6 %collective-permute-start.20 = (bf16[4,8,896]{2,1,0:T(8,128)(2,1)S(1)}, bf16[4,8,896]{2,1,0:T(8,128)(2,1)S(1)}, u32[]{:S(2)}, u32[]{:S(2)}) collective-permute-start(bf16[4,8,896]{2,1,0:T(8,128)(2,1)S(1)} %shard_map.188), channel_id=1, source_target_pairs={{0,16},{4,12},{8,24},{12,4},{16,0},{20,28},{24,8},{28,20},{1,17},{... | collective-permute-start | bytes 172040 | tf_op jit(solution)/shard_map/ppermute | solution.py:730
  42.6 0.5 shard_map.191
  43.2 1.0 %collective-permute-start.23 = (bf16[192,256]{1,0:T(8,128)(2,1)S(1)}, bf16[192,256]{1,0:T(8,128)(2,1)S(1)}, u32[]{:S(2)}, u32[]{:S(2)}) collective-permute-start(bf16[192,256]{1,0:T(8,128)(2,1)S(1)} %get-tuple-element.149), channel_id=1, source_target_pairs={{0,28},{4,8},{8,4},{12,16},{16,12},{20,24},{24,20},{28,0},{1,29},{... | collective-permute-start | bytes 294920 | tf_op jit(solution)/shard_map/ppermute | solution.py:797
  44.2 2.2 %collective-permute-done.20.q1 = bf16[4,8,896]{2,1,0:T(8,128)(2,1)S(1)} collective-permute-done((bf16[4,8,896]{2,1,0:T(8,128)(2,1)S(1)}, bf16[4,8,896]{2,1,0:T(8,128)(2,1)S(1)}, u32[]{:S(2)}, u32[]{:S(2)}) %collective-permute-start.20) | collective-permute-done | bytes 57376 | tf_op jit(solution)/shard_map/ppermute | solution.py:730
  46.4 0.1 shard_map.190
  46.5 2.1 %collective-permute-start.24 = (bf16[8,3456]{1,0:T(8,128)(2,1)S(1)}, bf16[8,3456]{1,0:T(8,128)(2,1)S(1)}, u32[]{:S(2)}, u32[]{:S(2)}) collective-permute-start(bf16[8,3456]{1,0:T(8,128)(2,1)S(1)} %get-tuple-element.153), channel_id=1, source_target_pairs={{0,3},{1,2},{2,1},{3,0},{4,7},{5,6},{6,5},{7,4},{8,11},{9,10},{10,... | collective-permute-start | bytes 165896 | tf_op jit(solution)/shard_map/ppermute | solution.py:721
  48.6 2.4 %collective-permute-start.26 = (bf16[8,3456]{1,0:T(8,128)(2,1)S(1)}, bf16[8,3456]{1,0:T(8,128)(2,1)S(1)}, u32[]{:S(2)}, u32[]{:S(2)}) collective-permute-start(bf16[8,3456]{1,0:T(8,128)(2,1)S(1)} %get-tuple-element.155), channel_id=1, source_target_pairs={{0,1},{1,0},{2,3},{3,2},{4,5},{5,4},{6,7},{7,6},{8,9},{9,8},{10,11... | collective-permute-start | bytes 165896 | tf_op jit(solution)/shard_map/ppermute | solution.py:721
  51.0 1.1 %shard_map.192 = bf16[8,64,256]{2,1,0:T(8,128)(2,1)} custom-call(f32[512,256]{1,0:T(8,128)S(1)} %get-tuple-element.101.middle_ref, bf16[512,768]{1,0:T(8,128)(2,1)S(1)} %get-tuple-element.144.gated_ref, bf16[768,256]{1,0:T(8,128)(2,1)S(1)} %get-tuple-element.145.w_down_ref), custom_call_target="tpu_custom_call" | custom-call | flops 1000000000 | bytes 4000000 | tf_op jit(solution)/shard_map/pallas_call | solution.py:640
  52.1 1.1 %shard_map.193 = f32[8,64,256]{2,1,0:T(8,128)} custom-call(f32[512,256]{1,0:T(8,128)S(1)} %get-tuple-element.91.inputs_ref, f32[2,256]{1,0:T(2,128)S(1)} %get-tuple-element.146.gain_ref, f32[512,256]{1,0:T(8,128)S(1)} %get-tuple-element.147.own_ref, bf16[192,256]{1,0:T(8,128)(2,1)S(1)} %collective-permute-done.22.rim_swap_ref, ...), custom_call_target="tpu_custom_call" | custom-call | flops 1000000000 | bytes 4000000 | tf_op jit(solution)/shard_map/pallas_call | solution.py:640
  53.2 1.0 %collective-permute-done.25.two_ref = bf16[8,3456]{1,0:T(8,128)(2,1)S(1)} collective-permute-done((bf16[8,3456]{1,0:T(8,128)(2,1)S(1)}, bf16[8,3456]{1,0:T(8,128)(2,1)S(1)}, u32[]{:S(2)}, u32[]{:S(2)}) %collective-permute-start.25) | collective-permute-done | bytes 55328 | tf_op jit(solution)/shard_map/ppermute | solution.py:721
  54.2 0.7 %shard_map.194 = (f32[8,768]{1,0:T(8,128)}, f32[8,256]{1,0:T(8,128)}, f32[8,1536]{1,0:T(8,128)}, f32[24,256]{1,0:T(8,128)}, f32[24,256]{1,0:T(8,128)}, /*index=5*/f32[24,256]{1,0:T(8,128)}, f32[4]{0:T(128)}) custom-call(f32[24,2]{1,0:T(8,128)S(1)} %get-tuple-element.151.cond_ref, f32[8,3456]{1,0:T(8,128)S(1)} %get-tuple-element.152.own_ref, ...), custom_call_target="tpu_custom_call" | custom-call | flops 1000000000 | bytes 4000000 | tf_op jit(solution)/shard_map/pallas_call | solution.py:640
  (48 shorter events, 0.5 us)
Async XLA Ops:
  0.6 9.2 %copy-start = (bf16[8,64,256]{2,1,0:T(8,128)(2,1)S(1)}, bf16[8,64,256]{2,1,0:T(8,128)(2,1)}, u32[]{:S(2)}) copy-start(bf16[8,64,256]{2,1,0:T(8,128)(2,1)} %feat_ref.1) | copy-start | bytes 786436
  0.7 9.4 %copy-start.3 = (s32[64,64]{1,0:T(8,128)S(1)}, s32[64,64]{1,0:T(8,128)}, u32[]{:S(2)}) copy-start(s32[64,64]{1,0:T(8,128)} %param.12) | copy-start | bytes 49156
  1.8 10.2 %collective-permute-start.4 = (bf16[8,3456]{1,0:T(8,128)(2,1)S(1)}, bf16[8,3456]{1,0:T(8,128)(2,1)S(1)}, u32[]{:S(2)}, u32[]{:S(2)}) collective-permute-start(bf16[8,3456]{1,0:T(8,128)(2,1)S(1)} %get-tuple-element.94), channel_id=1, source_target_pairs={{0,2},{1,3},{2,0},{3,1},{4,6},{5,7},{6,4},{7,5},{8,10},{9,11},{10,... | collective-permute-start | bytes 165896 | tf_op jit(solution)/shard_map/ppermute | solution.py:721
  5.9 6.1 %collective-permute-start.2 = (bf16[8,3456]{1,0:T(8,128)(2,1)S(1)}, bf16[8,3456]{1,0:T(8,128)(2,1)S(1)}, u32[]{:S(2)}, u32[]{:S(2)}) collective-permute-start(bf16[8,3456]{1,0:T(8,128)(2,1)S(1)} %get-tuple-element.94), channel_id=1, source_target_pairs={{0,3},{1,2},{2,1},{3,0},{4,7},{5,6},{6,5},{7,4},{8,11},{9,10},{10,... | collective-permute-start | bytes 165896 | tf_op jit(solution)/shard_map/ppermute | solution.py:721
  7.2 4.7 %collective-permute-start.3 = (bf16[8,3456]{1,0:T(8,128)(2,1)S(1)}, bf16[8,3456]{1,0:T(8,128)(2,1)S(1)}, u32[]{:S(2)}, u32[]{:S(2)}) collective-permute-start(bf16[8,3456]{1,0:T(8,128)(2,1)S(1)} %get-tuple-element.93.p0), channel_id=1, source_target_pairs={{0,1},{1,0},{2,3},{3,2},{4,5},{5,4},{6,7},{7,6},{8,9},{9,8},{10,11... | collective-permute-start | bytes 165896 | tf_op jit(solution)/shard_map/ppermute | solution.py:721
  7.4 7.7 %collective-permute-start.7 = (bf16[8,3584]{1,0:T(8,128)(2,1)S(1)}, bf16[8,3584]{1,0:T(8,128)(2,1)S(1)}, u32[]{:S(2)}, u32[]{:S(2)}) collective-permute-start(bf16[8,3584]{1,0:T(8,128)(2,1)S(1)} %get-tuple-element.97), channel_id=1, source_target_pairs={{0,24},{4,28},{8,16},{12,20},{16,8},{20,12},{24,0},{28,4},{1,25},{... | collective-permute-start | bytes 172040 | tf_op jit(solution)/shard_map/ppermute | solution.py:721
  9.9 7.6 %collective-permute-start.1 = (bf16[3,64,256]{2,1,0:T(8,128)(2,1)S(1)}, bf16[3,64,256]{2,1,0:T(8,128)(2,1)S(1)}, u32[]{:S(2)}, u32[]{:S(2)}) collective-permute-start(bf16[3,64,256]{2,1,0:T(8,128)(2,1)S(1)} %get-tuple-element.163), channel_id=1, source_target_pairs={{0,28},{4,8},{8,4},{12,16},{16,12},{20,24},{24,20},{28,0},{1,29},{... | collective-permute-start | bytes 294920 | tf_op jit(solution)/shard_map/ppermute | solution.py:797
  12.0 6.9 %collective-permute-start = (bf16[3,64,256]{2,1,0:T(8,128)(2,1)S(1)}, bf16[3,64,256]{2,1,0:T(8,128)(2,1)S(1)}, u32[]{:S(2)}, u32[]{:S(2)}) collective-permute-start(bf16[3,64,256]{2,1,0:T(8,128)(2,1)S(1)} %get-tuple-element.164), channel_id=1, source_target_pairs={{0,4},{4,0},{8,12},{12,8},{16,20},{20,16},{24,28},{28,24},{1,5},{5... | collective-permute-start | bytes 294920 | tf_op jit(solution)/shard_map/ppermute | solution.py:721
  12.0 6.9 %copy-start.1 = (bf16[8,64,256]{2,1,0:T(8,128)(2,1)S(1)}, bf16[8,64,256]{2,1,0:T(8,128)(2,1)}, u32[]{:S(2)}) copy-start(bf16[8,64,256]{2,1,0:T(8,128)(2,1)} %cot_ref.1) | copy-start | bytes 786436
  12.0 6.9 %copy-start.2 = (f32[4]{0:T(128)S(1)}, f32[4]{0:T(128)}, u32[]{:S(2)}) copy-start(f32[4]{0:T(128)} %scale_ref.1) | copy-start | bytes 52
  12.0 12.2 %collective-permute-start.6 = (bf16[4,8,3456]{2,1,0:T(8,128)(2,1)S(1)}, bf16[4,8,3456]{2,1,0:T(8,128)(2,1)S(1)}, u32[]{:S(2)}, u32[]{:S(2)}) collective-permute-start(bf16[4,8,3456]{2,1,0:T(8,128)(2,1)S(1)} %shard_map.180.p0), channel_id=1, source_target_pairs={{0,16},{4,20},{8,24},{12,28},{16,0},{20,4},{24,8},{28,12},{1,17},{... | collective-permute-start | bytes 663560 | tf_op jit(solution)/shard_map/ppermute | solution.py:721
  13.6 10.6 %collective-permute-start.5 = (bf16[4,8,3456]{2,1,0:T(8,128)(2,1)S(1)}, bf16[4,8,3456]{2,1,0:T(8,128)(2,1)S(1)}, u32[]{:S(2)}, u32[]{:S(2)}) collective-permute-start(bf16[4,8,3456]{2,1,0:T(8,128)(2,1)S(1)} %shard_map.180.p0), channel_id=1, source_target_pairs={{0,8},{4,12},{8,0},{12,4},{16,24},{20,28},{24,16},{28,20},{1,9},{5... | collective-permute-start | bytes 663560 | tf_op jit(solution)/shard_map/ppermute | solution.py:721
  15.1 8.5 %collective-permute-start.10 = (bf16[8,3456]{1,0:T(8,128)(2,1)S(1)}, bf16[8,3456]{1,0:T(8,128)(2,1)S(1)}, u32[]{:S(2)}, u32[]{:S(2)}) collective-permute-start(bf16[8,3456]{1,0:T(8,128)(2,1)S(1)} %get-tuple-element.99), channel_id=1, source_target_pairs={{0,2},{1,3},{2,0},{3,1},{4,6},{5,7},{6,4},{7,5},{8,10},{9,11},{10,... | collective-permute-start | bytes 165896 | tf_op jit(solution)/shard_map/ppermute | solution.py:721
  17.5 6.1 %collective-permute-start.8 = (bf16[8,3456]{1,0:T(8,128)(2,1)S(1)}, bf16[8,3456]{1,0:T(8,128)(2,1)S(1)}, u32[]{:S(2)}, u32[]{:S(2)}) collective-permute-start(bf16[8,3456]{1,0:T(8,128)(2,1)S(1)} %get-tuple-element.99), channel_id=1, source_target_pairs={{0,3},{1,2},{2,1},{3,0},{4,7},{5,6},{6,5},{7,4},{8,11},{9,10},{10,... | collective-permute-start | bytes 165896 | tf_op jit(solution)/shard_map/ppermute | solution.py:721
  18.9 4.7 %collective-permute-start.9 = (bf16[8,3456]{1,0:T(8,128)(2,1)S(1)}, bf16[8,3456]{1,0:T(8,128)(2,1)S(1)}, u32[]{:S(2)}, u32[]{:S(2)}) collective-permute-start(bf16[8,3456]{1,0:T(8,128)(2,1)S(1)} %get-tuple-element.98.p0), channel_id=1, source_target_pairs={{0,1},{1,0},{2,3},{3,2},{4,5},{5,4},{6,7},{7,6},{8,9},{9,8},{10,11... | collective-permute-start | bytes 165896 | tf_op jit(solution)/shard_map/ppermute | solution.py:721
  23.6 1.5 %collective-permute-start.11 = (bf16[4,8,3456]{2,1,0:T(8,128)(2,1)S(1)}, bf16[4,8,3456]{2,1,0:T(8,128)(2,1)S(1)}, u32[]{:S(2)}, u32[]{:S(2)}) collective-permute-start(bf16[4,8,3456]{2,1,0:T(8,128)(2,1)S(1)} %shard_map.180.p0), channel_id=1, source_target_pairs={{0,4},{4,0},{8,12},{12,8},{16,20},{20,16},{24,28},{28,24},{1,5},{5... | collective-permute-start | bytes 663560 | tf_op jit(solution)/shard_map/ppermute | solution.py:721
  23.7 1.7 %collective-permute-start.14 = (bf16[4,8,3456]{2,1,0:T(8,128)(2,1)S(1)}, bf16[4,8,3456]{2,1,0:T(8,128)(2,1)S(1)}, u32[]{:S(2)}, u32[]{:S(2)}) collective-permute-start(bf16[4,8,3456]{2,1,0:T(8,128)(2,1)S(1)} %shard_map.182.p3), channel_id=1, source_target_pairs={{0,4},{4,0},{8,12},{12,8},{16,20},{20,16},{24,28},{28,24},{1,5},{5... | collective-permute-start | bytes 663560 | tf_op jit(solution)/shard_map/ppermute | solution.py:721
  24.2 1.5 %collective-permute-start.12 = (bf16[4,8,3456]{2,1,0:T(8,128)(2,1)S(1)}, bf16[4,8,3456]{2,1,0:T(8,128)(2,1)S(1)}, u32[]{:S(2)}, u32[]{:S(2)}) collective-permute-start(bf16[4,8,3456]{2,1,0:T(8,128)(2,1)S(1)} %collective-permute-done.5.p1), channel_id=1, source_target_pairs={{0,4},{4,0},{8,12},{12,8},{16,20},{20,16},{24,28},{28,24},{1,5},{5... | collective-permute-start | bytes 663560 | tf_op jit(solution)/shard_map/ppermute | solution.py:721
  24.3 1.7 %collective-permute-start.13 = (bf16[4,8,3456]{2,1,0:T(8,128)(2,1)S(1)}, bf16[4,8,3456]{2,1,0:T(8,128)(2,1)S(1)}, u32[]{:S(2)}, u32[]{:S(2)}) collective-permute-start(bf16[4,8,3456]{2,1,0:T(8,128)(2,1)S(1)} %collective-permute-done.6.p2), channel_id=1, source_target_pairs={{0,4},{4,0},{8,12},{12,8},{16,20},{20,16},{24,28},{28,24},{1,5},{5... | collective-permute-start | bytes 663560 | tf_op jit(solution)/shard_map/ppermute | solution.py:721
  30.6 3.6 %collective-permute-start.15 = (bf16[4,4,8,2560]{3,2,1,0:T(8,128)(2,1)S(1)}, bf16[4,4,8,2560]{3,2,1,0:T(8,128)(2,1)S(1)}, u32[]{:S(2)}, u32[]{:S(2)}) collective-permute-start(bf16[4,4,8,2560]{3,2,1,0:T(8,128)(2,1)S(1)} %get-tuple-element.103), channel_id=1, source_target_pairs={{0,4},{4,0},{8,12},{12,8},{16,20},{20,16},{24,28},{28,24},{1,5},{5... | collective-permute-start | bytes 1966088 | tf_op jit(solution)/shard_map/ppermute | solution.py:721
  33.9 1.6 %collective-permute-start.17 = (bf16[4,4,8,896]{3,2,1,0:T(8,128)(2,1)S(1)}, bf16[4,4,8,896]{3,2,1,0:T(8,128)(2,1)S(1)}, u32[]{:S(2)}, u32[]{:S(2)}) collective-permute-start(bf16[4,4,8,896]{3,2,1,0:T(8,128)(2,1)S(1)} %get-tuple-element.126), channel_id=1, source_target_pairs={{0,4},{4,0},{8,12},{12,8},{16,20},{20,16},{24,28},{28,24},{1,5},{5... | collective-permute-start | bytes 688136 | tf_op jit(solution)/shard_map/ppermute | solution.py:721
  34.3 6.0 %collective-permute-start.16 = (bf16[4,8,2560]{2,1,0:T(8,128)(2,1)S(1)}, bf16[4,8,2560]{2,1,0:T(8,128)(2,1)S(1)}, u32[]{:S(2)}, u32[]{:S(2)}) collective-permute-start(bf16[4,8,2560]{2,1,0:T(8,128)(2,1)S(1)} %get-tuple-element.106), channel_id=1, source_target_pairs={{0,8},{4,20},{8,0},{12,28},{16,24},{20,4},{24,16},{28,12},{1,9},{5... | collective-permute-start | bytes 491528 | tf_op jit(solution)/shard_map/ppermute | solution.py:733
  35.5 4.8 %collective-permute-start.18 = (bf16[4,8,896]{2,1,0:T(8,128)(2,1)S(1)}, bf16[4,8,896]{2,1,0:T(8,128)(2,1)S(1)}, u32[]{:S(2)}, u32[]{:S(2)}) collective-permute-start(bf16[4,8,896]{2,1,0:T(8,128)(2,1)S(1)} %get-tuple-element.127), channel_id=1, source_target_pairs={{0,8},{4,20},{8,0},{12,28},{16,24},{20,4},{24,16},{28,12},{1,9},{5... | collective-permute-start | bytes 172040 | tf_op jit(solution)/shard_map/ppermute | solution.py:733
  36.6 9.8 %collective-permute-start.21 = (bf16[4,8,3456]{2,1,0:T(8,128)(2,1)S(1)}, bf16[4,8,3456]{2,1,0:T(8,128)(2,1)S(1)}, u32[]{:S(2)}, u32[]{:S(2)}) collective-permute-start(bf16[4,8,3456]{2,1,0:T(8,128)(2,1)S(1)} %shard_map.189), channel_id=1, source_target_pairs={{0,8},{4,20},{8,0},{12,28},{16,24},{20,4},{24,16},{28,12},{1,9},{5... | collective-permute-start | bytes 663560 | tf_op jit(solution)/shard_map/ppermute | solution.py:733
  40.4 6.0 %collective-permute-start.19 = (bf16[4,8,2560]{2,1,0:T(8,128)(2,1)S(1)}, bf16[4,8,2560]{2,1,0:T(8,128)(2,1)S(1)}, u32[]{:S(2)}, u32[]{:S(2)}) collective-permute-start(bf16[4,8,2560]{2,1,0:T(8,128)(2,1)S(1)} %shard_map.187), channel_id=1, source_target_pairs={{0,16},{4,12},{8,24},{12,4},{16,0},{20,28},{24,8},{28,20},{1,17},{... | collective-permute-start | bytes 491528 | tf_op jit(solution)/shard_map/ppermute | solution.py:730
  41.0 5.4 %collective-permute-start.20 = (bf16[4,8,896]{2,1,0:T(8,128)(2,1)S(1)}, bf16[4,8,896]{2,1,0:T(8,128)(2,1)S(1)}, u32[]{:S(2)}, u32[]{:S(2)}) collective-permute-start(bf16[4,8,896]{2,1,0:T(8,128)(2,1)S(1)} %shard_map.188), channel_id=1, source_target_pairs={{0,16},{4,12},{8,24},{12,4},{16,0},{20,28},{24,8},{28,20},{1,17},{... | collective-permute-start | bytes 172040 | tf_op jit(solution)/shard_map/ppermute | solution.py:730
  43.1 9.0 %collective-permute-start.22 = (bf16[192,256]{1,0:T(8,128)(2,1)S(1)}, bf16[192,256]{1,0:T(8,128)(2,1)S(1)}, u32[]{:S(2)}, u32[]{:S(2)}) collective-permute-start(bf16[192,256]{1,0:T(8,128)(2,1)S(1)} %get-tuple-element.148), channel_id=1, source_target_pairs={{0,4},{4,0},{8,12},{12,8},{16,20},{20,16},{24,28},{28,24},{1,5},{5... | collective-permute-start | bytes 294920 | tf_op jit(solution)/shard_map/ppermute | solution.py:721
  43.2 8.9 %collective-permute-start.23 = (bf16[192,256]{1,0:T(8,128)(2,1)S(1)}, bf16[192,256]{1,0:T(8,128)(2,1)S(1)}, u32[]{:S(2)}, u32[]{:S(2)}) collective-permute-start(bf16[192,256]{1,0:T(8,128)(2,1)S(1)} %get-tuple-element.149), channel_id=1, source_target_pairs={{0,28},{4,8},{8,4},{12,16},{16,12},{20,24},{24,20},{28,0},{1,29},{... | collective-permute-start | bytes 294920 | tf_op jit(solution)/shard_map/ppermute | solution.py:797
  46.5 6.6 %collective-permute-start.24 = (bf16[8,3456]{1,0:T(8,128)(2,1)S(1)}, bf16[8,3456]{1,0:T(8,128)(2,1)S(1)}, u32[]{:S(2)}, u32[]{:S(2)}) collective-permute-start(bf16[8,3456]{1,0:T(8,128)(2,1)S(1)} %get-tuple-element.153), channel_id=1, source_target_pairs={{0,3},{1,2},{2,1},{3,0},{4,7},{5,6},{6,5},{7,4},{8,11},{9,10},{10,... | collective-permute-start | bytes 165896 | tf_op jit(solution)/shard_map/ppermute | solution.py:721
  48.6 5.6 %collective-permute-start.25 = (bf16[8,3456]{1,0:T(8,128)(2,1)S(1)}, bf16[8,3456]{1,0:T(8,128)(2,1)S(1)}, u32[]{:S(2)}, u32[]{:S(2)}) collective-permute-start(bf16[8,3456]{1,0:T(8,128)(2,1)S(1)} %get-tuple-element.154), channel_id=1, source_target_pairs={{0,2},{1,3},{2,0},{3,1},{4,6},{5,7},{6,4},{7,5},{8,10},{9,11},{10,... | collective-permute-start | bytes 165896 | tf_op jit(solution)/shard_map/ppermute | solution.py:721
  48.6 5.6 %collective-permute-start.26 = (bf16[8,3456]{1,0:T(8,128)(2,1)S(1)}, bf16[8,3456]{1,0:T(8,128)(2,1)S(1)}, u32[]{:S(2)}, u32[]{:S(2)}) collective-permute-start(bf16[8,3456]{1,0:T(8,128)(2,1)S(1)} %get-tuple-element.155), channel_id=1, source_target_pairs={{0,1},{1,0},{2,3},{3,2},{4,5},{5,4},{6,7},{7,6},{8,9},{9,8},{10,11... | collective-permute-start | bytes 165896 | tf_op jit(solution)/shard_map/ppermute | solution.py:721
